TPU v7x, 32 devices: a whole 2x2x4 slice. The times are simulated.
32 devices in a mesh: gx: 8 (over y, x, core), gy: 4 (over z).
Axes of the slice: x: 2, y: 2, z: 4, core: 2. Of those that a mesh axis runs over, the one named last changes fastest.
Arguments:
- tokens: bfloat16 [8192, 1536], P('gx', 'gy'), may hold values from -6 to 6
- first_gain: float32 [1536], P('gy'), may hold values from 0.5 to 1.5
- w_query: float32 [1536, 1536], P('gx', 'gy'), may hold values from -0.15625 to 0.15625
- w_key: float32 [1536, 512], P('gx', 'gy'), may hold values from -0.15625 to 0.15625
- w_value: float32 [1536, 512], P('gx', 'gy'), may hold values from -0.15625 to 0.15625
- w_out: float32 [1536, 1536], P('gx', 'gy'), may hold values from -0.625 to 0.625
- second_gain: float32 [1536], P('gy'), may hold values from 0.5 to 1.5
- w_router: float32 [1536, 40], P('gx'), may hold values from -0.078125 to 0.078125
- w_gate: float32 [1536, 40, 512], P('gx', None, 'gy'), may hold values from -0.15625 to 0.15625
- w_up: float32 [1536, 40, 512], P('gx', None, 'gy'), may hold values from -0.15625 to 0.15625
- w_down: float32 [1536, 40, 512], P('gx', None, 'gy'), may hold values from -0.75 to 0.75
- routes: int32 [8192, 8], P('gx'), may hold values from 0 to 39, all different within a row; in each aligned block of 1024 rows (0 to 1023, 1024 to 2047, ...) at most 256 rows name the same one
- block_cotangent: bfloat16 [8192, 1536], P('gx', 'gy'), may hold values from -6 to 6
Outputs:
- block_out: bfloat16 [8192, 1536], P('gx', 'gy')
- input_grad: bfloat16 [8192, 1536], P('gx', 'gy')
- first_gain_grad: float32 [1536], P('gy')
- query_grad: float32 [1536, 1536], P('gx', 'gy')
- key_grad: float32 [1536, 512], P('gx', 'gy')
- value_grad: float32 [1536, 512], P('gx', 'gy')
- out_proj_grad: float32 [1536, 1536], P('gx', 'gy')
- second_gain_grad: float32 [1536], P('gy')
- router_grad: float32 [1536, 40], P('gx')
- gate_grad: float32 [1536, 40, 512], P('gx', None, 'gy')
- up_grad: float32 [1536, 40, 512], P('gx', None, 'gy')
- down_grad: float32 [1536, 40, 512], P('gx', None, 'gy')
Inputs may be any that keep to these rules, and one draw needn't show every extreme that they name: `routes`: each row names 8 different experts. Within the rows of one device (aligned blocks of 1024 rows) no expert is named by more than 256 rows, and in every draw some expert is named by exactly 256 rows of some block.
All inputs are finite; a program needn't handle non-finite values.
Results may differ from a plain program's by a relative error of at most 0.018.
Values may be sent and summed in bfloat16 or wider, within the bound.
No kernel may reach another device: no remote copies, remote signals or barrier semaphores. Data moves between devices by JAX's collectives and lax.ppermute only.
A program may use at most 448 MiB of HBM per device.

v0:
```python
from functools import partial
import math

import jax
import jax.numpy as jnp
from jax import lax
from jax.sharding import PartitionSpec as P

D = 1536
HD = 64
CAP = 256


epsilon = 1e-06
rope_base = 10000.0
masked = -1e30


def row_total(values):
    return lax.psum(values, "gy")


def features(values):
    return lax.all_gather(values, "gy", axis=1, tiled=True)


def partial_sums(values):
    return lax.psum_scatter(values, "gy", scatter_dimension=1, tiled=True)


def weight_grad(term, rows_here):
    return lax.psum_scatter(
        term(jnp.int32(0), rows_here * lax.axis_size("gx")).astype(jnp.bfloat16),
        "gx",
        scatter_dimension=0,
        tiled=True,
    ).astype(jnp.float32)


def keep_weights(weights):
    return (
        lax.all_gather(weights[0], "gx", axis=0, tiled=True),
        lax.all_gather(weights[1], "gx", axis=0, tiled=True),
        lax.all_gather(weights[2], "gx", axis=0, tiled=True),
        lax.all_gather(weights[3], "gx", axis=0, tiled=True),
    )


def with_weights(step, initial, whole):
    return step(initial, whole, 0)


def norm_scale(values, width):
    return lax.rsqrt(row_total(jnp.sum(values * values, axis=1)) / width + epsilon)[:, None]


def norm_back(values, row_scale, gain, grad_norm, width):
    scaled = grad_norm * gain
    inner_sum = row_total(jnp.sum(scaled * values, axis=1))[:, None]
    grad_in = row_scale * scaled - values * row_scale * row_scale * row_scale * inner_sum / width
    return (grad_in, jnp.sum(grad_norm * values * row_scale, axis=0))


def rope_tables(length, head_size):
    half_width = head_size // 2
    frequency = jnp.exp(
        jnp.arange(half_width, dtype=jnp.float32) * (-2.0 * math.log(rope_base) / head_size)
    )
    angles = jnp.arange(length, dtype=jnp.float32)[:, None] * frequency[None, :]
    return (jnp.cos(angles)[:, None, :], jnp.sin(angles)[:, None, :])


def rotate(values, cosine, sine_tab):
    half_width = values.shape[-1] // 2
    first_half = values[..., :half_width]
    second_half = values[..., half_width:]
    return jnp.concatenate(
        [
            first_half * cosine - second_half * sine_tab,
            second_half * cosine + first_half * sine_tab,
        ],
        axis=-1,
    )


def contract_rows(source, totals, pieces, offset):
    return tuple(
        (jnp.dot(source, part_rows, preferred_element_type=jnp.float32) for part_rows in pieces)
    )


def produce_columns(sources, running, pieces, offset):
    new_cols = sum(
        (
            lax.dot_general(
                source, part_rows, (((1,), (1,)), ((), ())), preferred_element_type=jnp.float32
            )
            for source, part_rows in zip(sources, pieces)
        )
    )
    return new_cols


def block_scores(query_block, key_rows, first_row, score_scale):
    scores = (
        jnp.einsum("qkgd,tkd->kgqt", query_block, key_rows, preferred_element_type=jnp.float32)
        * score_scale
    )
    row_ids = first_row + lax.broadcasted_iota(jnp.int32, scores.shape, 2)
    col_ids = lax.broadcasted_iota(jnp.int32, scores.shape, 3)
    return jnp.where(col_ids <= row_ids, scores, masked)


def attend(query_rows, key_rows, value_rows, score_scale, block_rows):
    length = query_rows.shape[0]

    def one_block(number):
        first_row = number * block_rows
        query_block = lax.dynamic_slice_in_dim(query_rows, first_row, block_rows, 0)
        scores = block_scores(query_block, key_rows, first_row, score_scale)
        top_score = jnp.max(scores, axis=3, keepdims=True)
        expo_score = jnp.exp(scores - top_score)
        row_sum = jnp.sum(expo_score, axis=3, keepdims=True)
        attn_probs = (expo_score / row_sum).astype(jnp.bfloat16)
        mixed = jnp.einsum(
            "kgqt,tkd->qkgd", attn_probs, value_rows, preferred_element_type=jnp.float32
        )
        return (mixed, (top_score + jnp.log(row_sum))[..., 0])

    mixed, log_total = lax.map(one_block, jnp.arange(length // block_rows))
    return (mixed.reshape(length, -1), log_total)


def attend_back(query_rows, key_rows, value_rows, grad_mixed, log_total, score_scale, block_rows):
    length = query_rows.shape[0]

    def one_block(carried, number):
        grad_keys, grad_values = carried
        first_row = number * block_rows
        query_block = lax.dynamic_slice_in_dim(query_rows, first_row, block_rows, 0)
        grad_block = lax.dynamic_slice_in_dim(grad_mixed, first_row, block_rows, 0)
        scores = block_scores(query_block, key_rows, first_row, score_scale)
        attn_probs = jnp.exp(scores - log_total[number][..., None])
        grad_probs = jnp.einsum(
            "qkgd,tkd->kgqt", grad_block, value_rows, preferred_element_type=jnp.float32
        )
        inner_sum = jnp.sum(attn_probs * grad_probs, axis=3, keepdims=True)
        grad_scores = (attn_probs * (grad_probs - inner_sum)).astype(jnp.bfloat16)
        grad_query = (
            jnp.einsum("kgqt,tkd->qkgd", grad_scores, key_rows, preferred_element_type=jnp.float32)
            * score_scale
        )
        grad_keys = (
            grad_keys
            + jnp.einsum(
                "kgqt,qkgd->tkd", grad_scores, query_block, preferred_element_type=jnp.float32
            )
            * score_scale
        )
        grad_values = grad_values + jnp.einsum(
            "kgqt,qkgd->tkd",
            attn_probs.astype(jnp.bfloat16),
            grad_block,
            preferred_element_type=jnp.float32,
        )
        return ((grad_keys, grad_values), grad_query)

    initial = (jnp.zeros(key_rows.shape, jnp.float32), jnp.zeros(value_rows.shape, jnp.float32))
    (grad_keys, grad_values), grad_query = lax.scan(
        one_block, initial, jnp.arange(length // block_rows)
    )
    return (grad_query.reshape(query_rows.shape), grad_keys, grad_values)


def shards(
    tokens,
    first_gain,
    w_query,
    w_key,
    w_value,
    w_out,
    second_gain,
    w_router,
    w_gate,
    w_up,
    w_down,
    routes,
    block_cotangent,
):
    length = tokens.shape[0]
    rows_here = w_query.shape[0]
    heads_here = w_query.shape[1] // HD
    groups_here = w_key.shape[1] // HD
    share_heads = heads_here // groups_here
    experts_n = w_router.shape[1]
    hidden_here = w_gate.shape[2]
    block_rows = min(512, length)
    score_scale = HD ** (-0.5)
    lead_flag = (lax.axis_index("gy") == 0).astype(jnp.float32)
    query_w = w_query.astype(jnp.bfloat16)
    key_w = w_key.astype(jnp.bfloat16)
    value_w = w_value.astype(jnp.bfloat16)
    out_w = w_out.astype(jnp.bfloat16)
    router_w = w_router.astype(jnp.bfloat16)
    gate_w = w_gate.astype(jnp.bfloat16)
    up_w = w_up.astype(jnp.bfloat16)
    down_w = w_down.astype(jnp.bfloat16)
    gain_one = lax.optimization_barrier(first_gain.astype(jnp.bfloat16)).astype(jnp.float32)
    gain_two = lax.optimization_barrier(second_gain.astype(jnp.bfloat16)).astype(jnp.float32)
    attn_whole = keep_weights((query_w, key_w, value_w, out_w))
    expert_whole = keep_weights((gate_w, up_w, router_w, down_w))
    qkv_whole = attn_whole[:3]
    out_whole = attn_whole[3]
    in_whole = expert_whole[:3]
    down_whole = expert_whole[3]
    token_f = tokens.astype(jnp.float32)
    scale_one = norm_scale(token_f, D)
    normed_one = features((token_f * scale_one * gain_one).astype(jnp.bfloat16))
    query_init = jnp.zeros((length, query_w.shape[1]), jnp.float32)
    pair_init = jnp.zeros((length, key_w.shape[1]), jnp.float32)
    query_raw, key_raw, value_raw = with_weights(
        partial(contract_rows, normed_one), (query_init, pair_init, pair_init), qkv_whole
    )
    cosine, sine_tab = rope_tables(length, HD)
    query_rows = rotate(query_raw.reshape(length, heads_here, HD), cosine, sine_tab).astype(
        jnp.bfloat16
    )
    key_rows = rotate(key_raw.reshape(length, groups_here, HD), cosine, sine_tab).astype(
        jnp.bfloat16
    )
    value_rows = value_raw.reshape(length, groups_here, HD).astype(jnp.bfloat16)
    query_group = query_rows.reshape(length, groups_here, share_heads, HD)
    mixed, log_total = attend(query_group, key_rows, value_rows, score_scale, block_rows)
    mixed = mixed.astype(jnp.bfloat16)
    attn_partial = with_weights(
        lambda running, part_rows, offset: produce_columns((mixed,), running, (part_rows,), offset),
        jnp.zeros((length, D), jnp.float32),
        out_whole,
    )
    residual = token_f + partial_sums(attn_partial)
    scale_two = norm_scale(residual, D)
    normed_two = features((residual * scale_two * gain_two).astype(jnp.bfloat16))
    chosen_hot = (
        routes[:, :, None] == jnp.arange(experts_n, dtype=jnp.int32)[None, None, :]
    ).astype(jnp.float32)
    member = jnp.sum(chosen_hot, axis=1).astype(jnp.bfloat16)
    lower_mask = (
        lax.broadcasted_iota(jnp.int32, (length, length), 1)
        < lax.broadcasted_iota(jnp.int32, (length, length), 0)
    ).astype(jnp.bfloat16)
    before = jnp.dot(lower_mask, member, preferred_element_type=jnp.float32)
    slot_rank = jnp.sum(before[:, None, :] * chosen_hot, axis=2).astype(jnp.int32)
    token_ids = jnp.broadcast_to(jnp.arange(length, dtype=jnp.int32)[:, None], routes.shape)
    slot_owner = jnp.full((experts_n, CAP), length, jnp.int32).at[routes, slot_rank].set(token_ids)
    owner_flat = slot_owner.reshape(-1)
    padded = jnp.concatenate([normed_two, jnp.zeros((1, D), jnp.bfloat16)], axis=0)
    slot_rows = padded[slot_owner]

    def expert_rows(totals, pieces, offset):
        row_count = pieces[0].shape[0]
        return (
            jnp.einsum("ecn,nef->ecf", slot_rows, pieces[0], preferred_element_type=jnp.float32),
            jnp.einsum("ecn,nef->ecf", slot_rows, pieces[1], preferred_element_type=jnp.float32),
            jnp.dot(normed_two, pieces[2], preferred_element_type=jnp.float32),
        )

    slot_init = jnp.zeros((experts_n, CAP, hidden_here), jnp.float32)
    gate_pre, up_pre, logits = with_weights(
        expert_rows, (slot_init, slot_init, jnp.zeros((length, experts_n), jnp.float32)), in_whole
    )
    picked = jnp.sum(logits[:, None, :] * chosen_hot, axis=2)
    gate_exp = jnp.exp(picked - jnp.max(picked, axis=1, keepdims=True))
    gate_probs = gate_exp / jnp.sum(gate_exp, axis=1, keepdims=True)
    slot_share = jnp.zeros((experts_n, CAP), jnp.float32).at[routes, slot_rank].set(gate_probs)
    sigmoid_g = jax.nn.sigmoid(gate_pre)
    silu_gate = gate_pre * sigmoid_g
    active = (silu_gate * up_pre).astype(jnp.bfloat16)

    def down_columns(running, part_rows, offset):
        row_count = part_rows.shape[0]
        out_cols = (
            jnp.einsum("ecf,nef->ecn", active, part_rows, preferred_element_type=jnp.float32)
            * slot_share[:, :, None]
        )
        token_cols = (
            jnp.zeros((length + 1, row_count), jnp.float32)
            .at[owner_flat]
            .add(out_cols.reshape(-1, row_count))[:length]
        )
        return token_cols

    expert_out = partial_sums(
        with_weights(down_columns, jnp.zeros((length, D), jnp.float32), down_whole)
    )
    block_out = (residual + expert_out).astype(jnp.bfloat16)
    cotangent = block_cotangent.astype(jnp.float32)
    cotangent_full = features(block_cotangent)
    cotangent_rows = jnp.concatenate([cotangent_full, jnp.zeros((1, D), jnp.bfloat16)], axis=0)[
        slot_owner
    ]
    slot_grad = (slot_share[:, :, None] * cotangent_rows).astype(jnp.bfloat16)

    def down_back(totals, part_rows, offset):
        row_count = part_rows.shape[0]
        out_cols = jnp.einsum("ecf,nef->ecn", active, part_rows, preferred_element_type=jnp.float32)
        return (
            jnp.einsum("ecn,nef->ecf", slot_grad, part_rows, preferred_element_type=jnp.float32),
            jnp.sum(cotangent_rows * out_cols, axis=2),
        )

    grad_active, grad_share = with_weights(
        down_back, (slot_init, jnp.zeros((experts_n, CAP), jnp.float32)), down_whole
    )

    def down_term(offset, row_count):
        return jnp.einsum("ecn,ecf->nef", slot_grad, active, preferred_element_type=jnp.float32)

    down_grad = weight_grad(down_term, rows_here)
    grad_gates = row_total(grad_share[routes, slot_rank])
    grad_picked = gate_probs * (
        grad_gates - jnp.sum(gate_probs * grad_gates, axis=1, keepdims=True)
    )
    grad_logits = jnp.sum(grad_picked[:, :, None] * chosen_hot, axis=1).astype(jnp.bfloat16)
    grad_gate = (grad_active * up_pre * sigmoid_g * (1.0 + gate_pre * (1.0 - sigmoid_g))).astype(
        jnp.bfloat16
    )
    grad_up = (grad_active * silu_gate).astype(jnp.bfloat16)

    def expert_term(offset, row_count):
        term_parts = [
            jnp.einsum(
                "ecn,ecf->nef", slot_rows, grad_gate, preferred_element_type=jnp.float32
            ).reshape(row_count, -1),
            jnp.einsum(
                "ecn,ecf->nef", slot_rows, grad_up, preferred_element_type=jnp.float32
            ).reshape(row_count, -1),
            lax.dot_general(
                normed_two,
                grad_logits,
                (((0,), (0,)), ((), ())),
                preferred_element_type=jnp.float32,
            ),
        ]
        return jnp.concatenate(term_parts, axis=1)

    expert_sums = weight_grad(expert_term, rows_here)
    span_cols = experts_n * hidden_here
    gate_grad = expert_sums[:, :span_cols].reshape(rows_here, experts_n, hidden_here)
    up_grad = expert_sums[:, span_cols : 2 * span_cols].reshape(rows_here, experts_n, hidden_here)
    router_grad = expert_sums[:, 2 * span_cols :]

    def expert_cols(running, pieces, offset):
        row_count = pieces[0].shape[0]
        slot_cols = jnp.einsum(
            "ecf,nef->ecn", grad_gate, pieces[0], preferred_element_type=jnp.float32
        ) + jnp.einsum("ecf,nef->ecn", grad_up, pieces[1], preferred_element_type=jnp.float32)
        token_cols = (
            jnp.zeros((length + 1, row_count), jnp.float32)
            .at[owner_flat]
            .add(slot_cols.reshape(-1, row_count))[:length]
        )
        router_cols = (
            lax.dot_general(
                grad_logits, pieces[2], (((1,), (1,)), ((), ())), preferred_element_type=jnp.float32
            )
            * lead_flag
        )
        return token_cols + router_cols

    grad_normed_two = partial_sums(
        with_weights(expert_cols, jnp.zeros((length, D), jnp.float32), in_whole)
    )
    grad_from_norm, second_gain_grad = norm_back(residual, scale_two, gain_two, grad_normed_two, D)
    grad_residual = cotangent + grad_from_norm
    grad_attn_full = features(grad_residual.astype(jnp.bfloat16))

    def out_term(offset, row_count):
        return lax.dot_general(
            grad_attn_full, mixed, (((0,), (0,)), ((), ())), preferred_element_type=jnp.float32
        )

    out_proj_grad = weight_grad(out_term, rows_here)
    grad_mixed = with_weights(
        lambda running, part_rows, offset: contract_rows(
            grad_attn_full, (running,), (part_rows,), offset
        )[0],
        jnp.zeros((length, heads_here * HD), jnp.float32),
        out_whole,
    ).astype(jnp.bfloat16)
    grad_query, grad_keys, grad_values = attend_back(
        query_group,
        key_rows,
        value_rows,
        grad_mixed.reshape(length, groups_here, share_heads, HD),
        log_total,
        score_scale,
        block_rows,
    )
    grad_q_raw = (
        rotate(grad_query.reshape(length, heads_here, HD), cosine, -sine_tab)
        .astype(jnp.bfloat16)
        .reshape(length, -1)
    )
    grad_k_raw = rotate(grad_keys, cosine, -sine_tab).astype(jnp.bfloat16).reshape(length, -1)
    grad_v_raw = grad_values.astype(jnp.bfloat16).reshape(length, -1)
    grad_qkv = jnp.concatenate([grad_q_raw, grad_k_raw, grad_v_raw], axis=1)

    def attn_term(offset, row_count):
        return lax.dot_general(
            normed_one, grad_qkv, (((0,), (0,)), ((), ())), preferred_element_type=jnp.float32
        )

    attn_sums = weight_grad(attn_term, rows_here)
    query_cols = query_w.shape[1]
    pair_cols = key_w.shape[1]
    query_grad = attn_sums[:, :query_cols]
    key_grad = attn_sums[:, query_cols : query_cols + pair_cols]
    value_grad = attn_sums[:, query_cols + pair_cols :]
    grad_normed_one = partial_sums(
        with_weights(
            partial(produce_columns, (grad_q_raw, grad_k_raw, grad_v_raw)),
            jnp.zeros((length, D), jnp.float32),
            qkv_whole,
        )
    )
    grad_from_first, first_gain_grad = norm_back(token_f, scale_one, gain_one, grad_normed_one, D)
    input_grad = (grad_residual + grad_from_first).astype(jnp.bfloat16)
    first_gain_grad, second_gain_grad = lax.psum((first_gain_grad, second_gain_grad), "gx")
    return (
        block_out,
        input_grad,
        first_gain_grad,
        query_grad,
        key_grad,
        value_grad,
        out_proj_grad,
        second_gain_grad,
        router_grad,
        gate_grad,
        up_grad,
        down_grad,
    )


def solution(mesh):
    placed = (
        P("gx", "gy"),
        P("gy"),
        P("gx", "gy"),
        P("gx", "gy"),
        P("gx", "gy"),
        P("gx", "gy"),
        P("gy"),
        P("gx", None),
        P("gx", None, "gy"),
        P("gx", None, "gy"),
        P("gx", None, "gy"),
        P("gx", None),
        P("gx", "gy"),
    )
    return jax.shard_map(
        shards,
        mesh=mesh,
        in_specs=placed,
        out_specs=(
            P("gx", "gy"),
            P("gx", "gy"),
            P("gy"),
            P("gx", "gy"),
            P("gx", "gy"),
            P("gx", "gy"),
            P("gx", "gy"),
            P("gy"),
            P("gx", None),
            P("gx", None, "gy"),
            P("gx", None, "gy"),
            P("gx", None, "gy"),
        ),
        check_vma=False,
    )
```

profile of v0, /device:TPU:0, one launch (start us, length us, event | category | flops | bytes accessed | tf_op | source)
XLA Modules:
  0.0 1976.8 jit_solution(15884206359101808204)
XLA Ops:
  50.7 36.6 %all-gather.11.cloned.1.call-done = bf16[1024,1536]{1,0:T(8,128)(2,1)} async-done(((bf16[1024,384]{1,0:T(8,128)(2,1)}), bf16[1024,1536]{1,0:T(8,128)(2,1)}) %all-gather.11.cloned.1.call-update) | async-done | bytes 3145744 | tf_op jit(solution)/shard_map/all_gather | solution.py:24
  117.9 26.2 %while.27 = (s32[]{:T(128)}, bf16[2,512,2,3,64]{1,4,3,2,0:T(8,128)(2,1)S(1)}, f32[2,2,3,512]{3,2,1,0:T(4,128)}, s32[2]{0:T(128)S(1)}, bf16[1024,2,3,64]{0,3,2,1:...) while((s32[]{:T(128)}, ...), condition=%wide.region_5.6_spmd, body=%wide.region_2.5_spmd.sunk | while | flops 852489728 | bytes 39572144 | solution.py:130
  152.5 110.2 %reduce-scatter.11.cloned.1.call-done = f32[1024,384]{1,0:T(8,128)} async-done(((f32[1024,1536]{1,0:T(8,128)}), f32[1024,384]{1,0:T(8,128)}) %reduce-scatter.11.cloned.1.call-update) | async-done | bytes 1572880 | tf_op jit(solution)/shard_map/reduce_scatter | solution.py:28
  301.1 26.8 %all-gather.25.cloned.1.call-done = bf16[1024,1536]{1,0:T(8,128)(2,1)} async-done(((bf16[1024,384]{1,0:T(8,128)(2,1)}), bf16[1024,1536]{1,0:T(8,128)(2,1)}) %all-gather.25.cloned.1.call-update) | async-done | bytes 3145744 | tf_op jit(solution)/shard_map/all_gather | solution.py:24
  330.0 61.9 %all-gather.17.cloned.1.call-done = bf16[1024,1536]{1,0:T(8,128)(2,1)} async-done(((bf16[1024,384]{1,0:T(8,128)(2,1)}), bf16[1024,1536]{1,0:T(8,128)(2,1)}) %all-gather.17.cloned.1.call-update) | async-done | bytes 3145744 | tf_op jit(solution)/shard_map/all_gather | solution.py:24
  399.5 30.5 %scatter_custom_fusion.2 = s32[10240]{0:T(1024)S(1)} fusion(s32[8192]{0:T(1024)S(1)} %reshape.274, s32[8192]{0:T(1024)S(1)} %reshape.276, s32[]{:T(128)} %constant.54.clone.1), kind=kCustom, calls=%fused_computation.162 | custom fusion | bytes 40964
  434.3 64.1 %gather_fusion = bf16[10240,1536]{1,0:T(8,128)(2,1)} fusion(bf16[1025,1536]{1,0:T(8,128)(2,1)} %concatenate.44, s32[10240]{0:T(1024)S(1)} %broadcast_clamp_fusion), kind=kCustom, calls=%fused_computation | custom fusion | bytes 62955520 | tf_op jit(solution)/shard_map/gather | solution.py:257
  498.4 46.4 %gather_fusion.1 = bf16[10240,1536]{1,0:T(8,128)(2,1)} fusion(bf16[1025,1536]{1,0:T(8,128)(2,1)S(1)} %concatenate.45, s32[10240]{0:T(1024)S(1)} %broadcast_clamp_fusion), kind=kCustom, calls=%fused_computation.1 | custom fusion | bytes 62955520 | tf_op jit(solution)/shard_map/gather | solution.py:298
  591.6 62.1 %all-gather.23.cloned.1.call-done = bf16[1536,40,128]{2,0,1:T(8,128)(2,1)} async-done(((bf16[192,40,128]{2,0,1:T(8,128)(2,1)}), bf16[1536,40,128]{2,0,1:T(8,128)(2,1)}) %all-gather.23.cloned.1.call-update) | async-done | bytes 15728656 | tf_op jit(solution)/shard_map/all_gather | solution.py:45
  653.7 38.7 %fusion.42 = (f32[40,256]{1,0:T(8,128)S(1)}, f32[40,256,1536]{2,1,0:T(8,128)}) fusion(bf16[40,256,1536]{2,1,0:T(8,128)(2,1)} %bitcast.233, bf16[40,256,128]{2,1,0:T(8,128)(2,1)S(1)} %get-tuple-element.262, bf16[1536,40,128]{2,0,1:T(8,128)(2,1)} %all-gather.23.cloned.1.call-done), kind=kOutput, calls=%fused_computation.61 | convolution fusion | flops 4073707520 | bytes 112762880 | tf_op jit(solution)/shard_map/ecf,nef->ecn/dot_general | solution.py:282
  692.5 65.0 %gather_fusion.2 = f32[8192]{0:T(1024)S(1)} fusion(f32[40,256]{1,0:T(8,128)S(1)} %get-tuple-element.264, s32[8192]{0:T(1024)S(1)} %reshape.252), kind=kCustom, calls=%fused_computation.2 | custom fusion | bytes 131072 | tf_op jit(solution)/shard_map/gather | solution.py:319
  777.7 30.6 %scatter_custom_fusion.3 = f32[10240]{0:T(1024)S(1)} fusion(s32[8192]{0:T(1024)} %copy-done.59, f32[8192]{0:T(1024)S(1)} %reshape.282, f32[]{:T(128)} %constant.50.clone.1), kind=kCustom, calls=%fused_computation.160 | custom fusion | bytes 41472
  831.5 28.0 %fusion.97 = f32[40,256,1536]{2,1,0:T(8,128)} fusion(bf16[40,256,128]{2,1,0:T(8,128)(2,1)S(1)} %get-tuple-element.243, bf16[1536,40,128]{2,0,1:T(8,128)(2,1)} %all-gather.19.cloned.1.call-done), kind=kOutput, calls=%fused_computation.178 | convolution fusion | flops 4026531840 | bytes 81264640 | tf_op jit(solution)/shard_map/ecf,nef->ecn/dot_general | solution.py:354
  859.5 48.1 %convolution_add_fusion = f32[40,256,1536]{2,1,0:T(8,128)} fusion(f32[40,256,1536]{2,1,0:T(8,128)} %fusion.97, bf16[40,256,128]{2,1,0:T(8,128)(2,1)} %get-tuple-element.242, bf16[1536,40,128]{2,0,1:T(8,128)(2,1)} %all-gather.21.cloned.1.call-done), kind=kOutput, calls=%fused_computation.62 | convolution fusion | flops 4042260480 | bytes 144179200 | tf_op jit(solution)/shard_map/ecf,nef->ecn/dot_general | solution.py:356
  907.6 102.6 %scatter_custom_fusion.1 = f32[1025,1536]{1,0:T(8,128)} fusion(s32[10240]{0:T(1024)} %bitcast.259, f32[10240,1536]{1,0:T(8,128)} %bitcast.236, f32[]{:T(128)} %constant.50.clone.1), kind=kCustom, calls=%fused_computation.83 | custom fusion | flops 15728640 | bytes 6298112 | tf_op jit(solution)/shard_map/scatter-add | solution.py:360
  1016.7 42.7 %broadcast_multiply_fusion = f32[40,256,1536]{2,1,0:T(8,128)} fusion(f32[40,256,1536]{2,1,0:T(8,128)} %get-tuple-element.265, f32[40,256]{1,0:T(8,128)S(1)} %reshape.234), kind=kLoop, calls=%fused_computation.64 | loop fusion | flops 15728640 | bytes 125870080 | tf_op jit(solution)/shard_map/mul | solution.py:282
  1059.4 102.5 %scatter_custom_fusion = f32[1025,1536]{1,0:T(8,128)} fusion(s32[10240]{0:T(1024)} %bitcast.260, f32[10240,1536]{1,0:T(8,128)} %bitcast.239, f32[]{:T(128)} %constant.50.clone.1), kind=kCustom, calls=%fused_computation.85 | custom fusion | flops 15728640 | bytes 6298112 | tf_op jit(solution)/shard_map/scatter-add | solution.py:288
  1181.1 95.4 %reduce-scatter.13.cloned.1.call-done = f32[1024,384]{1,0:T(8,128)} async-done(((f32[1024,1536]{1,0:T(8,128)}), f32[1024,384]{1,0:T(8,128)}) %reduce-scatter.13.cloned.1.call-update) | async-done | bytes 1572880 | tf_op jit(solution)/shard_map/reduce_scatter | solution.py:28
  1280.8 63.8 %all-gather.27.cloned.1.call-done = bf16[1024,1536]{1,0:T(8,128)(2,1)} async-done(((bf16[1024,384]{1,0:T(8,128)(2,1)}), bf16[1024,1536]{1,0:T(8,128)(2,1)}) %all-gather.27.cloned.1.call-update) | async-done | bytes 3145744 | tf_op jit(solution)/shard_map/all_gather | solution.py:24
  1353.2 111.8 %while.28 = (s32[]{:T(128)}, f32[1024,2,64]{0,2,1:T(8,128)S(1)}, f32[1024,2,64]{0,2,1:T(8,128)}, f32[2,512,2,3,64]{1,0,4,3,2:T(2,128)}, s32[2]{0:T(128)S(1)}, /*...) while((s32[]{:T(128)}, f32[1024,2,64]{0,2,1:T(8,128)S(1)}, ...), condition=%wide.region_28.29_spmd.clone, body=%wide.region_26.28_spmd.clone.sunk | while | flops 2045572608 | bytes 195105200 | solution.py:169
  1569.3 54.5 %pad_maximum_fusion = bf16[1536,10280]{0,1:T(8,128)(2,1)} fusion(bf16[1536,40]{0,1:T(8,128)(2,1)S(1)} %convolution_convert_fusion.4, bf16[1536,5120]{0,1:T(8,128)(2,1)} %bitcast.238, bf16[1536,5120]{0,1:T(8,128)(2,1)} %bitcast.237), kind=kLoop, calls=%fused_computation.63 | loop fusion | flops 94740480 | bytes 63160320 | tf_op jit(solution)/shard_map/concatenate | solution.py:344
  1623.9 37.6 %copy.95 = bf16[1536,10280]{1,0:T(8,128)(2,1)} copy(bf16[1536,10280]{0,1:T(8,128)(2,1)} %pad_maximum_fusion) | data formatting | bytes 63160320
  1670.3 69.4 %reduce-scatter.17.cloned.1.call-done = f32[1024,384]{1,0:T(8,128)} async-done(((f32[1024,1536]{1,0:T(8,128)}), f32[1024,384]{1,0:T(8,128)}) %reduce-scatter.17.cloned.1.call-update) | async-done | bytes 1572880 | tf_op jit(solution)/shard_map/reduce_scatter | solution.py:28
  1770.4 171.9 %reduce-scatter.25.cloned.1.call-done = bf16[192,10280]{1,0:T(8,128)(2,1)} async-done(((bf16[1536,10280]{1,0:T(8,128)(2,1)}), bf16[192,10280]{1,0:T(8,128)(2,1)}) %reduce-scatter.25.cloned.1.call-update) | async-done | bytes 3947536
  (345 shorter events, 565.2 us)
Async XLA Ops:
  7.2 80.2 %all-gather.11.cloned.1.call-start = ((), (), s32[]{:S(2)}) async-start(), calls=%async_computation.8 | async-start | bytes 3932160 | tf_op jit(solution)/shard_map/all_gather | solution.py:24
  25.6 86.8 %all-gather.13.cloned.1.call-start = ((), (), s32[]{:S(2)}) async-start(), calls=%async_computation.9 | async-start | bytes 1327104 | tf_op jit(solution)/shard_map/all_gather | solution.py:42
  27.4 117.8 %all-gather.15.cloned.1.call-start = ((), (), s32[]{:S(2)}) async-start(), calls=%async_computation.10 | async-start | bytes 1327104 | tf_op jit(solution)/shard_map/all_gather | solution.py:45
  29.1 233.6 %reduce-scatter.11.cloned.1.call-start = ((), (), s32[]{:S(2)}) async-start(), calls=%async_computation.11 | async-start | bytes 7864320 | tf_op jit(solution)/shard_map/reduce_scatter | solution.py:28
  151.7 110.9 %copy-start.8 = (bf16[1024,384]{1,0:T(8,128)(2,1)S(1)}, bf16[1024,384]{1,0:T(8,128)(2,1)}, u32[]{:S(2)}) copy-start(bf16[1024,384]{1,0:T(8,128)(2,1)} %param.17) | copy-start | bytes 2359300
  151.8 176.2 %all-gather.25.cloned.1.call-start = ((), (), s32[]{:S(2)}) async-start(), calls=%async_computation.17 | async-start | bytes 3932160 | tf_op jit(solution)/shard_map/all_gather | solution.py:24
  152.4 239.5 %all-gather.17.cloned.1.call-start = ((), (), s32[]{:S(2)}) async-start(), calls=%async_computation.12 | async-start | bytes 3932160 | tf_op jit(solution)/shard_map/all_gather | solution.py:24
  152.4 129.3 %copy-start.60 = (f32[384]{0:T(512)}, f32[384]{0:T(512)S(1)}, u32[]{:S(2)}) copy-start(f32[384]{0:T(512)S(1)} %convert_element_type.181) | copy-start | bytes 4612
  277.5 269.1 %all-gather.19.cloned.1.call-start = ((), (), s32[]{:S(2)}) async-start(), calls=%async_computation.13 | async-start | bytes 17694720 | tf_op jit(solution)/shard_map/all_gather | solution.py:42
  281.8 285.4 %all-gather.21.cloned.1.call-start = ((), (), s32[]{:S(2)}) async-start(), calls=%async_computation.14 | async-start | bytes 17694720 | tf_op jit(solution)/shard_map/all_gather | solution.py:43
  286.0 367.7 %all-gather.23.cloned.1.call-start = ((), (), s32[]{:S(2)}) async-start(), calls=%async_computation.15 | async-start | bytes 17694720 | tf_op jit(solution)/shard_map/all_gather | solution.py:45
  290.3 877.6 %reduce-scatter.15.cloned.1.call-start = ((), (), s32[]{:S(2)}) async-start(), calls=%async_computation.18 | async-start | bytes 7864320 | tf_op jit(solution)/shard_map/reduce_scatter | solution.py:28
  777.4 232.8 %copy-start.42 = (bf16[1024,40]{0,1:T(8,128)(2,1)}, bf16[1024,40]{0,1:T(8,128)(2,1)S(1)}, u32[]{:S(2)}) copy-start(bf16[1024,40]{0,1:T(8,128)(2,1)S(1)} %select_reduce_fusion) | copy-start | bytes 245764
  808.3 208.4 %copy-start.40 = (f32[40,256]{1,0:T(8,128)}, f32[40,256]{1,0:T(8,128)S(1)}, u32[]{:S(2)}) copy-start(f32[40,256]{1,0:T(8,128)S(1)} %reshape.234) | copy-start | bytes 122884
  1016.7 259.8 %reduce-scatter.13.cloned.1.call-start = ((), (), s32[]{:S(2)}) async-start(), calls=%async_computation.16 | async-start | bytes 7864320 | tf_op jit(solution)/shard_map/reduce_scatter | solution.py:28
  1167.7 108.7 %copy-start.29 = (bf16[1024,384]{1,0:T(8,128)(2,1)S(1)}, bf16[1024,384]{1,0:T(8,128)(2,1)}, u32[]{:S(2)}) copy-start(bf16[1024,384]{1,0:T(8,128)(2,1)} %param.29) | copy-start | bytes 2359300
  1167.8 176.8 %all-gather.27.cloned.1.call-start = ((), (), s32[]{:S(2)}) async-start(), calls=%async_computation.19 | async-start | bytes 3932160 | tf_op jit(solution)/shard_map/all_gather | solution.py:24
  1171.6 173.0 %copy-start.22 = (bf16[48,8,2,512]{3,1,2,0:T(8,128)(2,1)S(1)}, bf16[48,8,2,512]{3,1,2,0:T(8,128)(2,1)}, u32[]{:S(2)}) copy-start(bf16[48,8,2,512]{3,1,2,0:T(8,128)(2,1)} %copy-done.21) | copy-start | bytes 2359300
  1280.7 380.9 %reduce-scatter.21.cloned.1.call-start = ((), (), s32[]{:S(2)}) async-start(), calls=%async_computation.22 | async-start | bytes 1327104 | tf_op jit(solution)/shard_map/reduce_scatter | solution.py:32
  1349.4 314.0 %reduce-scatter.19.cloned.1.call-start = ((), (), s32[]{:S(2)}) async-start(), calls=%async_computation.21 | async-start | bytes 2211840 | tf_op jit(solution)/shard_map/reduce_scatter | solution.py:32
  1353.2 115.7 %copy-start.28 = (f32[1024,32]{0,1:T(8,128)S(1)}, f32[1024,32]{0,1:T(8,128)}, u32[]{:S(2)}) copy-start(f32[1024,32]{0,1:T(8,128)} %copy-done.27) | copy-start | bytes 393220
  1475.2 191.4 %reduce-scatter.23.cloned.1.call-start = ((), (), s32[]{:S(2)}) async-start(), calls=%async_computation.23 | async-start | bytes 17694720 | tf_op jit(solution)/shard_map/reduce_scatter | solution.py:32
  1515.5 224.2 %reduce-scatter.17.cloned.1.call-start = ((), (), s32[]{:S(2)}) async-start(), calls=%async_computation.20 | async-start | bytes 7864320 | tf_op jit(solution)/shard_map/reduce_scatter | solution.py:28
  1523.2 419.1 %reduce-scatter.25.cloned.1.call-start = ((), (), s32[]{:S(2)}) async-start(), calls=%async_computation.24 | async-start | bytes 35831808
  (69 other events, 1722.2 us)
Sparse Core Ops, SparseCore 0:
  25.8 61.5 all-gather.10
  89.8 22.6 all-gather.12
  115.0 24.0 all-gather.14
  151.9 110.7 reduce-scatter.10
  264.1 63.8 all-gather.24
  329.9 61.9 all-gather.16
  394.4 84.0 all-gather.18
  480.9 85.4 all-gather.20
  568.3 85.4 all-gather.22
  1016.8 107.9 reduce-scatter.14
  1167.9 108.4 reduce-scatter.12
  1280.8 63.7 all-gather.26
  1349.5 35.3 reduce-scatter.20
  1475.3 38.8 reduce-scatter.18
  1517.5 109.1 reduce-scatter.22
  1628.9 110.7 reduce-scatter.16
  1743.2 199.0 reduce-scatter.24
where the time goes:
time: 1980 us
  waiting for transfers between devices  721 us (36%)
  local copies, waits for them, and re-layouts  407 us (21%)
  matrix products  362 us (18%)
  other arithmetic  357 us (18%)
  blocking collectives  108 us (5%)
    reduce_scatter x4, waiting for transfers between devices, partial_sums(): return lax.psum_scatter(values, 'gy', scatter_dimension=1, tiled=True)  275 us
    all_gather x4, waiting for transfers between devices, features(): return lax.all_gather(values, 'gy', axis=1, tiled=True)  189 us
    unnamed x18, waiting for transfers between devices  173 us
    unnamed x142, local copies, waits for them, and re-layouts  141 us
    scatter-add x1, other arithmetic, expert_cols(): token_cols = jnp.zeros((length + 1, row_count), jnp.float32).at[owner_fla...  103 us
    scatter-add x1, other arithmetic, down_columns(): token_cols = jnp.zeros((length + 1, row_count), jnp.float32).at[owner_fla...  102 us
    gather x3, local copies, waits for them, and re-layouts, shards(): grad_gates = row_total(grad_share[routes, slot_rank])  65.5 us
    psum x5, blocking collectives, row_total(): return lax.psum(values, 'gy')  64.5 us
  transfers between devices with their start and end apart: 17, of which 10 were waited for; matrix products, arithmetic and copies ran while one was open for 36% of the time, Pallas kernels for 0%

commit v1 on v0

v1 whole, which is shorter than its diff:
```python
from functools import partial
import math

import jax
import jax.numpy as jnp
import numpy as np
from jax import lax
from jax.experimental import pallas as pl
from jax.experimental.pallas import tpu as pltpu
from jax.sharding import PartitionSpec as P

D = 1536
HD = 64
FFZ = 128
epsilon = 1e-06
rope_base = 10000.0
masked = -1e30
BF = jnp.bfloat16
F32 = jnp.float32


def dot(a, b, dims=((1,), (0,)), out=F32):
    return lax.dot_general(a, b, (dims, ((), ())), preferred_element_type=F32).astype(out)


def flip(bit, size):
    return [(i, i ^ bit) for i in range(size)]


def swap_core(x):
    return lax.ppermute(x, "gx", flip(1, lax.axis_size("gx")))


def swap_x(x):
    return lax.ppermute(x, "gx", flip(2, lax.axis_size("gx")))


def swap_y(x):
    return lax.ppermute(x, "gx", flip(4, lax.axis_size("gx")))


def core_groups(size):
    return [[i for i in range(size) if i % 2 == c] for c in range(2)]


def place_chips(chunks, chip):
    rows = chunks[0].shape[0]
    whole = jnp.zeros((4 * rows, chunks[0].shape[1]), chunks[0].dtype)
    for k, part in enumerate(chunks):
        whole = lax.dynamic_update_slice(whole, part, ((chip ^ k) * rows, 0))
    return whole


def gather_chips(own):
    size = lax.axis_size("gx")
    if size != 8:
        return lax.all_gather(own, "gx", axis=0, tiled=True, axis_index_groups=core_groups(size))
    half = own.shape[1] // 2
    from_x = swap_x(own)
    from_y = swap_y(own)
    corner = jnp.concatenate([swap_y(from_x[:, :half]), swap_x(from_y[:, half:])], axis=1)
    return place_chips([own, from_x, from_y, corner], lax.axis_index("gx") // 2)


def reduce_chips(term, rows, half):
    size = lax.axis_size("gx")
    chip = lax.axis_index("gx") // 2
    if size != 8:
        whole = jnp.concatenate([term(0, rows * size // 2, 0), term(0, rows * size // 2, 1)], axis=1)
        return lax.psum_scatter(
            whole, "gx", scatter_dimension=0, tiled=True, axis_index_groups=core_groups(size)
        )
    a1, a3 = term((chip ^ 1) * rows, rows, 0), term((chip ^ 3) * rows, rows, 0)
    b2, b3 = term((chip ^ 2) * rows, rows, 1), term((chip ^ 3) * rows, rows, 1)
    got_a0, got_a2 = swap_x(a1), swap_x(a3)
    got_b0, got_b1 = swap_y(b2), swap_y(b3)
    a0, a2 = term(chip * rows, rows, 0), term((chip ^ 2) * rows, rows, 0)
    b0, b1 = term(chip * rows, rows, 1), term((chip ^ 1) * rows, rows, 1)
    last_a, last_b = swap_y(a2 + got_a2), swap_x(b1 + got_b1)
    side_a = a0.astype(F32) + got_a0 + last_a
    side_b = b0.astype(F32) + got_b0 + last_b
    return jnp.concatenate([side_a, side_b], axis=1).astype(BF)


def rope_tables(length):
    frequency = np.exp(np.arange(HD // 2, dtype=np.float32) * np.float32(-2.0 * math.log(rope_base) / HD))
    angles = np.arange(length, dtype=np.float32)[:, None] * frequency[None, :].astype(np.float32)
    return (jnp.asarray(np.cos(angles), F32)[:, None, :], jnp.asarray(np.sin(angles), F32)[:, None, :])


def rotate(values, cosine, sine_tab):
    half_width = values.shape[-1] // 2
    first_half = values[..., :half_width]
    second_half = values[..., half_width:]
    return jnp.concatenate(
        [
            first_half * cosine - second_half * sine_tab,
            second_half * cosine + first_half * sine_tab,
        ],
        axis=-1,
    )


def block_scores(query_block, key_rows, first_row, score_scale):
    scores = (
        jnp.einsum("qkgd,tkd->kgqt", query_block, key_rows, preferred_element_type=jnp.float32)
        * score_scale
    )
    row_ids = first_row + lax.broadcasted_iota(jnp.int32, scores.shape, 2)
    col_ids = lax.broadcasted_iota(jnp.int32, scores.shape, 3)
    return jnp.where(col_ids <= row_ids, scores, masked)


def attend(query_rows, key_rows, value_rows, score_scale, block_rows):
    length = query_rows.shape[0]

    def one_block(number):
        first_row = number * block_rows
        query_block = lax.dynamic_slice_in_dim(query_rows, first_row, block_rows, 0)
        scores = block_scores(query_block, key_rows, first_row, score_scale)
        top_score = jnp.max(scores, axis=3, keepdims=True)
        expo_score = jnp.exp(scores - top_score)
        row_sum = jnp.sum(expo_score, axis=3, keepdims=True)
        attn_probs = (expo_score / row_sum).astype(jnp.bfloat16)
        mixed = jnp.einsum(
            "kgqt,tkd->qkgd", attn_probs, value_rows, preferred_element_type=jnp.float32
        )
        return (mixed, (top_score + jnp.log(row_sum))[..., 0])

    mixed, log_total = lax.map(one_block, jnp.arange(length // block_rows))
    return (mixed.reshape(length, -1), log_total)


def attend_back(query_rows, key_rows, value_rows, grad_mixed, log_total, score_scale, block_rows):
    length = query_rows.shape[0]

    def one_block(carried, number):
        grad_keys, grad_values = carried
        first_row = number * block_rows
        query_block = lax.dynamic_slice_in_dim(query_rows, first_row, block_rows, 0)
        grad_block = lax.dynamic_slice_in_dim(grad_mixed, first_row, block_rows, 0)
        scores = block_scores(query_block, key_rows, first_row, score_scale)
        attn_probs = jnp.exp(scores - log_total[number][..., None])
        grad_probs = jnp.einsum(
            "qkgd,tkd->kgqt", grad_block, value_rows, preferred_element_type=jnp.float32
        )
        inner_sum = jnp.sum(attn_probs * grad_probs, axis=3, keepdims=True)
        grad_scores = (attn_probs * (grad_probs - inner_sum)).astype(jnp.bfloat16)
        grad_query = (
            jnp.einsum("kgqt,tkd->qkgd", grad_scores, key_rows, preferred_element_type=jnp.float32)
            * score_scale
        )
        grad_keys = (
            grad_keys
            + jnp.einsum(
                "kgqt,qkgd->tkd", grad_scores, query_block, preferred_element_type=jnp.float32
            )
            * score_scale
        )
        grad_values = grad_values + jnp.einsum(
            "kgqt,qkgd->tkd",
            attn_probs.astype(jnp.bfloat16),
            grad_block,
            preferred_element_type=jnp.float32,
        )
        return ((grad_keys, grad_values), grad_query)

    initial = (jnp.zeros(key_rows.shape, jnp.float32), jnp.zeros(value_rows.shape, jnp.float32))
    (grad_keys, grad_values), grad_query = lax.scan(
        one_block, initial, jnp.arange(length // block_rows)
    )
    return (grad_query.reshape(query_rows.shape), grad_keys, grad_values)


def expert_body(h_ref, wg_ref, wu_ref, draw_ref, gate_ref, dg_ref, du_ref, ga_ref, dsum_ref):
    step = pl.program_id(1)
    h = h_ref[...]
    g = jnp.dot(h, wg_ref[...], preferred_element_type=F32)
    u = jnp.dot(h, wu_ref[...], preferred_element_type=F32)
    lanes = lax.broadcasted_iota(jnp.int32, gate_ref.shape, 1)
    sums = dsum_ref[...]
    sums = jnp.where(step == 0, jnp.zeros_like(sums), sums)
    for half in range(2):
        cols = slice(half * FFZ, (half + 1) * FFZ)
        expert = step * 2 + half
        hot = lanes == expert
        gate = jnp.sum(jnp.where(hot, gate_ref[...], 0.0), axis=1, keepdims=True)
        gg, uu = g[:, cols], u[:, cols]
        draw = draw_ref[:, cols].astype(F32)
        sig = 1.0 / (1.0 + jnp.exp(-gg))
        silu = gg * sig
        act = silu * uu
        back = gate * draw
        ga_ref[:, cols] = (gate * act).astype(BF)
        du_ref[:, cols] = (back * silu).astype(BF)
        dg_ref[:, cols] = (back * uu * (sig + silu * (1.0 - sig))).astype(BF)
        sums = jnp.where(hot, jnp.sum(act * draw, axis=1, keepdims=True), sums)
    dsum_ref[...] = sums


def expert_forward(h, w_gate, w_up, draw, gate):
    tokens, width = draw.shape
    rows = 1024
    steps = width // (2 * FFZ)
    wide = pl.BlockSpec((rows, 2 * FFZ), lambda i, j: (i, j))
    weight = pl.BlockSpec((D, 2 * FFZ), lambda i, j: (0, j))
    small = pl.BlockSpec((rows, 128), lambda i, j: (i, 0))
    return pl.pallas_call(
        expert_body,
        grid=(tokens // rows, steps),
        in_specs=[pl.BlockSpec((rows, D), lambda i, j: (i, 0)), weight, weight, wide, small],
        out_specs=[wide, wide, wide, small],
        out_shape=[jax.ShapeDtypeStruct((tokens, width), BF)] * 3
        + [jax.ShapeDtypeStruct((tokens, 128), F32)],
        compiler_params=pltpu.CompilerParams(vmem_limit_bytes=56 * 1024 * 1024),
        cost_estimate=pl.CostEstimate(
            flops=4 * tokens * D * width, bytes_accessed=tokens * width * 8 + D * width * 8, transcendentals=tokens * width
        ),
    )(h, w_gate, w_up, draw, gate)


def pad_lanes(x, width=128):
    return jnp.pad(x, ((0, 0), (0, width - x.shape[1])))


def shards(
    tokens,
    first_gain,
    w_query,
    w_key,
    w_value,
    w_out,
    second_gain,
    w_router,
    w_gate,
    w_up,
    w_down,
    routes,
    block_cotangent,
):
    length = tokens.shape[0]
    rows_here = w_query.shape[0]
    chip_rows = 2 * rows_here
    heads_here = w_query.shape[1] // HD
    groups_here = w_key.shape[1] // HD
    share_heads = heads_here // groups_here
    experts_n = w_router.shape[1]
    mine_n = experts_n // 2
    hidden_here = w_gate.shape[2]
    span = mine_n * hidden_here
    slice_cols = tokens.shape[1]
    block_rows = min(512, length)
    score_scale = HD ** (-0.5)
    core = lax.axis_index("gx") % 2
    plane = lax.axis_index("gy")

    gains = jnp.stack([first_gain, second_gain]).astype(BF)
    gains = jnp.pad(gains, ((0, 14), (0, 0)))
    joined = lax.all_gather(jnp.concatenate([tokens, gains], axis=0), "gy", axis=1, tiled=True)
    token_full = joined[:length]
    gain_full = joined[length : length + 2].astype(F32)
    gain_one, gain_two = gain_full[0], gain_full[1]

    attn_own = jnp.concatenate(
        [w_query.astype(BF), w_key.astype(BF), w_value.astype(BF), w_out.astype(BF), pad_lanes(w_router.astype(BF))],
        axis=1,
    )
    attn_pair = swap_core(attn_own)

    def core_order(own, other):
        first = jnp.where(core == 0, own, other)
        second = jnp.where(core == 0, other, own)
        return first, second

    attn_whole = gather_chips(jnp.concatenate(core_order(attn_own, attn_pair), axis=0))
    query_cols, pair_cols = w_query.shape[1], w_key.shape[1]
    qkv_cols = query_cols + 2 * pair_cols
    qkv_w = attn_whole[:, :qkv_cols]
    out_w = attn_whole[:, qkv_cols : qkv_cols + w_out.shape[1]]
    router_w = attn_whole[:, qkv_cols + w_out.shape[1] :]

    def expert_rows(weight):
        both = weight.astype(BF).reshape(rows_here, 2, span)
        keep = jnp.where(core == 0, both[:, 0], both[:, 1])
        give = jnp.where(core == 0, both[:, 1], both[:, 0])
        return gather_chips(jnp.concatenate(core_order(keep, swap_core(give)), axis=0))

    down_w = expert_rows(w_down)
    gate_w = expert_rows(w_gate)
    up_w = expert_rows(w_up)

    cot_own = lax.all_gather(block_cotangent, "gy", axis=1, tiled=True)
    cot_both = jnp.concatenate([cot_own, swap_core(cot_own)], axis=0)
    down_raw = dot(cot_both, down_w, out=BF)

    iota = jnp.arange(128, dtype=jnp.int32)
    routes_both = jnp.concatenate([routes, swap_core(routes)], axis=0)
    member = jnp.any(routes_both[:, :, None] == iota[None, None, :], axis=1)

    xf = token_full.astype(F32)
    scale_one = lax.rsqrt(jnp.mean(xf * xf, axis=1, keepdims=True) + epsilon)
    normed_one = (xf * scale_one * gain_one).astype(BF)
    qkv_raw = dot(normed_one, qkv_w)
    cosine, sine_tab = rope_tables(length)
    query_rows = rotate(qkv_raw[:, :query_cols].reshape(length, heads_here, HD), cosine, sine_tab).astype(BF)
    key_rows = rotate(
        qkv_raw[:, query_cols : query_cols + pair_cols].reshape(length, groups_here, HD), cosine, sine_tab
    ).astype(BF)
    value_rows = qkv_raw[:, query_cols + pair_cols :].reshape(length, groups_here, HD).astype(BF)
    query_group = query_rows.reshape(length, groups_here, share_heads, HD)
    mixed, log_total = attend(query_group, key_rows, value_rows, score_scale, block_rows)
    mixed = mixed.astype(BF)
    attn_partial = dot(mixed, out_w, ((1,), (1,)), BF)
    attn_slice = lax.psum_scatter(attn_partial, "gy", scatter_dimension=1, tiled=True)
    token_slice = tokens.astype(F32)
    residual = token_slice + attn_slice.astype(F32)
    residual_own = lax.all_gather(residual.astype(BF), "gy", axis=1, tiled=True)
    residual_both = jnp.concatenate([residual_own, swap_core(residual_own)], axis=0)

    rf = residual_both.astype(F32)
    scale_two = lax.rsqrt(jnp.mean(rf * rf, axis=1, keepdims=True) + epsilon)
    normed_two = (rf * scale_two * gain_two).astype(BF)
    logits = jnp.where(member, dot(normed_two, router_w), masked)
    gate_exp = jnp.exp(logits - jnp.max(logits, axis=1, keepdims=True))
    gate_all = gate_exp / jnp.sum(gate_exp, axis=1, keepdims=True)
    gate_mine = pad_lanes(lax.dynamic_slice_in_dim(gate_all, core * mine_n, mine_n, 1))
    grad_gate, grad_up, gated, dsum = expert_forward(normed_two, gate_w, up_w, down_raw, gate_mine)

    dsum_own, dsum_got = dsum[:length, :mine_n], swap_core(dsum[length:, :mine_n])
    dsum_pair = jnp.concatenate(core_order(dsum_own, dsum_got), axis=1).T
    dsum_all = jnp.sum(lax.all_gather(dsum_pair, "gy", axis=0), axis=0).T
    gate_own = gate_all[:length, :experts_n]
    grad_picked = gate_own * (dsum_all - jnp.sum(gate_own * dsum_all, axis=1, keepdims=True))
    grad_logits = grad_picked.astype(BF)

    def back_half(rows):
        return (
            dot(grad_gate[rows], gate_w, ((1,), (1,))) + dot(grad_up[rows], up_w, ((1,), (1,)))
        ).astype(BF)

    back_other = swap_core(back_half(slice(length, 2 * length)))
    back_own = back_half(slice(0, length))
    back_sum = (back_own.astype(F32) + back_other.astype(F32)).astype(BF)
    router_slice = lax.dynamic_slice_in_dim(router_w[:, :experts_n], plane * slice_cols, slice_cols, 0)
    grad_normed_two = lax.psum_scatter(back_sum, "gy", scatter_dimension=1, tiled=True).astype(F32) + dot(
        grad_logits, router_slice, ((1,), (1,))
    )
    grad_h2_full = lax.all_gather(grad_normed_two.astype(BF), "gy", axis=1, tiled=True)

    def column_term(left, right):
        half = right.shape[1] // 2

        def term(first_row, rows, side):
            return dot(
                lax.dynamic_slice_in_dim(left, first_row, rows, 1),
                right[:, side * half : (side + 1) * half],
                ((0,), (0,)),
                BF,
            )

        return term

    def expert_grad(left, right):
        total = reduce_chips(column_term(left, right), chip_rows, span // 2)
        keep = jnp.where(core == 0, total[:rows_here], total[rows_here:])
        give = jnp.where(core == 0, total[rows_here:], total[:rows_here])
        both = jnp.concatenate(core_order(keep, swap_core(give)), axis=1)
        return both.reshape(rows_here, experts_n, hidden_here).astype(F32)

    down_grad = expert_grad(cot_both, gated)
    gate_grad = expert_grad(normed_two, grad_gate)
    up_grad = expert_grad(normed_two, grad_up)
    router_grad = lax.psum_scatter(
        dot(normed_two[:length], grad_logits, ((0,), (0,)), BF), "gx", scatter_dimension=0, tiled=True
    ).astype(F32)

    moe_other = swap_core(dot(gated[length:], down_w, ((1,), (1,)), BF))
    moe_own = (dot(gated[:length], down_w, ((1,), (1,))) + moe_other.astype(F32)).astype(BF)
    moe_slice = lax.psum_scatter(moe_own, "gy", scatter_dimension=1, tiled=True)
    block_out = (residual + moe_slice.astype(F32)).astype(BF)

    scale_own = scale_two[:length]
    grad_h2_f = grad_h2_full.astype(F32)
    inner = jnp.sum(grad_h2_f * gain_two * rf[:length], axis=1, keepdims=True)
    grad_res_full = (
        cot_own.astype(F32)
        + scale_own * grad_h2_f * gain_two
        - rf[:length] * scale_own * scale_own * scale_own * inner / D
    ).astype(BF)
    gain_two_slice = second_gain.astype(BF).astype(F32)
    grad_residual = (
        block_cotangent.astype(F32)
        + scale_own * grad_normed_two * gain_two_slice
        - residual * scale_own * scale_own * scale_own * inner / D
    )
    second_gain_grad = jnp.sum(grad_normed_two * residual * scale_own, axis=0)

    grad_mixed = dot(grad_res_full, out_w, out=BF)
    grad_query, grad_keys, grad_values = attend_back(
        query_group,
        key_rows,
        value_rows,
        grad_mixed.reshape(length, groups_here, share_heads, HD),
        log_total,
        score_scale,
        block_rows,
    )
    grad_q_raw = (
        rotate(grad_query.reshape(length, heads_here, HD), cosine, -sine_tab).astype(BF).reshape(length, -1)
    )
    grad_k_raw = rotate(grad_keys, cosine, -sine_tab).astype(BF).reshape(length, -1)
    grad_v_raw = grad_values.astype(BF).reshape(length, -1)
    grad_qkv = jnp.concatenate([grad_q_raw, grad_k_raw, grad_v_raw], axis=1)

    grad_normed_one = lax.psum_scatter(
        dot(grad_qkv, qkv_w, ((1,), (1,)), BF), "gy", scatter_dimension=1, tiled=True
    ).astype(F32)

    out_sum = lax.psum_scatter(
        dot(grad_res_full, mixed, ((0,), (0,)), BF), "gx", scatter_dimension=0, tiled=True
    ).astype(F32)
    qkv_sum = lax.psum_scatter(
        dot(normed_one, grad_qkv, ((0,), (0,)), BF), "gx", scatter_dimension=0, tiled=True
    ).astype(F32)
    query_grad = qkv_sum[:, :query_cols]
    key_grad = qkv_sum[:, query_cols : query_cols + pair_cols]
    value_grad = qkv_sum[:, query_cols + pair_cols :]

    gain_one_slice = first_gain.astype(BF).astype(F32)
    scaled = grad_normed_one * gain_one_slice
    inner_one = lax.psum(jnp.sum(scaled * token_slice, axis=1), "gy")[:, None]
    input_grad = (
        grad_residual
        + scale_one * scaled
        - token_slice * scale_one * scale_one * scale_one * inner_one / D
    ).astype(BF)
    first_gain_grad = jnp.sum(grad_normed_one * token_slice * scale_one, axis=0)
    first_gain_grad, second_gain_grad = lax.psum((first_gain_grad, second_gain_grad), "gx")
    return (
        block_out,
        input_grad,
        first_gain_grad,
        query_grad,
        key_grad,
        value_grad,
        out_sum,
        second_gain_grad,
        router_grad,
        gate_grad,
        up_grad,
        down_grad,
    )


def solution(mesh):
    placed = (
        P("gx", "gy"),
        P("gy"),
        P("gx", "gy"),
        P("gx", "gy"),
        P("gx", "gy"),
        P("gx", "gy"),
        P("gy"),
        P("gx", None),
        P("gx", None, "gy"),
        P("gx", None, "gy"),
        P("gx", None, "gy"),
        P("gx", None),
        P("gx", "gy"),
    )
    return jax.shard_map(
        shards,
        mesh=mesh,
        in_specs=placed,
        out_specs=(
            P("gx", "gy"),
            P("gx", "gy"),
            P("gy"),
            P("gx", "gy"),
            P("gx", "gy"),
            P("gx", "gy"),
            P("gx", "gy"),
            P("gy"),
            P("gx", None),
            P("gx", None, "gy"),
            P("gx", None, "gy"),
            P("gx", None, "gy"),
        ),
        check_vma=False,
    )
```

time: 1980 us -> 1040 us (0.53)
  waiting for transfers between devices: 721 us -> 264 us
  local copies, waits for them, and re-layouts: 407 us -> 162 us
  other arithmetic: 357 us -> 115 us
  blocking collectives: 108 us -> 49.1 us
  Pallas kernels: 0 us -> 52.7 us
  starting transfers between devices: 0.7 us -> 46.5 us
  matrix products: 362 us -> 320 us
    reduce_scatter x7 -> x2, waiting for transfers between devices: 275 us -> 0.01 us  [the longest x1 0.01 us: shards(): lax.psum_scatter(dot(normed_one, grad_qkv, ((0,), (0,)), BF), 'gx', scatt...]
    all_gather x9 -> x4, waiting for transfers between devices: 273 us -> 33.5 us  [the longest x1 19.1 us: shards(): lax.all_gather(jnp.concatenate([tokens, gains], axis=0), 'gy', axis=1, ti...]
    ppermute x0 -> x47, waiting for transfers between devices: none -> 223 us  [the longest x17 154 us: swap_x(): return lax.ppermute(x, 'gx', flip(2, lax.axis_size('gx')))]
    scatter-add x2 -> x0, other arithmetic: 205 us -> none  [the longest x1 103 us: expert_cols(): token_cols = jnp.zeros((length + 1, row_count), jnp.float32).at[owner_fla...]
    gather x5 -> x0, local copies, waits for them, and re-layouts: 176 us -> none  [the longest x3 65.5 us: shards(): grad_gates = row_total(grad_share[routes, slot_rank])]
    unnamed x18 -> x16, waiting for transfers between devices: 173 us -> 6.65 us
    unnamed x142 -> x236, local copies, waits for them, and re-layouts: 141 us -> 48.3 us
    psum x5 -> x1, blocking collectives: 64.5 us -> 10.5 us  [shards(): inner_one = lax.psum(jnp.sum(scaled * token_slice, axis=1), 'gy')[:, None]]
  transfers between devices with their start and end apart: 17 -> 58, of which waited for: 10 -> 21; matrix products, arithmetic and copies ran while one was open for 36% -> 46% of each run, Pallas kernels for 0% -> 0%
where the time goes in v1:
time: 1040 us; the launch traced here: 1030 us
  matrix products  320 us (31%)
  waiting for transfers between devices  264 us (25%)
  local copies, waits for them, and re-layouts  162 us (16%)
  other arithmetic  115 us (11%)
  Pallas kernels  52.7 us (5%)
  blocking collectives  49.1 us (5%)
  starting transfers between devices  46.5 us (4%)
  between operations  15.8 us (2%)
    dot_general x40, matrix products, dot(): lax.dot_general(a, b, (dims, ((), ())), preferred_element_type=F32)  250 us
    ppermute x17, waiting for transfers between devices, swap_x(): return lax.ppermute(x, 'gx', flip(2, lax.axis_size('gx')))  154 us
    ppermute x17, waiting for transfers between devices, swap_y(): return lax.ppermute(x, 'gx', flip(4, lax.axis_size('gx')))  67.5 us
    pallas_call x1, Pallas kernels, expert_forward(): pl.pallas_call(expert_body, grid=(tokens // rows, steps), in_specs=[pl.Bl...  52.7 us
    unnamed x236, local copies, waits for them, and re-layouts  48.3 us
    dynamic_update_slice x4, local copies, waits for them, and re-layouts, attend(): mixed, log_total = lax.map(one_block, jnp.arange(length // block_rows))  31.5 us
    all_gather x1, blocking collectives, shards(): dsum_all = jnp.sum(lax.all_gather(dsum_pair, 'gy', axis=0), axis=0).T  26.2 us
    ppermute x17, starting transfers between devices, swap_y(): return lax.ppermute(x, 'gx', flip(4, lax.axis_size('gx')))  23.5 us
  transfers between devices with their start and end apart: 58, of which 21 were waited for; matrix products, arithmetic and copies ran while one was open for 46% of the time, Pallas kernels for 0%

profile of v1, /device:TPU:0, one launch (start us, length us, event | category | flops | bytes accessed | tf_op | source)
XLA Modules:
  0.0 1031.3 jit_solution(10109541234020578611)
XLA Ops:
  23.2 18.8 %collective-permute-done.2 = bf16[384,1152]{1,0:T(8,128)(2,1)} collective-permute-done((bf16[384,1152]{1,0:T(8,128)(2,1)}, bf16[384,1152]{1,0:T(8,128)(2,1)}, u32[]{:S(2)}, u32[]{:S(2)}) %collective-permute-start.2) | collective-permute-done | bytes 884768 | tf_op jit(solution)/shard_map/ppermute | solution.py:39
  58.6 19.1 %all-gather.6.cloned.1.call-done = bf16[1040,1536]{1,0:T(8,128)(2,1)} async-done(((bf16[1040,384]{1,0:T(8,128)(2,1)}), bf16[1040,1536]{1,0:T(8,128)(2,1)}) %all-gather.6.cloned.1.call-update) | async-done | bytes 3194896 | tf_op jit(solution)/shard_map/all_gather | solution.py:259
  87.4 26.7 %while.27 = (s32[]{:T(128)}, bf16[2,512,2,3,64]{1,4,3,2,0:T(8,128)(2,1)S(1)}, f32[2,2,3,512]{3,2,1,0:T(4,128)}, s32[2]{0:T(128)S(1)}, bf16[1024,2,3,64]{0,3,2,1:...) while((s32[]{:T(128)}, ...), condition=%wide.region_4.5_spmd, body=%wide.region_1.4_spmd.sunk | while | flops 852489728 | bytes 39571644 | solution.py:130
  198.0 20.3 %collective-permute-done.7 = bf16[384,2560]{1,0:T(8,128)(2,1)S(1)} collective-permute-done((bf16[384,2560]{1,0:T(8,128)(2,1)}, bf16[384,2560]{1,0:T(8,128)(2,1)S(1)}, u32[]{:S(2)}, u32[]{:S(2)}) %collective-permute-start.7) | collective-permute-done | bytes 1966112 | tf_op jit(solution)/shard_map/ppermute | solution.py:35
  235.1 14.3 %all-gather.10.cloned.1.call-done = bf16[1024,1536]{1,0:T(8,128)(2,1)} async-done(((bf16[1024,384]{1,0:T(8,128)(2,1)}), bf16[1024,1536]{1,0:T(8,128)(2,1)}) %all-gather.10.cloned.1.call-update) | async-done | bytes 3145744 | tf_op jit(solution)/shard_map/all_gather | solution.py:292
  272.0 30.7 %collective-permute-done.18 = bf16[384,2560]{1,0:T(8,128)(2,1)} collective-permute-done((bf16[384,2560]{1,0:T(8,128)(2,1)}, bf16[384,2560]{1,0:T(8,128)(2,1)}, u32[]{:S(2)}, u32[]{:S(2)}) %collective-permute-start.18) | collective-permute-done | bytes 1966112 | tf_op jit(solution)/shard_map/ppermute | solution.py:35
  311.1 12.5 %collective-permute-done.10 = bf16[384,1280]{1,0:T(8,128)(2,1)S(1)} collective-permute-done((bf16[384,1280]{1,0:T(8,128)(2,1)S(1)}, bf16[384,1280]{1,0:T(8,128)(2,1)S(1)}, u32[]{:S(2)}, u32[]{:S(2)}) %collective-permute-start.10) | collective-permute-done | bytes 983072 | tf_op jit(solution)/shard_map/ppermute | solution.py:35
  331.0 13.7 %collective-permute-done.15 = bf16[384,1280]{1,0:T(8,128)(2,1)S(1)} collective-permute-done((bf16[384,1280]{1,0:T(8,128)(2,1)S(1)}, bf16[384,1280]{1,0:T(8,128)(2,1)S(1)}, u32[]{:S(2)}, u32[]{:S(2)}) %collective-permute-start.15) | collective-permute-done | bytes 983072 | tf_op jit(solution)/shard_map/ppermute | solution.py:35
  347.6 17.7 %collective-permute-done.21 = bf16[384,1280]{1,0:T(8,128)(2,1)S(1)} collective-permute-done((bf16[384,1280]{1,0:T(8,128)(2,1)S(1)}, bf16[384,1280]{1,0:T(8,128)(2,1)S(1)}, u32[]{:S(2)}, u32[]{:S(2)}) %collective-permute-start.21) | collective-permute-done | bytes 983072 | tf_op jit(solution)/shard_map/ppermute | solution.py:35
  373.7 22.6 %convolution_convert_fusion.draw_ref = bf16[2048,2560]{1,0:T(8,128)(2,1)} fusion(bf16[2048,1536]{1,0:T(8,128)(2,1)} %constant_dynamic-update-slice_fusion, bf16[1536,2560]{1,0:T(8,128)(2,1)} %maximum_dynamic-update-slice_fusion.2), kind=kOutput, calls=%fused_computation.53 | convolution fusion | flops 16111370240 | bytes 24641536 | tf_op jit(solution)/shard_map/dot_general | solution.py:23
  414.3 52.7 %shard_map.238 = (bf16[2048,2560]{1,0:T(8,128)(2,1)}, bf16[2048,2560]{1,0:T(8,128)(2,1)}, bf16[2048,2560]{1,0:T(8,128)(2,1)}, f32[2048,128]{1,0:T(8,128)}) custom-call(bf16[2048,1536]{1,0:T(8,128)(2,1)} %copy-done.33, bf16[1536,2560]{1,0:T(8,128)(2,1)} %maximum_dynamic-update-slice_fusion.wg_ref, ...), custom_call_target="tpu_custom_call" | custom-call | flops 32212254720 | bytes 73400320 | tf_op jit(solution)/shard_map/pallas_call | solution.py:208
  467.0 12.2 %fusion.51 = f32[1024,1536]{1,0:T(8,128)S(1)} fusion(bf16[1536,2560]{1,0:T(8,128)(2,1)} %maximum_dynamic-update-slice_fusion.1.wu_ref, bf16[2048,2560]{1,0:T(8,128)(2,1)} %get-tuple-element.111), kind=kOutput, calls=%fused_computation.74 | convolution fusion | flops 8053063680 | bytes 19398656 | tf_op jit(solution)/shard_map/dot_general | solution.py:23
  479.3 12.3 %add_convert_fusion.1 = bf16[1024,1536]{1,0:T(8,128)(2,1)S(1)} fusion(f32[1024,1536]{1,0:T(8,128)S(1)} %fusion.51, bf16[1536,2560]{1,0:T(8,128)(2,1)} %maximum_dynamic-update-slice_fusion.wg_ref, bf16[2048,2560]{1,0:T(8,128)(2,1)} %get-tuple-element.110), kind=kOutput, calls=%fused_computation.71 | convolution fusion | flops 8056209408 | bytes 22544384 | tf_op jit(solution)/shard_map/dot_general | solution.py:23
  492.2 12.2 %fusion.55 = f32[1024,1536]{1,0:T(8,128)S(1)} fusion(bf16[1536,2560]{1,0:T(8,128)(2,1)} %maximum_dynamic-update-slice_fusion.1.wu_ref, bf16[2048,2560]{1,0:T(8,128)(2,1)} %get-tuple-element.111), kind=kOutput, calls=%fused_computation.78 | convolution fusion | flops 8053063680 | bytes 19398656 | tf_op jit(solution)/shard_map/dot_general | solution.py:23
  510.6 12.5 %add_convert_fusion.2 = bf16[1024,1536]{1,0:T(8,128)(2,1)S(1)} fusion(f32[1024,1536]{1,0:T(8,128)S(1)} %fusion.55, bf16[1536,2560]{1,0:T(8,128)(2,1)} %maximum_dynamic-update-slice_fusion.wg_ref, bf16[2048,2560]{1,0:T(8,128)(2,1)} %get-tuple-element.110), kind=kOutput, calls=%fused_computation.72 | convolution fusion | flops 8056209408 | bytes 22544384 | tf_op jit(solution)/shard_map/dot_general | solution.py:23
  568.4 26.2 %all-gather = f32[160,1024]{1,0:T(8,128)S(1)} all-gather(f32[40,1024]{1,0:T(8,128)S(1)} %maximum_bitcast_fusion), channel_id=2, replica_groups=mesh['gx'=8,'gy'=4] {'gy'}, dimensions={0}, use_global_device_ids=true | all-gather | bytes 819200 | tf_op jit(solution)/shard_map/all_gather | solution.py:331
  634.6 12.7 %add_convert_fusion.3 = bf16[1024,1536]{1,0:T(8,128)(2,1)S(1)} fusion(bf16[1024,1536]{1,0:T(8,128)(2,1)} %collective-permute-done.23, bf16[1536,2560]{1,0:T(8,128)(2,1)} %maximum_dynamic-update-slice_fusion.2, bf16[2048,2560]{1,0:T(8,128)(2,1)} %get-tuple-element.109), kind=kOutput, calls=%fused_computation.73 | convolution fusion | flops 8057782272 | bytes 19398656 | tf_op jit(solution)/shard_map/dot_general | solution.py:23
  691.3 27.7 %collective-permute-done.44 = bf16[384,1280]{1,0:T(8,128)(2,1)S(1)} collective-permute-done((bf16[384,1280]{1,0:T(8,128)(2,1)S(1)}, bf16[384,1280]{1,0:T(8,128)(2,1)S(1)}, u32[]{:S(2)}, u32[]{:S(2)}) %collective-permute-start.44) | collective-permute-done | bytes 983072 | tf_op jit(solution)/shard_map/ppermute | solution.py:39
  743.1 105.4 %while.28 = (s32[]{:T(128)}, f32[1024,2,64]{0,2,1:T(8,128)S(1)}, f32[1024,2,64]{0,2,1:T(8,128)}, f32[2,512,2,3,64]{1,0,4,3,2:T(2,128)}, s32[2]{0:T(128)S(1)}, /*...) while((s32[]{:T(128)}, f32[1024,2,64]{0,2,1:T(8,128)S(1)}, ...), condition=%wide.region_17.18_spmd.clone, body=%wide.region_15.17_spmd.clone.sunk | while | flops 2045572608 | bytes 209785296 | solution.py:169
  781.0 14.9 %dynamic_update_slice.99 = f32[2,512,2,3,64]{1,0,4,3,2:T(2,128)} dynamic-update-slice(f32[2,512,2,3,64]{1,0,4,3,2:T(2,128)} %get-tuple-element.410, f32[1,512,2,3,64]{1,0,4,3,2:T(1,128)S(1)} %copy.129, s32[]{:T(128)S(6)} %copy.167, s32[]{:T(128)} %constant.115.clone.1..sunk.1, s32[]{:T(128)} %constant.115.clone.1..sunk.1, s32[]{:T(128)} %constant.115.clone.1..sunk.1, s32[]{:T(128)} %constant.115.clone.1..sunk.1) | dynamic-update-slice | bytes 1572868 | tf_op jit(solution)/shard_map/while/body/jit(dynamic_update_index_in_dim)/dynamic_update_slice | solution.py:130
  833.5 14.9 %dynamic_update_slice.99 = f32[2,512,2,3,64]{1,0,4,3,2:T(2,128)} dynamic-update-slice(f32[2,512,2,3,64]{1,0,4,3,2:T(2,128)} %get-tuple-element.410, f32[1,512,2,3,64]{1,0,4,3,2:T(1,128)S(1)} %copy.129, s32[]{:T(128)S(6)} %copy.167, s32[]{:T(128)} %constant.115.clone.1..sunk.1, s32[]{:T(128)} %constant.115.clone.1..sunk.1, s32[]{:T(128)} %constant.115.clone.1..sunk.1, s32[]{:T(128)} %constant.115.clone.1..sunk.1) | dynamic-update-slice | bytes 1572868 | tf_op jit(solution)/shard_map/while/body/jit(dynamic_update_index_in_dim)/dynamic_update_slice | solution.py:130
  893.3 27.7 %collective-permute-done.38 = bf16[384,1280]{1,0:T(8,128)(2,1)S(1)} collective-permute-done((bf16[384,1280]{1,0:T(8,128)(2,1)S(1)}, bf16[384,1280]{1,0:T(8,128)(2,1)S(1)}, u32[]{:S(2)}, u32[]{:S(2)}) %collective-permute-start.38) | collective-permute-done | bytes 983072 | tf_op jit(solution)/shard_map/ppermute | solution.py:35
  943.2 16.6 %collective-permute-done.45 = bf16[384,1280]{1,0:T(8,128)(2,1)} collective-permute-done((bf16[384,1280]{1,0:T(8,128)(2,1)}, bf16[384,1280]{1,0:T(8,128)(2,1)}, u32[]{:S(2)}, u32[]{:S(2)}) %collective-permute-start.45) | collective-permute-done | bytes 983072 | tf_op jit(solution)/shard_map/ppermute | solution.py:35
  1008.4 12.4 %all-reduce.3 = (f32[384]{0:T(512)}, f32[384]{0:T(512)}) all-reduce(f32[384]{0:T(512)S(1)} %get-tuple-element.150, f32[384]{0:T(512)S(1)} %get-tuple-element.152), channel_id=1, replica_groups=mesh['gx'=8,'gy'=4] {'gx'}, use_global_device_ids=true, to_apply=%region_22.23 | all-reduce | flops 768 | bytes 6144 | tf_op jit(solution)/shard_map/psum | solution.py:438
  (586 shorter events, 583.4 us)
Async XLA Ops:
  7.2 70.5 %all-gather.6.cloned.1.call-start = ((), (), s32[]{:S(2)}) async-start(), calls=%async_computation.7 | async-start | bytes 3993600 | tf_op jit(solution)/shard_map/all_gather | solution.py:259
  10.7 177.2 %reduce-scatter.22.cloned.1.call-start = ((), (), s32[]{:S(2)}) async-start(), calls=%async_computation.13 | async-start | bytes 3932160
  125.4 124.0 %all-gather.10.cloned.1.call-start = ((), (), s32[]{:S(2)}) async-start(), calls=%async_computation.9 | async-start | bytes 3932160 | tf_op jit(solution)/shard_map/all_gather | solution.py:292
  163.1 206.8 %all-gather.8.cloned.1.call-start = ((), (), s32[]{:S(2)}) async-start(), calls=%async_computation.8 | async-start | bytes 3932160 | tf_op jit(solution)/shard_map/all_gather | solution.py:317
  182.9 77.6 %collective-permute-start.12 = (bf16[384,2560]{1,0:T(8,128)(2,1)}, bf16[384,2560]{1,0:T(8,128)(2,1)}, u32[]{:S(2)}, u32[]{:S(2)}) collective-permute-start(bf16[384,2560]{1,0:T(8,128)(2,1)} %get-tuple-element.211), channel_id=1, source_target_pairs={{0,8},{4,12},{8,0},{12,4},{16,24},{20,28},{24,16},{28,20},{1,9},{5... | collective-permute-start | bytes 5898248 | tf_op jit(solution)/shard_map/ppermute | solution.py:35
  183.5 78.5 %collective-permute-start.13 = (bf16[384,2560]{1,0:T(8,128)(2,1)}, bf16[384,2560]{1,0:T(8,128)(2,1)}, u32[]{:S(2)}, u32[]{:S(2)}) collective-permute-start(bf16[384,2560]{1,0:T(8,128)(2,1)} %get-tuple-element.211), channel_id=1, source_target_pairs={{0,16},{4,20},{8,24},{12,28},{16,0},{20,4},{24,8},{28,12},{1,17},{... | collective-permute-start | bytes 5898248 | tf_op jit(solution)/shard_map/ppermute | solution.py:39
  190.5 408.3 %reduce-scatter.26.cloned.1.call-start = ((), (), s32[]{:S(2)}) async-start(), calls=%async_computation.15 | async-start | bytes 3932160
  196.8 105.9 %collective-permute-start.18 = (bf16[384,2560]{1,0:T(8,128)(2,1)}, bf16[384,2560]{1,0:T(8,128)(2,1)}, u32[]{:S(2)}, u32[]{:S(2)}) collective-permute-start(bf16[384,2560]{1,0:T(8,128)(2,1)} %get-tuple-element.219), channel_id=1, source_target_pairs={{0,8},{4,12},{8,0},{12,4},{16,24},{20,28},{24,16},{28,20},{1,9},{5... | collective-permute-start | bytes 5898248 | tf_op jit(solution)/shard_map/ppermute | solution.py:35
  218.3 85.8 %collective-permute-start.19 = (bf16[384,2560]{1,0:T(8,128)(2,1)}, bf16[384,2560]{1,0:T(8,128)(2,1)}, u32[]{:S(2)}, u32[]{:S(2)}) collective-permute-start(bf16[384,2560]{1,0:T(8,128)(2,1)} %get-tuple-element.219), channel_id=1, source_target_pairs={{0,16},{4,20},{8,24},{12,28},{16,0},{20,4},{24,8},{28,12},{1,17},{... | collective-permute-start | bytes 5898248 | tf_op jit(solution)/shard_map/ppermute | solution.py:39
  249.4 120.5 %collective-permute-start.16 = (bf16[1024,1536]{1,0:T(8,128)(2,1)}, bf16[1024,1536]{1,0:T(8,128)(2,1)}, u32[]{:S(2)}, u32[]{:S(2)}) collective-permute-start(bf16[1024,1536]{1,0:T(8,128)(2,1)} %all-gather.10.cloned.1.call-done), channel_id=1, source_target_pairs={{0,4},{4,0},{8,12},{12,8},{16,20},{20,16},{24,28},{28,24},{1,5},{5... | collective-permute-start | bytes 9437192 | tf_op jit(solution)/shard_map/ppermute | solution.py:31
  526.9 129.8 %reduce-scatter.30.cloned.1.call-start = ((), (), s32[]{:S(2)}) async-start(), calls=%async_computation.17 | async-start | bytes 442368
  598.8 125.4 %all-gather.12.cloned.1.call-start = ((), (), s32[]{:S(2)}) async-start(), calls=%async_computation.10 | async-start | bytes 3932160 | tf_op jit(solution)/shard_map/all_gather | solution.py:348
  603.1 376.8 %reduce-scatter.24.cloned.1.call-start = ((), (), s32[]{:S(2)}) async-start(), calls=%async_computation.14 | async-start | bytes 3932160
  611.5 255.6 %collective-permute-start.29 = (bf16[384,1280]{1,0:T(8,128)(2,1)}, bf16[384,1280]{1,0:T(8,128)(2,1)}, u32[]{:S(2)}, u32[]{:S(2)}) collective-permute-start(bf16[384,1280]{1,0:T(8,128)(2,1)} %fusion.161), channel_id=1, source_target_pairs={{0,16},{4,20},{8,24},{12,28},{16,0},{20,4},{24,8},{28,12},{1,17},{... | collective-permute-start | bytes 2949128 | tf_op jit(solution)/shard_map/ppermute | solution.py:39
  612.7 262.7 %collective-permute-start.26 = (bf16[384,1280]{1,0:T(8,128)(2,1)}, bf16[384,1280]{1,0:T(8,128)(2,1)}, u32[]{:S(2)}, u32[]{:S(2)}) collective-permute-start(bf16[384,1280]{1,0:T(8,128)(2,1)} %fusion.137), channel_id=1, source_target_pairs={{0,8},{4,12},{8,0},{12,4},{16,24},{20,28},{24,16},{28,20},{1,9},{5... | collective-permute-start | bytes 2949128 | tf_op jit(solution)/shard_map/ppermute | solution.py:35
  650.3 332.1 %reduce-scatter.20.cloned.1.call-start = ((), (), s32[]{:S(2)}) async-start(), calls=%async_computation.12 | async-start | bytes 1327104 | tf_op jit(solution)/shard_map/reduce_scatter | solution.py:419
  658.3 232.7 %collective-permute-start.36 = (bf16[384,1280]{1,0:T(8,128)(2,1)}, bf16[384,1280]{1,0:T(8,128)(2,1)}, u32[]{:S(2)}, u32[]{:S(2)}) collective-permute-start(bf16[384,1280]{1,0:T(8,128)(2,1)} %fusion.209), channel_id=1, source_target_pairs={{0,16},{4,20},{8,24},{12,28},{16,0},{20,4},{24,8},{28,12},{1,17},{... | collective-permute-start | bytes 2949128 | tf_op jit(solution)/shard_map/ppermute | solution.py:39
  687.6 171.4 %collective-permute-start.41 = (bf16[384,1280]{1,0:T(8,128)(2,1)}, bf16[384,1280]{1,0:T(8,128)(2,1)}, u32[]{:S(2)}, u32[]{:S(2)}) collective-permute-start(bf16[384,1280]{1,0:T(8,128)(2,1)} %fusion.239), channel_id=1, source_target_pairs={{0,8},{4,12},{8,0},{12,4},{16,24},{20,28},{24,16},{28,20},{1,9},{5... | collective-permute-start | bytes 2949128 | tf_op jit(solution)/shard_map/ppermute | solution.py:35
  719.0 149.6 %collective-permute-start.31 = (bf16[384,1280]{1,0:T(8,128)(2,1)}, bf16[384,1280]{1,0:T(8,128)(2,1)}, u32[]{:S(2)}, u32[]{:S(2)}) collective-permute-start(bf16[384,1280]{1,0:T(8,128)(2,1)} %fusion.278), channel_id=1, source_target_pairs={{0,8},{4,12},{8,0},{12,4},{16,24},{20,28},{24,16},{28,20},{1,9},{5... | collective-permute-start | bytes 2949128 | tf_op jit(solution)/shard_map/ppermute | solution.py:35
  742.9 241.1 %reduce-scatter.18.cloned.1.call-start = ((), (), s32[]{:S(2)}) async-start(), calls=%async_computation.11 | async-start | bytes 2211840 | tf_op jit(solution)/shard_map/reduce_scatter | solution.py:422
  858.9 134.7 %reduce-scatter.28.cloned.1.call-start = ((), (), s32[]{:S(2)}) async-start(), calls=%async_computation.16 | async-start | bytes 3932160
  867.1 68.1 %collective-permute-start.33 = (bf16[384,1280]{1,0:T(8,128)(2,1)}, bf16[384,1280]{1,0:T(8,128)(2,1)}, u32[]{:S(2)}, u32[]{:S(2)}) collective-permute-start(bf16[384,1280]{1,0:T(8,128)(2,1)} %fusion.185), channel_id=1, source_target_pairs={{0,8},{4,12},{8,0},{12,4},{16,24},{20,28},{24,16},{28,20},{1,9},{5... | collective-permute-start | bytes 2949128 | tf_op jit(solution)/shard_map/ppermute | solution.py:35
  875.4 67.6 %collective-permute-start.43 = (bf16[384,1280]{1,0:T(8,128)(2,1)}, bf16[384,1280]{1,0:T(8,128)(2,1)}, u32[]{:S(2)}, u32[]{:S(2)}) collective-permute-start(bf16[384,1280]{1,0:T(8,128)(2,1)} %fusion.257), channel_id=1, source_target_pairs={{0,16},{4,20},{8,24},{12,28},{16,0},{20,4},{24,8},{28,12},{1,17},{... | collective-permute-start | bytes 2949128 | tf_op jit(solution)/shard_map/ppermute | solution.py:39
  886.0 79.2 %collective-permute-start.40 = (bf16[384,1280]{1,0:T(8,128)(2,1)}, bf16[384,1280]{1,0:T(8,128)(2,1)}, u32[]{:S(2)}, u32[]{:S(2)}) collective-permute-start(bf16[384,1280]{1,0:T(8,128)(2,1)} %fusion.233), channel_id=1, source_target_pairs={{0,8},{4,12},{8,0},{12,4},{16,24},{20,28},{24,16},{28,20},{1,9},{5... | collective-permute-start | bytes 2949128 | tf_op jit(solution)/shard_map/ppermute | solution.py:35
  (156 other events, 2781.4 us)
Sparse Core Ops, SparseCore 0:
  10.8 66.8 all-gather.5
  125.6 58.8 reduce-scatter.21
  186.0 63.3 all-gather.9
  251.4 61.9 all-gather.7
  527.0 67.8 reduce-scatter.25
  598.9 34.2 reduce-scatter.29
  635.4 63.3 all-gather.11
  701.0 58.8 reduce-scatter.23
  763.2 36.8 reduce-scatter.19
  859.0 48.1 reduce-scatter.17
  935.1 58.4 reduce-scatter.27

commit v2 on v1

v2 whole, which is shorter than its diff:
```python
from functools import partial
import math

import jax
import jax.numpy as jnp
import numpy as np
from jax import lax
from jax.experimental import pallas as pl
from jax.experimental.pallas import tpu as pltpu
from jax.sharding import PartitionSpec as P

D = 1536
HD = 64
FFZ = 128
epsilon = 1e-06
BF = jnp.bfloat16
F32 = jnp.float32
masked = -1e30
VM = pl.BlockSpec(memory_space=pltpu.VMEM)
MB = 1024 * 1024

def rope_tables(length):
    frequency = np.exp(np.arange(HD // 2) * (-2.0 * math.log(10000.0) / HD)).astype(np.float32)
    angles = np.arange(length, dtype=np.float32)[:, None] * frequency[None, :]
    cosine, sine_tab = np.cos(angles), np.sin(angles)
    return (
        jnp.asarray(np.concatenate([cosine, cosine], axis=1), F32),
        jnp.asarray(np.concatenate([-sine_tab, sine_tab], axis=1), F32),
    )

def halves_swapped(x):
    return jnp.concatenate([x[:, HD // 2 :], x[:, : HD // 2]], axis=1)

def causal_scores(q, keys, first):
    rows, length = q.shape[0], keys.shape[0]
    scores = lax.dot_general(q, keys, (((1,), (1,)), ((), ())), preferred_element_type=F32)
    row_ids = first + lax.broadcasted_iota(jnp.int32, (rows, length), 0)
    col_ids = lax.broadcasted_iota(jnp.int32, (rows, length), 1)
    return jnp.where(col_ids <= row_ids, scores, masked)

def attend_body(heads, groups, block, qkv_ref, cos_ref, sin_ref, mixed_ref, q_ref, k_ref, v_ref, log_ref, mixed_scr):
    length = qkv_ref.shape[0]
    cosine, sine = cos_ref[...], sin_ref[...]
    for h in range(heads + groups):
        x = qkv_ref[:, h * HD : (h + 1) * HD]
        x = (x * cosine + halves_swapped(x) * sine).astype(BF)
        if h < heads:
            q_ref[h] = x * jnp.asarray(HD**-0.5, BF)
        else:
            k_ref[h - heads] = x
    for g in range(groups):
        at = (heads + groups + g) * HD
        v_ref[g] = qkv_ref[:, at : at + HD].astype(BF)
    log_ref[...] = jnp.zeros_like(log_ref)
    share = heads // groups

    def head(h, carry):
        group = h // share
        for i in range(length // block):
            rows = slice(i * block, (i + 1) * block)
            seen = slice(0, (i + 1) * block)
            scores = causal_scores(q_ref[h, rows], k_ref[group, seen], i * block)
            top = jnp.max(scores, axis=1, keepdims=True)
            expo = jnp.exp(scores - top)
            total = jnp.sum(expo, axis=1, keepdims=True)
            probs = (expo * (1.0 / total)).astype(BF)
            mixed_scr[h, rows] = jnp.dot(probs, v_ref[group, seen], preferred_element_type=F32).astype(BF)
            lanes = lax.broadcasted_iota(jnp.int32, (block, 128), 1)
            log_ref[rows] = jnp.where(lanes == h, top + jnp.log(total), log_ref[rows])
        return carry

    lax.fori_loop(0, heads, head, 0)
    for h in range(0, heads, 2):
        mixed_ref[:, h * HD : (h + 2) * HD] = jnp.concatenate([mixed_scr[h], mixed_scr[h + 1]], axis=1)

def attend(qkv, heads, groups, block=256):
    length = qkv.shape[0]
    cosine, sine = rope_tables(length)
    S = jax.ShapeDtypeStruct
    return pl.pallas_call(
        partial(attend_body, heads, groups, block),
        in_specs=[VM] * 3,
        out_specs=[VM] * 5,
        out_shape=[
            S((length, heads * HD), BF),
            S((heads, length, HD), BF),
            S((groups, length, HD), BF),
            S((groups, length, HD), BF),
            S((length, 128), F32),
        ],
        scratch_shapes=[pltpu.VMEM((heads, length, HD), BF)],
        compiler_params=pltpu.CompilerParams(vmem_limit_bytes=40 * MB),
    )(qkv, cosine, sine)

def attend_back_body(heads, groups, block, q_ref, k_ref, v_ref, log_ref, mixed_ref, do_ref, cos_ref, sin_ref, out_ref, do_scr, mixed_scr, dq_scr, dk_scr, dv_scr):
    length = do_ref.shape[0]
    share = heads // groups
    for h in range(heads):
        do_scr[h] = do_ref[:, h * HD : (h + 1) * HD]
        mixed_scr[h] = mixed_ref[:, h * HD : (h + 1) * HD]
    dk_scr[...] = jnp.zeros_like(dk_scr)
    dv_scr[...] = jnp.zeros_like(dv_scr)

    def head(h, carry):
        group = h // share
        for i in range(length // block):
            rows = slice(i * block, (i + 1) * block)
            seen = slice(0, (i + 1) * block)
            q, keys, values, do = q_ref[h, rows], k_ref[group, seen], v_ref[group, seen], do_scr[h, rows]
            lanes = lax.broadcasted_iota(jnp.int32, (block, 128), 1)
            log_total = jnp.sum(jnp.where(lanes == h, log_ref[rows], 0.0), axis=1, keepdims=True)
            probs = jnp.exp(causal_scores(q, keys, i * block) - log_total)
            grad_probs = lax.dot_general(do, values, (((1,), (1,)), ((), ())), preferred_element_type=F32)
            inner = jnp.sum(do.astype(F32) * mixed_scr[h, rows].astype(F32), axis=1, keepdims=True)
            grad_scores = (probs * (grad_probs - inner)).astype(BF)
            dq_scr[h, rows] = jnp.dot(grad_scores, keys, preferred_element_type=F32) * (HD**-0.5)
            across = (((0,), (0,)), ((), ()))
            dk_scr[group, seen] += lax.dot_general(grad_scores, q, across, preferred_element_type=F32)
            dv_scr[group, seen] += lax.dot_general(probs.astype(BF), do, across, preferred_element_type=F32)
        return carry

    lax.fori_loop(0, heads, head, 0)
    cosine, sine = cos_ref[...], sin_ref[...]

    def back(x):
        return (x * cosine - halves_swapped(x) * sine).astype(BF)

    cols = [back(dq_scr[h]) for h in range(heads)]
    cols += [back(dk_scr[g]) for g in range(groups)]
    cols += [dv_scr[g].astype(BF) for g in range(groups)]
    for p in range(0, len(cols), 2):
        out_ref[:, p * HD : (p + 2) * HD] = jnp.concatenate([cols[p], cols[p + 1]], axis=1)

def attend_back(q, k, v, log_total, mixed, do, block=256):
    heads, length, _ = q.shape
    groups = k.shape[0]
    cosine, sine = rope_tables(length)
    return pl.pallas_call(
        partial(attend_back_body, heads, groups, block),
        in_specs=[VM] * 8,
        out_specs=VM,
        out_shape=jax.ShapeDtypeStruct((length, (heads + 2 * groups) * HD), BF),
        scratch_shapes=[
            pltpu.VMEM((heads, length, HD), BF),
            pltpu.VMEM((heads, length, HD), BF),
            pltpu.VMEM((heads, length, HD), F32),
            pltpu.VMEM((groups, length, HD), F32),
            pltpu.VMEM((groups, length, HD), F32),
        ],
        compiler_params=pltpu.CompilerParams(vmem_limit_bytes=48 * MB),
    )(q, k, v, log_total, mixed, do, cosine, sine)

def expert_math(gate, draw, gg, uu):
    sig = 1.0 / (1.0 + jnp.exp(-gg))
    silu = gg * sig
    act = silu * uu
    back = gate * draw
    return (
        (gate * act).astype(BF),
        (back * uu * (sig + silu * (1.0 - sig))).astype(BF),
        (back * silu).astype(BF),
        jnp.sum(act * draw, axis=1, keepdims=True),
    )

def expert_body(rows, chunk, h_ref, wg_ref, wu_ref, draw_ref, gate_ref, out_ref, dsum_ref):
    step = pl.program_id(1)
    wg, wu = wg_ref[...], wu_ref[...]
    for m in range(rows // chunk):
        at = slice(m * chunk, (m + 1) * chunk)
        h = h_ref[at]
        g = jnp.dot(h, wg, preferred_element_type=F32)
        u = jnp.dot(h, wu, preferred_element_type=F32)
        lanes = lax.broadcasted_iota(jnp.int32, (chunk, 128), 1)
        gates = gate_ref[at]
        sums = jnp.where(step == 0, 0.0, dsum_ref[at])
        for half in range(2):
            cols = slice(half * FFZ, (half + 1) * FFZ)
            hot = lanes == step * 2 + half
            gate = jnp.sum(jnp.where(hot, gates, 0.0), axis=1, keepdims=True)
            ga, dg, du, s = expert_math(gate, draw_ref[at, cols].astype(F32), g[:, cols], u[:, cols])
            out_ref[0, at, cols] = ga
            out_ref[1, at, cols] = dg
            out_ref[2, at, cols] = du
            sums = jnp.where(hot, s, sums)
        dsum_ref[at] = sums

def expert_forward(h, w_all, draw, gate, rows=1024, chunk=256):
    tokens, width = draw.shape
    steps = width // (2 * FFZ)
    return pl.pallas_call(
        partial(expert_body, rows, chunk),
        grid=(tokens // rows, steps),
        in_specs=[
            pl.BlockSpec((rows, D), lambda i, j: (i, 0)),
            pl.BlockSpec((D, 2 * FFZ), lambda i, j: (0, steps + j)),
            pl.BlockSpec((D, 2 * FFZ), lambda i, j: (0, 2 * steps + j)),
            pl.BlockSpec((rows, 2 * FFZ), lambda i, j: (i, j)),
            pl.BlockSpec((rows, 128), lambda i, j: (i, 0)),
        ],
        out_specs=[
            pl.BlockSpec((3, rows, 2 * FFZ), lambda i, j: (0, i, j)),
            pl.BlockSpec((rows, 128), lambda i, j: (i, 0)),
        ],
        out_shape=[
            jax.ShapeDtypeStruct((3, tokens, width), BF),
            jax.ShapeDtypeStruct((tokens, 128), F32),
        ],
        compiler_params=pltpu.CompilerParams(vmem_limit_bytes=56 * MB),
    )(h, w_all, w_all, draw, gate)

def project_body(n, *refs):
    dims = (((1,), (1,)), ((), ()))
    o_ref = refs[2 * n]
    total = None
    for a_ref, w_ref in zip(refs[:n], refs[n : 2 * n]):
        a = a_ref[0] if len(a_ref.shape) == 3 else a_ref[...]
        term = lax.dot_general(a, w_ref[...], dims, preferred_element_type=F32)
        total = term if total is None else total + term
    cols = o_ref.shape[2]
    o_ref[0] = total[:, :cols].astype(BF)
    o_ref[1] = total[:, cols:].astype(BF)

def project(terms, parts):
    rows, width = terms[0][1][-2:]
    cols = D // parts
    n = len(terms)
    total = pl.pallas_call(
        partial(project_body, n),
        grid=(parts // 2,),
        in_specs=[pl.BlockSpec(t[1], partial(lambda at, j: at, t[2])) for t in terms]
        + [pl.BlockSpec((2 * cols, width), partial(lambda at, j: (j, at), t[4])) for t in terms],
        out_specs=pl.BlockSpec((2, rows, cols), lambda j: (j, 0, 0)),
        out_shape=jax.ShapeDtypeStruct((parts, rows, cols), BF),
        compiler_params=pltpu.CompilerParams(vmem_limit_bytes=56 * MB),
    )(*[t[0] for t in terms], *[t[3] for t in terms])
    return total.reshape(parts * rows, cols)

def term_body(steps, ids_ref, c0_ref, c1_ref, h0_ref, h1_ref, g_ref, a_ref, b_ref):
    side, m = pl.program_id(0), pl.program_id(1)
    rows = c0_ref.shape[1]
    across = (((0,), (0,)), ((), ()))

    def work(l0, l1, o_ref):
        g = g_ref[0]
        o_ref[:rows] = lax.dot_general(l0[...], g, across, preferred_element_type=F32).astype(BF)
        o_ref[rows:] = lax.dot_general(l1[...], g, across, preferred_element_type=F32).astype(BF)

    for s, o_ref in ((0, a_ref), (1, b_ref)):
        @pl.when((side == s) & (m == 0))
        def _():
            work(c0_ref, c1_ref, o_ref)

        @pl.when((side == s) & (m > 0))
        def _():
            work(h0_ref, h1_ref, o_ref)

def expert_terms(ids, c, h, grads, rows, cols=1280):
    tokens, width = grads.shape[1:]
    steps = width // 2 // cols
    last = 3 * steps - 1
    piece = lambda p: pl.BlockSpec((tokens, rows), lambda s, m, j, ids: (0, ids[2 * s + p]))
    out = jax.ShapeDtypeStruct((2 * rows, 3 * width // 2), BF)
    return pl.pallas_call(
        partial(term_body, steps),
        grid_spec=pltpu.PrefetchScalarGridSpec(
            num_scalar_prefetch=1,
            grid=(2, 3, steps),
            in_specs=[piece(0), piece(1), piece(0), piece(1),
                pl.BlockSpec((1, tokens, cols), lambda s, m, j, ids: (m, 0, s * steps + j))],
            out_specs=[
                pl.BlockSpec((2 * rows, cols), lambda s, m, j, ids: (0, jnp.where(s == 0, m * steps + j, last))),
                pl.BlockSpec((2 * rows, cols), lambda s, m, j, ids: (0, jnp.where(s == 0, 0, m * steps + j))),
            ],
        ),
        out_shape=[out, out],
        compiler_params=pltpu.CompilerParams(vmem_limit_bytes=56 * MB),
    )(ids, c, c, h, h, grads)

def prepare_body(core_ref, down_ref, gate_ref, up_ref, keep_ref, give_ref):
    first = core_ref[0] == 0
    rows, n2, _ = down_ref.shape
    n = n2 // 2
    for m, ref in enumerate((down_ref, gate_ref, up_ref)):
        flat = ref.reshape(rows * n2, FFZ)
        for e in range(n):
            lo = flat[pl.ds(e, rows, stride=n2), :]
            hi = flat[pl.ds(n + e, rows, stride=n2), :]
            at = (m * n + e) * FFZ
            keep_ref[:, at : at + FFZ] = jnp.where(first, lo, hi).astype(BF)
            give_ref[:, at : at + FFZ] = jnp.where(first, hi, lo).astype(BF)

def prepare(core, down, gate, up):
    rows, n, _ = down.shape
    part = 48
    wide = 3 * n * FFZ // 2
    weight = pl.BlockSpec((part, n, FFZ), lambda i, c: (i, 0, 0))
    out = pl.BlockSpec((part, wide), lambda i, c: (i, 0))
    return pl.pallas_call(
        prepare_body,
        grid_spec=pltpu.PrefetchScalarGridSpec(num_scalar_prefetch=1, grid=(rows // part,), in_specs=[weight] * 3, out_specs=[out] * 2),
        out_shape=[jax.ShapeDtypeStruct((rows, wide), BF)] * 2,
        compiler_params=pltpu.CompilerParams(vmem_limit_bytes=40 * MB),
    )(core, down, gate, up)

def place_body(offs_ref, *refs):
    fulls, lefts, rights, out = refs[:6], refs[6:8], refs[8:10], refs[10]
    rows = fulls[0].shape[0]

    def put(i, ref):
        out[pl.ds(pl.multiple_of(offs_ref[i] * rows, 16), rows), :] = ref[...]

    for i, ref in enumerate(fulls):
        put(i, ref)
    left = pl.program_id(0) < pl.num_programs(0) // 2

    @pl.when(left)
    def _():
        for i, ref in enumerate(lefts):
            put(6 + i, ref)

    @pl.when(jnp.logical_not(left))
    def _():
        for i, ref in enumerate(rights):
            put(6 + i, ref)

def place(offsets, fulls, lefts, rights, steps=10):
    rows, wide = fulls[0].shape
    cols = wide // steps
    half = steps // 2
    return pl.pallas_call(
        place_body,
        grid_spec=pltpu.PrefetchScalarGridSpec(
            num_scalar_prefetch=1,
            grid=(steps,),
            in_specs=[pl.BlockSpec((rows, cols), lambda j, o: (0, j))] * 6
            + [pl.BlockSpec((rows, cols), lambda j, o: (0, jnp.minimum(j, half - 1)))] * 2
            + [pl.BlockSpec((rows, cols), lambda j, o: (0, jnp.maximum(j - half, 0)))] * 2,
            out_specs=pl.BlockSpec((8 * rows, cols), lambda j, o: (0, j)),
        ),
        out_shape=jax.ShapeDtypeStruct((8 * rows, wide), fulls[0].dtype),
        compiler_params=pltpu.CompilerParams(vmem_limit_bytes=40 * MB),
    )(offsets, *fulls, *lefts, *rights)

def finish_body(core_ref, *refs):
    n_own = (len(refs) - 5) // 2
    own_a, own_b = refs[:n_own], refs[n_own : 2 * n_own]
    got_a, got_b = refs[2 * n_own], refs[2 * n_own + 1]
    outs = refs[2 * n_own + 2 :]
    first = core_ref[0] == 0
    rows, n4, _ = outs[0].shape
    n = n4 // 4
    for m, out in enumerate(outs):
        flat = out.reshape(rows * n4, FFZ)
        for s, (own, got) in enumerate(((own_a, got_a), (own_b, got_b))):
            for e in range(n):
                cols = slice((m * n + e) * FFZ, (m * n + e + 1) * FFZ)
                mine = own[0][:, cols].astype(F32)
                for ref in own[1:]:
                    mine = mine + ref[:, cols].astype(F32)
                theirs = got[:, cols].astype(F32)
                flat[pl.ds(s * n + e, rows, stride=n4), :] = jnp.where(first, mine, theirs)
                flat[pl.ds(2 * n + s * n + e, rows, stride=n4), :] = jnp.where(first, theirs, mine)

def finish(core, own_a, own_b, got_a, got_b, experts):
    rows, wide = got_a.shape
    part = 48
    steps = rows // part
    own = pl.BlockSpec((part, wide), lambda i, c: (c[0] * steps + i, 0))
    got = pl.BlockSpec((part, wide), lambda i, c: (i, 0))
    out = pl.BlockSpec((part, experts, FFZ), lambda i, c: (i, 0, 0))
    return pl.pallas_call(
        finish_body,
        grid_spec=pltpu.PrefetchScalarGridSpec(num_scalar_prefetch=1, grid=(steps,),
            in_specs=[own] * (len(own_a) + len(own_b)) + [got] * 2, out_specs=[out] * 3),
        out_shape=[jax.ShapeDtypeStruct((rows, experts, FFZ), F32)] * 3,
        compiler_params=pltpu.CompilerParams(vmem_limit_bytes=40 * MB),
    )(core, *own_a, *own_b, got_a, got_b)


def dot(a, b, dims=((1,), (0,)), out=F32):
    return lax.dot_general(a, b, (dims, ((), ())), preferred_element_type=F32).astype(out)


def flip(bit, size):
    return [(i, i ^ bit) for i in range(size)]


def swap_core(x):
    return lax.ppermute(x, "gx", flip(1, lax.axis_size("gx")))


def swap_x(x):
    return lax.ppermute(x, "gx", flip(2, lax.axis_size("gx")))


def swap_y(x):
    return lax.ppermute(x, "gx", flip(4, lax.axis_size("gx")))


def core_groups(size):
    return [[i for i in range(size) if i % 2 == c] for c in range(2)]


def after(x, *earlier):
    return lax.optimization_barrier((x, earlier))[0]


def plane_sum(x):
    size = lax.axis_size("gy")
    total = x
    for d in range(1, size):
        total = total + lax.ppermute(x, "gy", [(i, (i + d) % size) for i in range(size)])
    return total


def plane_scatter(parts):
    return lax.psum_scatter(parts, "gy", scatter_dimension=0, tiled=True)


def draw_body(c_ref, w_ref, o_ref):
    o_ref[...] = jnp.dot(c_ref[...], w_ref[...], preferred_element_type=F32).astype(BF)


def expert_draw(c, w_all):
    tokens = c.shape[0]
    width = w_all.shape[1] // 3
    cols = 2 * FFZ
    return pl.pallas_call(
        draw_body,
        grid=(width // cols,),
        in_specs=[
            pl.BlockSpec((tokens, D), lambda j: (0, 0)),
            pl.BlockSpec((D, cols), lambda j: (0, j)),
        ],
        out_specs=pl.BlockSpec((tokens, cols), lambda j: (0, j)),
        out_shape=jax.ShapeDtypeStruct((tokens, width), BF),
        compiler_params=pltpu.CompilerParams(vmem_limit_bytes=48 * MB),
    )(c, w_all)


def pad_lanes(x, width=128):
    return jnp.pad(x, ((0, 0), (0, width - x.shape[1])))


def shards(
    tokens,
    first_gain,
    w_query,
    w_key,
    w_value,
    w_out,
    second_gain,
    w_router,
    w_gate,
    w_up,
    w_down,
    routes,
    block_cotangent,
):
    length, slice_cols = tokens.shape
    rows_here = w_query.shape[0]
    chip_rows = 2 * rows_here
    heads = w_query.shape[1] // HD
    groups = w_key.shape[1] // HD
    experts_n = w_router.shape[1]
    mine_n = experts_n // 2
    span = mine_n * w_gate.shape[2]
    planes = lax.axis_size("gy")
    size = lax.axis_size("gx")
    core = lax.axis_index("gx") % 2
    chip = lax.axis_index("gx") // 2
    core_array = core.astype(jnp.int32)[None]
    plane = lax.axis_index("gy")
    small_mesh = size == 8

    def core_order(own, other):
        return jnp.where(core == 0, own, other), jnp.where(core == 0, other, own)

    gains = jnp.pad(jnp.stack([first_gain, second_gain]).astype(BF), ((0, 14), (0, 0)))
    joined = lax.all_gather(jnp.concatenate([tokens, gains], axis=0), "gy", axis=1, tiled=True)

    attn_own = jnp.concatenate(
        [w_query.astype(BF), w_key.astype(BF), w_value.astype(BF), w_out.astype(BF), pad_lanes(w_router.astype(BF))],
        axis=1,
    )
    keep, give = prepare(core_array, w_down, w_gate, w_up)
    attn_pair = jnp.concatenate(core_order(attn_own, swap_core(attn_own)), axis=0)
    got = swap_core(give)
    if small_mesh:
        half = attn_pair.shape[1] // 2
        attn_x, attn_y = swap_x(attn_pair), swap_y(attn_pair)
        attn_corner = jnp.concatenate([swap_y(attn_x[:, :half]), swap_x(attn_y[:, half:])], axis=1)
        attn_whole = jnp.zeros((4 * chip_rows, 2 * half), BF)
        for k, piece in enumerate((attn_pair, attn_x, attn_y, attn_corner)):
            attn_whole = lax.dynamic_update_slice(attn_whole, piece, ((chip ^ k) * chip_rows, 0))
        half = keep.shape[1] // 2
        keep_x, keep_y = swap_x(keep), swap_y(keep)
        got_x, got_y = swap_x(got), swap_y(got)
        lefts = [swap_y(keep_x[:, :half]), swap_y(got_x[:, :half])]
        rights = [swap_x(keep_y[:, half:]), swap_x(got_y[:, half:])]
        offsets = jnp.stack([((chip ^ k) * 2 + (core ^ o)) for k in range(4) for o in range(2)]).astype(jnp.int32)
        w_all = place(offsets, [keep, got, keep_x, got_x, keep_y, got_y], lefts, rights)
    else:
        attn_whole = lax.all_gather(attn_pair, "gx", axis=0, tiled=True, axis_index_groups=core_groups(size))
        pair = jnp.concatenate(core_order(keep, got), axis=0)
        w_all = lax.all_gather(pair, "gx", axis=0, tiled=True, axis_index_groups=core_groups(size))
    query_cols, pair_cols = w_query.shape[1], w_key.shape[1]
    qkv_cols = query_cols + 2 * pair_cols
    qkv_w = attn_whole[:, :qkv_cols]
    out_w = attn_whole[:, qkv_cols : qkv_cols + w_out.shape[1]]
    router_w = attn_whole[:, qkv_cols + w_out.shape[1] :]

    joined = after(joined, keep, got)
    token_full = joined[:length]
    gain_full = joined[length : length + 2].astype(F32)
    gain_one, gain_two = gain_full[0], gain_full[1]
    cot_own = lax.all_gather(after(block_cotangent, joined), "gy", axis=1, tiled=True)
    cot_both = jnp.concatenate([cot_own, swap_core(cot_own)], axis=0)
    down_raw = expert_draw(cot_both, w_all)

    iota = lax.broadcasted_iota(jnp.int32, (2 * length, 128), 1)
    routes_both = jnp.concatenate([routes, swap_core(routes)], axis=0)
    member = routes_both[:, 0:1] == iota
    for k in range(1, routes.shape[1]):
        member = member | (routes_both[:, k : k + 1] == iota)

    xf = token_full.astype(F32)
    scale_one = lax.rsqrt(jnp.mean(xf * xf, axis=1, keepdims=True) + epsilon)
    normed_one = (xf * scale_one * gain_one).astype(BF)
    qkv_raw = dot(normed_one, qkv_w)
    mixed, q_rot, k_rot, v_rot, log_total = attend(qkv_raw, heads, groups)
    whole_block = (length, heads * HD)
    attn_parts = project([(mixed, whole_block, (0, 0), out_w, 0)], planes)
    token_slice = tokens.astype(F32)
    residual = token_slice + plane_scatter(attn_parts).astype(F32)
    residual_own = lax.all_gather(residual.astype(BF), "gy", axis=1, tiled=True)
    residual_both = jnp.concatenate([residual_own, swap_core(residual_own)], axis=0)

    rf = residual_both.astype(F32)
    scale_two = lax.rsqrt(jnp.mean(rf * rf, axis=1, keepdims=True) + epsilon)
    normed_two = (rf * scale_two * gain_two).astype(BF)
    logits = jnp.where(member, dot(normed_two, router_w), masked)
    gate_exp = jnp.exp(logits - jnp.max(logits, axis=1, keepdims=True))
    gate_all = gate_exp / jnp.sum(gate_exp, axis=1, keepdims=True)
    gate_mine = pad_lanes(lax.dynamic_slice_in_dim(gate_all, core * mine_n, mine_n, 1))
    grads, dsum = expert_forward(normed_two, w_all, down_raw, gate_mine, 2 * length, 256)

    def back_half(i):
        block = (1, length, span)
        return project([(grads, block, (1, i, 0), w_all, 1), (grads, block, (2, i, 0), w_all, 2)], planes)

    back_other = swap_core(back_half(1))
    back_own = back_half(0)
    back_sum = (back_own.astype(F32) + back_other.astype(F32)).astype(BF)
    back_slice = plane_scatter(back_sum).astype(F32)

    dsum_own, dsum_got = dsum[:length, :mine_n], swap_core(dsum[length:, :mine_n])
    dsum_all = plane_sum(jnp.concatenate(core_order(dsum_own, dsum_got), axis=1).T).T
    gate_own = gate_all[:length, :experts_n]
    grad_picked = gate_own * (dsum_all - jnp.sum(gate_own * dsum_all, axis=1, keepdims=True))
    grad_logits = grad_picked.astype(BF)
    router_slice = lax.dynamic_slice_in_dim(router_w[:, :experts_n], plane * slice_cols, slice_cols, 0)
    grad_normed_two = back_slice + dot(grad_logits, router_slice, ((1,), (1,)))
    grad_h2_full = lax.all_gather(grad_normed_two.astype(BF), "gy", axis=1, tiled=True)

    if small_mesh:
        def terms(a, b, inputs):
            ids = jnp.stack([chip ^ k for k in a + b]).astype(jnp.int32)
            return expert_terms(ids, *inputs, chip_rows)

        inputs = after((cot_both, normed_two, grads), back_own)
        give_a, give_b = terms((1, 3), (2, 3), inputs)
        got_a, got_b = swap_x(give_a), swap_y(give_b)
        own_a, own_b = terms((0, 2), (0, 1), after(inputs, give_a, give_b))
        moe_inputs = after((grads, w_all), own_a, own_b)
        next_a = (own_a[chip_rows:].astype(F32) + got_a[chip_rows:].astype(F32)).astype(BF)
        next_b = (own_b[chip_rows:].astype(F32) + got_b[chip_rows:].astype(F32)).astype(BF)
        last_a, last_b = swap_y(next_a), swap_x(next_b)
        sum_a, sum_b = [own_a, got_a, last_a], [own_b, got_b, last_b]
    else:
        moe_inputs = (grads, w_all)
        next_a = next_b = back_sum

        def whole_term(side, m):
            left = cot_both if m == 0 else normed_two
            right = grads[m][:, side * (span // 2) : (side + 1) * (span // 2)]
            return dot(left, right, ((0,), (0,)), BF)

        def chips_sum(side):
            whole = jnp.concatenate([whole_term(side, m) for m in range(3)], axis=1)
            return [
                lax.psum_scatter(
                    whole, "gx", scatter_dimension=0, tiled=True, axis_index_groups=core_groups(size)
                )
            ]

        sum_a, sum_b = chips_sum(0), chips_sum(1)

    def partner_rows(parts):
        picked = [lax.dynamic_slice_in_dim(p, (1 - core) * rows_here, rows_here, 0).astype(F32) for p in parts]
        return swap_core(sum(picked).astype(BF))

    down_grad, gate_grad, up_grad = finish(
        core_array, sum_a, sum_b, partner_rows(sum_a), partner_rows(sum_b), experts_n
    )

    def moe_half(i):
        return project([(moe_inputs[0], (1, length, span), (0, i, 0), moe_inputs[1], 0)], planes)

    moe_other = swap_core(moe_half(1))
    moe_parts = (moe_half(0).astype(F32) + moe_other.astype(F32)).astype(BF)
    moe_slice = plane_scatter(after(moe_parts, grad_h2_full))
    block_out = (residual + moe_slice.astype(F32)).astype(BF)

    grad_h2_full = after(grad_h2_full, moe_parts, next_a, next_b)
    scale_own = scale_two[:length]
    residual_f = residual_own.astype(F32)
    grad_h2_f = grad_h2_full.astype(F32)
    inner = jnp.sum(grad_h2_f * gain_two * residual_f, axis=1, keepdims=True)
    grad_res_full = (
        cot_own.astype(F32)
        + scale_own * grad_h2_f * gain_two
        - residual_f * scale_own * scale_own * scale_own * inner / D
    ).astype(BF)
    gain_two_slice = second_gain.astype(BF).astype(F32)
    grad_residual = (
        block_cotangent.astype(F32)
        + scale_own * grad_normed_two * gain_two_slice
        - residual * scale_own * scale_own * scale_own * inner / D
    )
    second_gain_grad = jnp.sum(grad_normed_two * residual * scale_own, axis=0)

    grad_mixed = dot(grad_res_full, out_w, out=BF)
    grad_qkv = attend_back(q_rot, k_rot, v_rot, log_total, mixed, grad_mixed)
    dh_parts = project([(grad_qkv, (length, qkv_cols), (0, 0), qkv_w, 0)], planes)
    grad_normed_one = plane_scatter(dh_parts).astype(F32)

    left = after((grad_res_full, normed_one), dh_parts)
    attn_terms = jnp.concatenate(
        [dot(left[1], grad_qkv, ((0,), (0,)), BF), dot(left[0], mixed, ((0,), (0,)), BF),
         pad_lanes(dot(normed_two[:length], grad_logits, ((0,), (0,)), BF))],
        axis=1,
    )
    attn_sums = chips_total(attn_terms, chip, core, rows_here)
    query_grad = attn_sums[:, :query_cols]
    key_grad = attn_sums[:, query_cols : query_cols + pair_cols]
    value_grad = attn_sums[:, query_cols + pair_cols : qkv_cols]
    out_grad = attn_sums[:, qkv_cols : qkv_cols + w_out.shape[1]]
    router_grad = attn_sums[:, qkv_cols + w_out.shape[1] :][:, :experts_n]

    gain_one_slice = first_gain.astype(BF).astype(F32)
    scaled = grad_normed_one * gain_one_slice
    inner_one = plane_sum(jnp.sum(scaled * token_slice, axis=1)[None, :])[0][:, None]
    input_grad = (
        grad_residual
        + scale_one * scaled
        - token_slice * scale_one * scale_one * scale_one * inner_one / D
    ).astype(BF)
    first_gain_grad = jnp.sum(grad_normed_one * token_slice * scale_one, axis=0)
    first_gain_grad, second_gain_grad = lax.psum((first_gain_grad, second_gain_grad), "gx")
    return (
        block_out,
        input_grad,
        first_gain_grad,
        query_grad,
        key_grad,
        value_grad,
        out_grad,
        second_gain_grad,
        router_grad,
        gate_grad,
        up_grad,
        down_grad,
    )


def chips_total(terms, chip, core, rows_here):
    size = lax.axis_size("gx")
    if size != 8:
        return lax.psum_scatter(terms, "gx", scatter_dimension=0, tiled=True).astype(F32)
    cols = terms.shape[1]
    blocks = terms.reshape(4, 2, rows_here, cols)
    keep = jnp.where(core == 0, blocks[:, 0], blocks[:, 1])
    give = jnp.where(core == 0, blocks[:, 1], blocks[:, 0])
    mine = (keep.astype(F32) + swap_core(give).astype(F32)).astype(BF)
    half = cols // 2

    def part(k, side):
        return lax.dynamic_index_in_dim(mine, chip ^ k, 0, False)[:, side * half : (side + 1) * half]

    give_a = jnp.stack([part(1, 0), part(3, 0)])
    give_b = jnp.stack([part(2, 1), part(3, 1)])
    got_a, got_b = swap_x(give_a).astype(F32), swap_y(give_b).astype(F32)
    last_a = swap_y((part(2, 0).astype(F32) + got_a[1]).astype(BF))
    last_b = swap_x((part(1, 1).astype(F32) + got_b[1]).astype(BF))
    return jnp.concatenate(
        [part(0, 0).astype(F32) + got_a[0] + last_a.astype(F32), part(0, 1).astype(F32) + got_b[0] + last_b.astype(F32)],
        axis=1,
    )


def solution(mesh):
    placed = (
        P("gx", "gy"),
        P("gy"),
        P("gx", "gy"),
        P("gx", "gy"),
        P("gx", "gy"),
        P("gx", "gy"),
        P("gy"),
        P("gx", None),
        P("gx", None, "gy"),
        P("gx", None, "gy"),
        P("gx", None, "gy"),
        P("gx", None),
        P("gx", "gy"),
    )
    return jax.shard_map(
        shards,
        mesh=mesh,
        in_specs=placed,
        out_specs=(
            P("gx", "gy"),
            P("gx", "gy"),
            P("gy"),
            P("gx", "gy"),
            P("gx", "gy"),
            P("gx", "gy"),
            P("gx", "gy"),
            P("gy"),
            P("gx", None),
            P("gx", None, "gy"),
            P("gx", None, "gy"),
            P("gx", None, "gy"),
        ),
        check_vma=False,
    )
```

time: 1040 us -> 931 us (0.90)
  matrix products: 320 us -> 22.1 us
  Pallas kernels: 52.7 us -> 291 us
  waiting for transfers between devices: 264 us -> 407 us
  local copies, waits for them, and re-layouts: 162 us -> 53.1 us
  blocking collectives: 49.1 us -> 12.4 us
  other arithmetic: 115 us -> 81.3 us
    pallas_call x1 -> x15, Pallas kernels: 52.7 us -> 291 us  [the longest x6 86.3 us: project(): pl.pallas_call(partial(project_body, n), grid=(parts // 2,), in_specs=[pl...]
    dot_general x40 -> x7, matrix products: 250 us -> 22.1 us  [dot(): lax.dot_general(a, b, (dims, ((), ())), preferred_element_type=F32)]
    ppermute x17 -> x10, waiting for transfers between devices: 154 us -> 82 us  [swap_x(): return lax.ppermute(x, 'gx', flip(2, lax.axis_size('gx')))]
    dot_general x14 -> x0, matrix products: 69.6 us -> none  [the longest x4 21.2 us: block_scores(): jnp.einsum('qkgd,tkd->kgqt', query_block, key_rows, preferred_element_typ...]
    ppermute x17 -> x10, waiting for transfers between devices: 67.5 us -> 126 us  [swap_y(): return lax.ppermute(x, 'gx', flip(4, lax.axis_size('gx')))]
    reduce_scatter x2 -> x4, waiting for transfers between devices: 0.01 us -> 58.2 us  [plane_scatter(): return lax.psum_scatter(parts, 'gy', scatter_dimension=0, tiled=True)]
    all_gather x1, waiting for transfers between devices: 0.01 us -> 55.2 us  [shards(): residual_own = lax.all_gather(residual.astype(BF), 'gy', axis=1, tiled=True)]
    dynamic_update_slice x12 -> x2, local copies, waits for them, and re-layouts: 50.4 us -> 4.29 us  [shards(): lax.dynamic_update_slice(attn_whole, piece, ((chip ^ k) * chip_rows, 0))]
  transfers between devices with their start and end apart: 58 -> 45, of which waited for: 21 -> 18; matrix products, arithmetic and copies ran while one was open for 46% -> 10% of each run, Pallas kernels for 0% -> 19%
where the time goes in v2:
time: 931 us; the launch traced here: 921 us
  waiting for transfers between devices  407 us (44%)
  Pallas kernels  291 us (31%)
  other arithmetic  81.3 us (9%)
  local copies, waits for them, and re-layouts  53.1 us (6%)
  starting transfers between devices  38.6 us (4%)
  matrix products  22.1 us (2%)
  between operations  15.1 us (2%)
  blocking collectives  12.4 us (1%)
    ppermute x10, waiting for transfers between devices, swap_y(): return lax.ppermute(x, 'gx', flip(4, lax.axis_size('gx')))  126 us
    pallas_call x6, Pallas kernels, project(): pl.pallas_call(partial(project_body, n), grid=(parts // 2,), in_specs=[pl...  86.3 us
    ppermute x10, waiting for transfers between devices, swap_x(): return lax.ppermute(x, 'gx', flip(2, lax.axis_size('gx')))  82 us
    pallas_call x2, Pallas kernels, expert_terms(): pl.pallas_call(partial(term_body, steps), grid_spec=pltpu.PrefetchScalarG...  67.5 us
    reduce_scatter x4, waiting for transfers between devices, plane_scatter(): return lax.psum_scatter(parts, 'gy', scatter_dimension=0, tiled=True)  58.2 us
    all_gather x1, waiting for transfers between devices, shards(): residual_own = lax.all_gather(residual.astype(BF), 'gy', axis=1, tiled=True)  55.2 us
    pallas_call x1, Pallas kernels, expert_forward(): pl.pallas_call(partial(expert_body, rows, chunk), grid=(tokens // rows, s...  46 us
    ppermute x6, waiting for transfers between devices, plane_sum(): lax.ppermute(x, 'gy', [(i, (i + d) % size) for i in range(size)])  43.8 us
  transfers between devices with their start and end apart: 45, of which 18 were waited for; matrix products, arithmetic and copies ran while one was open for 10% of the time, Pallas kernels for 19%

profile of v2, /device:TPU:0, one launch (start us, length us, event | category | flops | bytes accessed | tf_op | source)
XLA Modules:
  0.0 920.7 jit_solution(15426886653149008694)
XLA Ops:
  33.2 18.7 %collective-permute-done.3 = bf16[384,1152]{1,0:T(8,128)(2,1)} collective-permute-done((bf16[384,1152]{1,0:T(8,128)(2,1)}, bf16[384,1152]{1,0:T(8,128)(2,1)}, u32[]{:S(2)}, u32[]{:S(2)}) %collective-permute-start.3) | collective-permute-done | bytes 884768 | tf_op jit(solution)/shard_map/ppermute | solution.py:397
  88.2 17.1 %shard_map.257 = (bf16[1024,384]{1,0:T(8,128)(2,1)S(1)}, bf16[6,1024,64]{2,1,0:T(8,128)(2,1)S(1)}, bf16[2,1024,64]{2,1,0:T(8,128)(2,1)S(1)}, bf16[2,1024,64]{2,1,0:T(8,128)(2,1)S(1)}, f32[1024,128]{1,0:T(8,128)S(1)}) custom-call(f32[1024,640]{1,0:T(8,128)S(1)} %fusion.65.qkv_ref, f32[1024,64]{1,0:T(8,128)S(1)} %copy-done.7, f32[1024,64]{1,0:T(8,128)S(1)} %copy-done.9), custom_call_target="tpu_custom_call" | custom-call | tf_op jit(solution)/shard_map/pallas_call | solution.py:80
  114.8 58.2 %reduce-scatter.5.cloned.1.call-done = bf16[1024,384]{1,0:T(8,128)(2,1)} async-done(((bf16[4096,384]{1,0:T(8,128)(2,1)}), bf16[1024,384]{1,0:T(8,128)(2,1)}) %reduce-scatter.5.cloned.1.call-update) | async-done | bytes 786448 | tf_op jit(solution)/shard_map/reduce_scatter | solution.py:417
  179.6 62.8 %collective-permute-done.7.refs_2_ = bf16[192,7680]{1,0:T(8,128)(2,1)S(1)} collective-permute-done((bf16[192,7680]{1,0:T(8,128)(2,1)S(1)}, bf16[192,7680]{1,0:T(8,128)(2,1)S(1)}, u32[]{:S(2)}, u32[]{:S(2)}) %collective-permute-start.7) | collective-permute-done | bytes 2949152 | tf_op jit(solution)/shard_map/ppermute | solution.py:393
  246.6 55.2 %all-gather.7.cloned.1.call-done = bf16[1024,1536]{1,0:T(8,128)(2,1)} async-done(((bf16[1024,384]{1,0:T(8,128)(2,1)}), bf16[1024,1536]{1,0:T(8,128)(2,1)}) %all-gather.7.cloned.1.call-update) | async-done | bytes 3145744 | tf_op jit(solution)/shard_map/all_gather | solution.py:536
  315.1 23.6 %collective-permute-done.11.refs_6_ = bf16[192,3840]{1,0:T(8,128)(2,1)} collective-permute-done((bf16[192,3840]{1,0:T(8,128)(2,1)}, bf16[192,3840]{1,0:T(8,128)(2,1)}, u32[]{:S(2)}, u32[]{:S(2)}) %collective-permute-start.11) | collective-permute-done | bytes 1474592 | tf_op jit(solution)/shard_map/ppermute | solution.py:397
  344.9 23.8 %collective-permute-done.12.refs_7_ = bf16[192,3840]{1,0:T(8,128)(2,1)} collective-permute-done((bf16[192,3840]{1,0:T(8,128)(2,1)}, bf16[192,3840]{1,0:T(8,128)(2,1)}, u32[]{:S(2)}, u32[]{:S(2)}) %collective-permute-start.12) | collective-permute-done | bytes 1474592 | tf_op jit(solution)/shard_map/ppermute | solution.py:397
  376.1 18.3 %shard_map.259.w_ref.wg_ref.wu_ref.refs_2_.refs_3_.refs_1_ = bf16[1536,7680]{1,0:T(8,128)(2,1)} custom-call(s32[8]{0:T(128)S(1)} %stack.90.offs_ref, bf16[192,7680]{1,0:T(8,128)(2,1)S(1)} %get-tuple-element.42.refs_0_, bf16[192,7680]{1,0:T(8,128)(2,1)} %collective-permute-done.refs_1_, bf16[192,7680]{1,0:T(8,128)(2,1)} %copy-done.27, ...), custom_call_target="tpu_custom_call" | custom-call | tf_op jit(solution)/shard_map/pallas_call | solution.py:330
  399.3 22.4 %shard_map.260.draw_ref = bf16[2048,2560]{1,0:T(8,128)(2,1)} custom-call(bf16[2048,1536]{1,0:T(8,128)(2,1)} %copy-done.17, bf16[1536,7680]{1,0:T(8,128)(2,1)} %shard_map.259.w_ref.wg_ref.wu_ref.refs_2_.refs_3_.refs_1_), custom_call_target="tpu_custom_call" | custom-call | tf_op jit(solution)/shard_map/pallas_call | solution.py:428
  439.9 46.0 %shard_map.261 = (bf16[3,2048,2560]{2,1,0:T(8,128)(2,1)}, f32[2048,128]{1,0:T(8,128)}) custom-call(bf16[2048,1536]{1,0:T(8,128)(2,1)} %copy-done.16, bf16[1536,7680]{1,0:T(8,128)(2,1)} %shard_map.259.w_ref.wg_ref.wu_ref.refs_2_.refs_3_.refs_1_, bf16[1536,7680]{1,0:T(8,128)(2,1)} %shard_map.259.w_ref.wg_ref.wu_ref.refs_2_.refs_3_.refs_1_, ...), custom_call_target="tpu_custom_call" | custom-call | tf_op jit(solution)/shard_map/pallas_call | solution.py:190
  485.9 24.1 %shard_map.267 = bf16[4,1024,384]{2,1,0:T(8,128)(2,1)} custom-call(bf16[3,2048,2560]{2,1,0:T(8,128)(2,1)} %get-tuple-element.58.refs_0_.refs_1_.g_ref, bf16[3,2048,2560]{2,1,0:T(8,128)(2,1)} %get-tuple-element.58.refs_0_.refs_1_.g_ref, bf16[1536,7680]{1,0:T(8,128)(2,1)} %shard_map.259.w_ref.wg_ref.wu_ref.refs_2_.refs_3_.refs_1_, ...), custom_call_target="tpu_custom_call" | custom-call | tf_op jit(solution)/shard_map/pallas_call | solution.py:227
  510.0 24.1 %shard_map.262 = bf16[4,1024,384]{2,1,0:T(8,128)(2,1)} custom-call(bf16[3,2048,2560]{2,1,0:T(8,128)(2,1)} %get-tuple-element.58.refs_0_.refs_1_.g_ref, bf16[3,2048,2560]{2,1,0:T(8,128)(2,1)} %get-tuple-element.58.refs_0_.refs_1_.g_ref, bf16[1536,7680]{1,0:T(8,128)(2,1)} %shard_map.259.w_ref.wg_ref.wu_ref.refs_2_.refs_3_.refs_1_, ...), custom_call_target="tpu_custom_call" | custom-call | tf_op jit(solution)/shard_map/pallas_call | solution.py:227
  539.1 33.8 %shard_map.263 = (bf16[768,3840]{1,0:T(8,128)(2,1)}, bf16[768,3840]{1,0:T(8,128)(2,1)}) custom-call(s32[4]{0:T(128)} %get-tuple-element.176.ids_ref, bf16[2048,1536]{1,0:T(8,128)(2,1)} %copy-done.17, bf16[2048,1536]{1,0:T(8,128)(2,1)} %copy-done.17, bf16[2048,1536]{1,0:T(8,128)(2,1)} %copy-done.16, bf16[2048,1536]{1,0:T(8,128)(2,1)} %copy-done.16, ...), custom_call_target="tpu_custom_call" | custom-call | tf_op jit(solution)/shard_map/pallas_call | solution.py:263
  575.8 33.7 %shard_map.264 = (bf16[768,3840]{1,0:T(8,128)(2,1)}, bf16[768,3840]{1,0:T(8,128)(2,1)}) custom-call(s32[4]{0:T(128)} %get-tuple-element.175.ids_ref, bf16[2048,1536]{1,0:T(8,128)(2,1)} %copy-done.17, bf16[2048,1536]{1,0:T(8,128)(2,1)} %copy-done.17, bf16[2048,1536]{1,0:T(8,128)(2,1)} %copy-done.16, bf16[2048,1536]{1,0:T(8,128)(2,1)} %copy-done.16, ...), custom_call_target="tpu_custom_call" | custom-call | tf_op jit(solution)/shard_map/pallas_call | solution.py:263
  609.5 13.4 %shard_map.266 = bf16[4,1024,384]{2,1,0:T(8,128)(2,1)} custom-call(bf16[3,2048,2560]{2,1,0:T(8,128)(2,1)} %get-tuple-element.58.refs_0_.refs_1_.g_ref, bf16[1536,7680]{1,0:T(8,128)(2,1)} %shard_map.259.w_ref.wg_ref.wu_ref.refs_2_.refs_3_.refs_1_), custom_call_target="tpu_custom_call" | custom-call | tf_op jit(solution)/shard_map/pallas_call | solution.py:227
  632.0 12.0 %collective-permute-done.22 = f32[40,1024]{0,1:T(8,128)S(1)} collective-permute-done((f32[40,1024]{0,1:T(8,128)S(1)}, f32[40,1024]{0,1:T(8,128)S(1)}, u32[]{:S(2)}, u32[]{:S(2)}) %collective-permute-start.22) | collective-permute-done | bytes 163872 | tf_op jit(solution)/shard_map/ppermute | solution.py:412
  646.3 31.8 %collective-permute-done.21 = f32[40,1024]{0,1:T(8,128)S(1)} collective-permute-done((f32[40,1024]{0,1:T(8,128)S(1)}, f32[40,1024]{0,1:T(8,128)S(1)}, u32[]{:S(2)}, u32[]{:S(2)}) %collective-permute-start.21) | collective-permute-done | bytes 163872 | tf_op jit(solution)/shard_map/ppermute | solution.py:412
  685.6 14.1 %shard_map.265 = bf16[4,1024,384]{2,1,0:T(8,128)(2,1)} custom-call(bf16[3,2048,2560]{2,1,0:T(8,128)(2,1)} %get-tuple-element.58.refs_0_.refs_1_.g_ref, bf16[1536,7680]{1,0:T(8,128)(2,1)} %shard_map.259.w_ref.wg_ref.wu_ref.refs_2_.refs_3_.refs_1_), custom_call_target="tpu_custom_call" | custom-call | tf_op jit(solution)/shard_map/pallas_call | solution.py:227
  715.1 29.3 %all-gather.11.cloned.1.call-done = bf16[1024,1536]{1,0:T(8,128)(2,1)} async-done(((bf16[1024,384]{1,0:T(8,128)(2,1)}), bf16[1024,1536]{1,0:T(8,128)(2,1)}) %all-gather.11.cloned.1.call-update) | async-done | bytes 3145744 | tf_op jit(solution)/shard_map/all_gather | solution.py:564
  757.7 19.5 %shard_map.268.refs_0_ = bf16[1024,640]{1,0:T(8,128)(2,1)S(1)} custom-call(bf16[6,1024,64]{2,1,0:T(8,128)(2,1)} %copy-done.11, bf16[2,1024,64]{2,1,0:T(8,128)(2,1)S(1)} %get-tuple-element.64.k_ref, bf16[2,1024,64]{2,1,0:T(8,128)(2,1)S(1)} %copy-done.13, f32[1024,128]{1,0:T(8,128)S(1)} %copy-done.15, bf16[1024,384]{1,0:T(8,128)(2,1)S(1)} %copy-done.5, ...), custom_call_target="tpu_custom_call" | custom-call | tf_op jit(solution)/shard_map/pallas_call | solution.py:138
  804.9 47.8 %collective-permute-done.33.refs_2_ = bf16[384,3840]{1,0:T(8,128)(2,1)S(1)} collective-permute-done((bf16[384,3840]{1,0:T(8,128)(2,1)}, bf16[384,3840]{1,0:T(8,128)(2,1)S(1)}, u32[]{:S(2)}, u32[]{:S(2)}) %collective-permute-start.33) | collective-permute-done | bytes 2949152 | tf_op jit(solution)/shard_map/ppermute | solution.py:397
  864.4 10.1 %collective-permute-done.31 = bf16[2,192,576]{2,1,0:T(8,128)(2,1)S(1)} collective-permute-done((bf16[2,192,576]{2,1,0:T(8,128)(2,1)S(1)}, bf16[2,192,576]{2,1,0:T(8,128)(2,1)S(1)}, u32[]{:S(2)}, u32[]{:S(2)}) %collective-permute-start.31) | collective-permute-done | bytes 442400 | tf_op jit(solution)/shard_map/ppermute | solution.py:397
  878.0 8.0 shard_map.270
  897.3 12.4 %all-reduce.4 = (f32[384]{0:T(512)}, f32[384]{0:T(512)}) all-reduce(f32[384]{0:T(512)S(1)} %get-tuple-element.132, f32[384]{0:T(512)S(1)} %get-tuple-element.134), channel_id=1, replica_groups=mesh['gx'=8,'gy'=4] {'gx'}, use_global_device_ids=true, to_apply=%region_12.13 | all-reduce | flops 768 | bytes 6144 | tf_op jit(solution)/shard_map/psum | solution.py:660
  (273 shorter events, 245.4 us)
Async XLA Ops:
  7.2 70.6 %all-gather.5.cloned.1.call-start = ((), (), s32[]{:S(2)}) async-start(), calls=%async_computation.4 | async-start | bytes 3993600 | tf_op jit(solution)/shard_map/all_gather | solution.py:480
  10.8 162.2 %reduce-scatter.5.cloned.1.call-start = ((), (), s32[]{:S(2)}) async-start(), calls=%async_computation.5 | async-start | bytes 3932160 | tf_op jit(solution)/shard_map/reduce_scatter | solution.py:417
  24.1 47.5 %collective-permute-start = (bf16[192,7680]{1,0:T(8,128)(2,1)}, bf16[192,7680]{1,0:T(8,128)(2,1)}, u32[]{:S(2)}, u32[]{:S(2)}) collective-permute-start(bf16[192,7680]{1,0:T(8,128)(2,1)} %get-tuple-element.43), channel_id=1, source_target_pairs={{0,4},{4,0},{8,12},{12,8},{16,20},{20,16},{24,28},{28,24},{1,5},{5... | collective-permute-start | bytes 8847368 | tf_op jit(solution)/shard_map/ppermute | solution.py:389
  114.0 132.6 %all-gather.9.cloned.1.call-start = ((), (), s32[]{:S(2)}) async-start(), calls=%async_computation.7 | async-start | bytes 3932160 | tf_op jit(solution)/shard_map/all_gather | solution.py:517
  114.7 187.1 %all-gather.7.cloned.1.call-start = ((), (), s32[]{:S(2)}) async-start(), calls=%async_computation.6 | async-start | bytes 3932160 | tf_op jit(solution)/shard_map/all_gather | solution.py:536
  175.4 504.2 %reduce-scatter.7.cloned.1.call-start = ((), (), s32[]{:S(2)}) async-start(), calls=%async_computation.8 | async-start | bytes 3932160 | tf_op jit(solution)/shard_map/reduce_scatter | solution.py:417
  175.5 66.9 %collective-permute-start.7 = (bf16[192,7680]{1,0:T(8,128)(2,1)S(1)}, bf16[192,7680]{1,0:T(8,128)(2,1)S(1)}, u32[]{:S(2)}, u32[]{:S(2)}) collective-permute-start(bf16[192,7680]{1,0:T(8,128)(2,1)S(1)} %get-tuple-element.42.refs_0_), channel_id=1, source_target_pairs={{0,8},{4,12},{8,0},{12,4},{16,24},{20,28},{24,16},{28,20},{1,9},{5... | collective-permute-start | bytes 8847368 | tf_op jit(solution)/shard_map/ppermute | solution.py:393
  177.0 69.6 %collective-permute-start.9 = (bf16[192,7680]{1,0:T(8,128)(2,1)S(1)}, bf16[192,7680]{1,0:T(8,128)(2,1)}, u32[]{:S(2)}, u32[]{:S(2)}) collective-permute-start(bf16[192,7680]{1,0:T(8,128)(2,1)S(1)} %get-tuple-element.42.refs_0_), channel_id=1, source_target_pairs={{0,16},{4,20},{8,24},{12,28},{16,0},{20,4},{24,8},{28,12},{1,17},{... | collective-permute-start | bytes 8847368 | tf_op jit(solution)/shard_map/ppermute | solution.py:397
  178.5 125.8 %collective-permute-start.8 = (bf16[192,7680]{1,0:T(8,128)(2,1)}, bf16[192,7680]{1,0:T(8,128)(2,1)}, u32[]{:S(2)}, u32[]{:S(2)}) collective-permute-start(bf16[192,7680]{1,0:T(8,128)(2,1)} %collective-permute-done.refs_1_), channel_id=1, source_target_pairs={{0,8},{4,12},{8,0},{12,4},{16,24},{20,28},{24,16},{28,20},{1,9},{5... | collective-permute-start | bytes 8847368 | tf_op jit(solution)/shard_map/ppermute | solution.py:393
  179.0 130.5 %collective-permute-start.10 = (bf16[192,7680]{1,0:T(8,128)(2,1)}, bf16[192,7680]{1,0:T(8,128)(2,1)}, u32[]{:S(2)}, u32[]{:S(2)}) collective-permute-start(bf16[192,7680]{1,0:T(8,128)(2,1)} %collective-permute-done.refs_1_), channel_id=1, source_target_pairs={{0,16},{4,20},{8,24},{12,28},{16,0},{20,4},{24,8},{28,12},{1,17},{... | collective-permute-start | bytes 8847368 | tf_op jit(solution)/shard_map/ppermute | solution.py:397
  245.1 93.6 %collective-permute-start.11 = (bf16[192,3840]{1,0:T(8,128)(2,1)}, bf16[192,3840]{1,0:T(8,128)(2,1)}, u32[]{:S(2)}, u32[]{:S(2)}) collective-permute-start(bf16[192,3840]{1,0:T(8,128)(2,1)} %slice.212), channel_id=1, source_target_pairs={{0,16},{4,20},{8,24},{12,28},{16,0},{20,4},{24,8},{28,12},{1,17},{... | collective-permute-start | bytes 4423688 | tf_op jit(solution)/shard_map/ppermute | solution.py:397
  246.6 148.0 %collective-permute-start.15 = (bf16[1024,1536]{1,0:T(8,128)(2,1)}, bf16[1024,1536]{1,0:T(8,128)(2,1)}, u32[]{:S(2)}, u32[]{:S(2)}) collective-permute-start(bf16[1024,1536]{1,0:T(8,128)(2,1)} %all-gather.9.cloned.1.call-done), channel_id=1, source_target_pairs={{0,4},{4,0},{8,12},{12,8},{16,20},{20,16},{24,28},{28,24},{1,5},{5... | collective-permute-start | bytes 9437192 | tf_op jit(solution)/shard_map/ppermute | solution.py:389
  301.9 119.8 %collective-permute-start.6 = (bf16[1024,1536]{1,0:T(8,128)(2,1)}, bf16[1024,1536]{1,0:T(8,128)(2,1)}, u32[]{:S(2)}, u32[]{:S(2)}) collective-permute-start(bf16[1024,1536]{1,0:T(8,128)(2,1)} %all-gather.7.cloned.1.call-done), channel_id=1, source_target_pairs={{0,4},{4,0},{8,12},{12,8},{16,20},{20,16},{24,28},{28,24},{1,5},{5... | collective-permute-start | bytes 9437192 | tf_op jit(solution)/shard_map/ppermute | solution.py:389
  313.6 55.1 %collective-permute-start.12 = (bf16[192,3840]{1,0:T(8,128)(2,1)}, bf16[192,3840]{1,0:T(8,128)(2,1)}, u32[]{:S(2)}, u32[]{:S(2)}) collective-permute-start(bf16[192,3840]{1,0:T(8,128)(2,1)} %slice.213), channel_id=1, source_target_pairs={{0,16},{4,20},{8,24},{12,28},{16,0},{20,4},{24,8},{28,12},{1,17},{... | collective-permute-start | bytes 4423688 | tf_op jit(solution)/shard_map/ppermute | solution.py:397
  538.4 206.0 %all-gather.11.cloned.1.call-start = ((), (), s32[]{:S(2)}) async-start(), calls=%async_computation.9 | async-start | bytes 3932160 | tf_op jit(solution)/shard_map/all_gather | solution.py:564
  572.8 132.2 %collective-permute-start.23 = (bf16[768,3840]{1,0:T(8,128)(2,1)}, bf16[768,3840]{1,0:T(8,128)(2,1)}, u32[]{:S(2)}, u32[]{:S(2)}) collective-permute-start(bf16[768,3840]{1,0:T(8,128)(2,1)} %get-tuple-element.51), channel_id=1, source_target_pairs={{0,8},{4,12},{8,0},{12,4},{16,24},{20,28},{24,16},{28,20},{1,9},{5... | collective-permute-start | bytes 17694728 | tf_op jit(solution)/shard_map/ppermute | solution.py:393
  574.3 135.8 %collective-permute-start.24 = (bf16[768,3840]{1,0:T(8,128)(2,1)}, bf16[768,3840]{1,0:T(8,128)(2,1)}, u32[]{:S(2)}, u32[]{:S(2)}) collective-permute-start(bf16[768,3840]{1,0:T(8,128)(2,1)} %get-tuple-element.52), channel_id=1, source_target_pairs={{0,16},{4,20},{8,24},{12,28},{16,0},{20,4},{24,8},{28,12},{1,17},{... | collective-permute-start | bytes 17694728 | tf_op jit(solution)/shard_map/ppermute | solution.py:397
  622.9 76.8 %collective-permute-start.17 = (bf16[4096,384]{1,0:T(8,128)(2,1)}, bf16[4096,384]{1,0:T(8,128)(2,1)}, u32[]{:S(2)}, u32[]{:S(2)}) collective-permute-start(bf16[4096,384]{1,0:T(8,128)(2,1)} %bitcast.103), channel_id=1, source_target_pairs={{0,4},{4,0},{8,12},{12,8},{16,20},{20,16},{24,28},{28,24},{1,5},{5... | collective-permute-start | bytes 9437192 | tf_op jit(solution)/shard_map/ppermute | solution.py:389
  631.8 46.3 %collective-permute-start.21 = (f32[40,1024]{0,1:T(8,128)S(1)}, f32[40,1024]{0,1:T(8,128)S(1)}, u32[]{:S(2)}, u32[]{:S(2)}) collective-permute-start(f32[40,1024]{0,1:T(8,128)S(1)} %maximum_bitcast_fusion), channel_id=1, source_target_pairs={{0,2},{1,3},{2,0},{3,1},{4,6},{5,7},{6,4},{7,5},{8,10},{9,11},{10,... | collective-permute-start | bytes 491528 | tf_op jit(solution)/shard_map/ppermute | solution.py:412
  682.5 204.6 %reduce-scatter.11.cloned.1.call-start = ((), (), s32[]{:S(2)}) async-start(), calls=%async_computation.11 | async-start | bytes 3932160 | tf_op jit(solution)/shard_map/reduce_scatter | solution.py:417
  784.0 125.7 %reduce-scatter.9.cloned.1.call-start = ((), (), s32[]{:S(2)}) async-start(), calls=%async_computation.10 | async-start | bytes 3932160 | tf_op jit(solution)/shard_map/reduce_scatter | solution.py:417
  786.8 65.9 %collective-permute-start.33 = (bf16[384,3840]{1,0:T(8,128)(2,1)}, bf16[384,3840]{1,0:T(8,128)(2,1)S(1)}, u32[]{:S(2)}, u32[]{:S(2)}) collective-permute-start(bf16[384,3840]{1,0:T(8,128)(2,1)} %add_convert_fusion.2), channel_id=1, source_target_pairs={{0,16},{4,20},{8,24},{12,28},{16,0},{20,4},{24,8},{28,12},{1,17},{... | collective-permute-start | bytes 8847368 | tf_op jit(solution)/shard_map/ppermute | solution.py:397
  788.4 66.8 %collective-permute-start.34 = (bf16[384,3840]{1,0:T(8,128)(2,1)}, bf16[384,3840]{1,0:T(8,128)(2,1)}, u32[]{:S(2)}, u32[]{:S(2)}) collective-permute-start(bf16[384,3840]{1,0:T(8,128)(2,1)} %add_convert_fusion.1), channel_id=1, source_target_pairs={{0,8},{4,12},{8,0},{12,4},{16,24},{20,28},{24,16},{28,20},{1,9},{5... | collective-permute-start | bytes 8847368 | tf_op jit(solution)/shard_map/ppermute | solution.py:393
  804.9 53.6 %collective-permute-start.28 = (bf16[4,192,1152]{2,1,0:T(8,128)(2,1)}, bf16[4,192,1152]{2,1,0:T(8,128)(2,1)}, u32[]{:S(2)}, u32[]{:S(2)}) collective-permute-start(bf16[4,192,1152]{2,1,0:T(8,128)(2,1)} %select_bitcast_fusion), channel_id=1, source_target_pairs={{0,4},{4,0},{8,12},{12,8},{16,20},{20,16},{24,28},{28,24},{1,5},{5... | collective-permute-start | bytes 5308424 | tf_op jit(solution)/shard_map/ppermute | solution.py:389
  (67 other events, 1254.6 us)
Sparse Core Ops, SparseCore 0:
  10.9 66.8 all-gather.4
  114.1 58.8 reduce-scatter.4
  174.5 63.3 all-gather.8
  239.9 61.9 all-gather.6
  538.5 60.6 reduce-scatter.6
  682.7 61.7 all-gather.10
  784.1 58.8 reduce-scatter.10
  845.3 60.4 reduce-scatter.8

commit v3 on v2

--- a/solution.py
+++ b/solution.py
@@ -18,6 +18,11 @@
 masked = -1e30
 VM = pl.BlockSpec(memory_space=pltpu.VMEM)
 MB = 1024 * 1024
+
+
+def lasts(us):
+    return pl.CostEstimate(flops=int(us * 1e9), bytes_accessed=int(us * 2.5e6), transcendentals=0)
+
 
 def rope_tables(length):
     frequency = np.exp(np.arange(HD // 2) * (-2.0 * math.log(10000.0) / HD)).astype(np.float32)
@@ -89,6 +94,7 @@
             S((length, 128), F32),
         ],
         scratch_shapes=[pltpu.VMEM((heads, length, HD), BF)],
+        cost_estimate=lasts(17),
         compiler_params=pltpu.CompilerParams(vmem_limit_bytes=40 * MB),
     )(qkv, cosine, sine)
 
@@ -147,6 +153,7 @@
             pltpu.VMEM((groups, length, HD), F32),
             pltpu.VMEM((groups, length, HD), F32),
         ],
+        cost_estimate=lasts(19),
         compiler_params=pltpu.CompilerParams(vmem_limit_bytes=48 * MB),
     )(q, k, v, log_total, mixed, do, cosine, sine)
 
@@ -184,7 +191,7 @@
             sums = jnp.where(hot, s, sums)
         dsum_ref[at] = sums
 
-def expert_forward(h, w_all, draw, gate, rows=1024, chunk=256):
+def expert_forward(h, w_gu, draw, gate, rows=1024, chunk=256):
     tokens, width = draw.shape
     steps = width // (2 * FFZ)
     return pl.pallas_call(
@@ -192,8 +199,8 @@
         grid=(tokens // rows, steps),
         in_specs=[
             pl.BlockSpec((rows, D), lambda i, j: (i, 0)),
+            pl.BlockSpec((D, 2 * FFZ), lambda i, j: (0, j)),
             pl.BlockSpec((D, 2 * FFZ), lambda i, j: (0, steps + j)),
-            pl.BlockSpec((D, 2 * FFZ), lambda i, j: (0, 2 * steps + j)),
             pl.BlockSpec((rows, 2 * FFZ), lambda i, j: (i, j)),
             pl.BlockSpec((rows, 128), lambda i, j: (i, 0)),
         ],
@@ -205,8 +212,9 @@
             jax.ShapeDtypeStruct((3, tokens, width), BF),
             jax.ShapeDtypeStruct((tokens, 128), F32),
         ],
+        cost_estimate=lasts(46),
         compiler_params=pltpu.CompilerParams(vmem_limit_bytes=56 * MB),
-    )(h, w_all, w_all, draw, gate)
+    )(h, w_gu, w_gu, draw, gate)
 
 def project_body(n, *refs):
     dims = (((1,), (1,)), ((), ()))
@@ -231,6 +239,7 @@
         + [pl.BlockSpec((2 * cols, width), partial(lambda at, j: (j, at), t[4])) for t in terms],
         out_specs=pl.BlockSpec((2, rows, cols), lambda j: (j, 0, 0)),
         out_shape=jax.ShapeDtypeStruct((parts, rows, cols), BF),
+        cost_estimate=lasts(rows * width * D * n / 3.5e8 + 2),
         compiler_params=pltpu.CompilerParams(vmem_limit_bytes=56 * MB),
     )(*[t[0] for t in terms], *[t[3] for t in terms])
     return total.reshape(parts * rows, cols)
@@ -273,73 +282,42 @@
             ],
         ),
         out_shape=[out, out],
+        cost_estimate=lasts(34),
         compiler_params=pltpu.CompilerParams(vmem_limit_bytes=56 * MB),
     )(ids, c, c, h, h, grads)
 
-def prepare_body(core_ref, down_ref, gate_ref, up_ref, keep_ref, give_ref):
+def prepare_body(core_ref, down_ref, gate_ref, up_ref, keep_d_ref, keep_gu_ref, give_d_ref, give_gu_ref):
     first = core_ref[0] == 0
     rows, n2, _ = down_ref.shape
     n = n2 // 2
     for m, ref in enumerate((down_ref, gate_ref, up_ref)):
         flat = ref.reshape(rows * n2, FFZ)
+        keep_ref, give_ref = (keep_d_ref, give_d_ref) if m == 0 else (keep_gu_ref, give_gu_ref)
         for e in range(n):
             lo = flat[pl.ds(e, rows, stride=n2), :]
             hi = flat[pl.ds(n + e, rows, stride=n2), :]
-            at = (m * n + e) * FFZ
+            at = (max(m - 1, 0) * n + e) * FFZ
             keep_ref[:, at : at + FFZ] = jnp.where(first, lo, hi).astype(BF)
             give_ref[:, at : at + FFZ] = jnp.where(first, hi, lo).astype(BF)
+
 
 def prepare(core, down, gate, up):
     rows, n, _ = down.shape
     part = 48
-    wide = 3 * n * FFZ // 2
+    span = n * FFZ // 2
     weight = pl.BlockSpec((part, n, FFZ), lambda i, c: (i, 0, 0))
-    out = pl.BlockSpec((part, wide), lambda i, c: (i, 0))
+    outs = [pl.BlockSpec((part, w), lambda i, c: (i, 0)) for w in (span, 2 * span)]
+    shapes = [jax.ShapeDtypeStruct((rows, w), BF) for w in (span, 2 * span)]
     return pl.pallas_call(
         prepare_body,
-        grid_spec=pltpu.PrefetchScalarGridSpec(num_scalar_prefetch=1, grid=(rows // part,), in_specs=[weight] * 3, out_specs=[out] * 2),
-        out_shape=[jax.ShapeDtypeStruct((rows, wide), BF)] * 2,
+        grid_spec=pltpu.PrefetchScalarGridSpec(
+            num_scalar_prefetch=1, grid=(rows // part,), in_specs=[weight] * 3, out_specs=outs * 2
+        ),
+        out_shape=shapes * 2,
+        cost_estimate=lasts(5),
         compiler_params=pltpu.CompilerParams(vmem_limit_bytes=40 * MB),
     )(core, down, gate, up)
 
-def place_body(offs_ref, *refs):
-    fulls, lefts, rights, out = refs[:6], refs[6:8], refs[8:10], refs[10]
-    rows = fulls[0].shape[0]
-
-    def put(i, ref):
-        out[pl.ds(pl.multiple_of(offs_ref[i] * rows, 16), rows), :] = ref[...]
-
-    for i, ref in enumerate(fulls):
-        put(i, ref)
-    left = pl.program_id(0) < pl.num_programs(0) // 2
-
-    @pl.when(left)
-    def _():
-        for i, ref in enumerate(lefts):
-            put(6 + i, ref)
-
-    @pl.when(jnp.logical_not(left))
-    def _():
-        for i, ref in enumerate(rights):
-            put(6 + i, ref)
-
-def place(offsets, fulls, lefts, rights, steps=10):
-    rows, wide = fulls[0].shape
-    cols = wide // steps
-    half = steps // 2
-    return pl.pallas_call(
-        place_body,
-        grid_spec=pltpu.PrefetchScalarGridSpec(
-            num_scalar_prefetch=1,
-            grid=(steps,),
-            in_specs=[pl.BlockSpec((rows, cols), lambda j, o: (0, j))] * 6
-            + [pl.BlockSpec((rows, cols), lambda j, o: (0, jnp.minimum(j, half - 1)))] * 2
-            + [pl.BlockSpec((rows, cols), lambda j, o: (0, jnp.maximum(j - half, 0)))] * 2,
-            out_specs=pl.BlockSpec((8 * rows, cols), lambda j, o: (0, j)),
-        ),
-        out_shape=jax.ShapeDtypeStruct((8 * rows, wide), fulls[0].dtype),
-        compiler_params=pltpu.CompilerParams(vmem_limit_bytes=40 * MB),
-    )(offsets, *fulls, *lefts, *rights)
 
 def finish_body(core_ref, *refs):
     n_own = (len(refs) - 5) // 2
@@ -373,6 +351,7 @@
         grid_spec=pltpu.PrefetchScalarGridSpec(num_scalar_prefetch=1, grid=(steps,),
             in_specs=[own] * (len(own_a) + len(own_b)) + [got] * 2, out_specs=[out] * 3),
         out_shape=[jax.ShapeDtypeStruct((rows, experts, FFZ), F32)] * 3,
+        cost_estimate=lasts(9),
         compiler_params=pltpu.CompilerParams(vmem_limit_bytes=40 * MB),
     )(core, *own_a, *own_b, got_a, got_b)
 
@@ -413,6 +392,15 @@
     return total
 
 
+def plane_shift(x, d):
+    size = lax.axis_size("gy")
+    return lax.ppermute(x, "gy", [(i, (i + d) % size) for i in range(size)])
+
+
+def plane_pieces(x):
+    return [x] + [plane_shift(x, d) for d in range(1, 4)]
+
+
 def plane_scatter(parts):
     return lax.psum_scatter(parts, "gy", scatter_dimension=0, tiled=True)
 
@@ -421,9 +409,9 @@
     o_ref[...] = jnp.dot(c_ref[...], w_ref[...], preferred_element_type=F32).astype(BF)
 
 
-def expert_draw(c, w_all):
+def expert_draw(c, w_down):
     tokens = c.shape[0]
-    width = w_all.shape[1] // 3
+    width = w_down.shape[1]
     cols = 2 * FFZ
     return pl.pallas_call(
         draw_body,
@@ -434,8 +422,103 @@
         ],
         out_specs=pl.BlockSpec((tokens, cols), lambda j: (0, j)),
         out_shape=jax.ShapeDtypeStruct((tokens, width), BF),
+        cost_estimate=lasts(22),
         compiler_params=pltpu.CompilerParams(vmem_limit_bytes=48 * MB),
-    )(c, w_all)
+    )(c, w_down)
+
+
+def norm_pieces(slots_ref, pieces, gains, normed_ref, scale_ref, joined_ref):
+    cols = pieces[0].shape[1]
+    total = 0.0
+    for ref in pieces:
+        x = ref[...].astype(F32)
+        total = total + jnp.sum(x * x, axis=1, keepdims=True)
+    scale = lax.rsqrt(total / D + epsilon)
+    scale_ref[...] = scale
+    for d, ref in enumerate(pieces):
+        at = pl.ds(pl.multiple_of(slots_ref[d] * cols, 128), cols)
+        x = ref[...]
+        if joined_ref is not None:
+            joined_ref[:, at] = x
+        normed_ref[:, at] = (x.astype(F32) * scale * gains[d].astype(F32)).astype(BF)
+
+
+def first_norm_body(slots_ref, *refs):
+    pieces, tails, (normed_ref, scale_ref, gain_ref) = refs[:4], refs[4:8], refs[8:]
+    cols = pieces[0].shape[1]
+    norm_pieces(slots_ref, pieces, [ref[0:1] for ref in tails], normed_ref, scale_ref, None)
+    for d, ref in enumerate(tails):
+        gain_ref[:, pl.ds(pl.multiple_of(slots_ref[d] * cols, 128), cols)] = ref[...]
+
+
+def second_norm_body(slots_ref, *refs):
+    pieces, gain_ref, (normed_ref, scale_ref, joined_ref) = refs[:4], refs[4], refs[5:]
+    cols = pieces[0].shape[1]
+    gains = [gain_ref[1:2, pl.ds(pl.multiple_of(slots_ref[d] * cols, 128), cols)] for d in range(4)]
+    norm_pieces(slots_ref, pieces, gains, normed_ref, scale_ref, joined_ref)
+
+
+def norm_planes(slots, pieces, gains=None):
+    first = gains is None
+    cols = pieces[0].shape[1]
+    length = pieces[0].shape[0] - (16 if first else 0)
+    rows = 256
+    wide = pl.BlockSpec((rows, D), lambda i, s: (i, 0))
+    piece = pl.BlockSpec((rows, cols), lambda i, s: (i, 0))
+    tail = pl.BlockSpec((16, cols), lambda i, s: (length // 16, 0))
+    all_gains = pl.BlockSpec((16, D), lambda i, s: (0, 0))
+    shape = jax.ShapeDtypeStruct
+    return pl.pallas_call(
+        first_norm_body if first else second_norm_body,
+        grid_spec=pltpu.PrefetchScalarGridSpec(
+            num_scalar_prefetch=1,
+            grid=(length // rows,),
+            in_specs=[piece] * 4 + ([tail] * 4 if first else [all_gains]),
+            out_specs=[wide, pl.BlockSpec((rows, 1), lambda i, s: (i, 0)), all_gains if first else wide],
+        ),
+        out_shape=[
+            shape((length, D), BF),
+            shape((length, 1), F32),
+            shape((16, D) if first else (length, D), BF),
+        ],
+        cost_estimate=lasts(6),
+    )(slots, *pieces, *(pieces if first else [gains]))
+
+
+def lay_body(slots_ref, *refs):
+    cols = refs[0].shape[1]
+    for d in range(4):
+        refs[4][:, pl.ds(pl.multiple_of(slots_ref[d] * cols, 128), cols)] = refs[d][...]
+
+
+def lay_planes(slots, pieces):
+    rows, cols = pieces[0].shape
+    return pl.pallas_call(
+        lay_body,
+        in_specs=[pl.BlockSpec(memory_space=pltpu.SMEM)] + [VM] * 4,
+        out_specs=VM,
+        out_shape=jax.ShapeDtypeStruct((rows, D), pieces[0].dtype),
+        cost_estimate=lasts(3),
+    )(slots, *pieces)
+
+
+def spread_body(slots_ref, a_ref, w_ref, *outs):
+    a = a_ref[...]
+    cols = outs[0].shape[1]
+    for d, o_ref in enumerate(outs):
+        w = w_ref[pl.ds(pl.multiple_of(slots_ref[d] * cols, 128), cols), :]
+        o_ref[...] = lax.dot_general(a, w, (((1,), (1,)), ((), ())), preferred_element_type=F32).astype(BF)
+
+
+def spread(slots, a, w):
+    rows = a.shape[0]
+    return pl.pallas_call(
+        spread_body,
+        in_specs=[pl.BlockSpec(memory_space=pltpu.SMEM), VM, VM],
+        out_specs=[VM] * 4,
+        out_shape=[jax.ShapeDtypeStruct((rows, D // 4), BF)] * 4,
+        cost_estimate=lasts(5),
+    )(slots, a, w)
 
 
 def pad_lanes(x, width=128):
@@ -476,47 +559,55 @@
     def core_order(own, other):
         return jnp.where(core == 0, own, other), jnp.where(core == 0, other, own)
 
-    gains = jnp.pad(jnp.stack([first_gain, second_gain]).astype(BF), ((0, 14), (0, 0)))
-    joined = lax.all_gather(jnp.concatenate([tokens, gains], axis=0), "gy", axis=1, tiled=True)
+    before = jnp.stack([(plane - d) % planes for d in range(4)]).astype(jnp.int32)
+    onward = jnp.stack([(plane + d) % planes for d in range(4)]).astype(jnp.int32)
+
+    gain_rows = jnp.pad(jnp.stack([first_gain, second_gain]).astype(BF), ((0, 14), (0, 0)))
+    joined = lax.all_gather(jnp.concatenate([tokens, gain_rows], axis=0), "gy", axis=1, tiled=True)
+    gains = joined[length:]
+    gain_two = gains[1:2].astype(F32)
 
     attn_own = jnp.concatenate(
         [w_query.astype(BF), w_key.astype(BF), w_value.astype(BF), w_out.astype(BF), pad_lanes(w_router.astype(BF))],
         axis=1,
     )
-    keep, give = prepare(core_array, w_down, w_gate, w_up)
-    attn_pair = jnp.concatenate(core_order(attn_own, swap_core(attn_own)), axis=0)
-    got = swap_core(give)
     if small_mesh:
+        attn_pair = jnp.concatenate(core_order(attn_own, swap_core(attn_own)), axis=0)
         half = attn_pair.shape[1] // 2
         attn_x, attn_y = swap_x(attn_pair), swap_y(attn_pair)
         attn_corner = jnp.concatenate([swap_y(attn_x[:, :half]), swap_x(attn_y[:, half:])], axis=1)
         attn_whole = jnp.zeros((4 * chip_rows, 2 * half), BF)
         for k, piece in enumerate((attn_pair, attn_x, attn_y, attn_corner)):
             attn_whole = lax.dynamic_update_slice(attn_whole, piece, ((chip ^ k) * chip_rows, 0))
-        half = keep.shape[1] // 2
-        keep_x, keep_y = swap_x(keep), swap_y(keep)
-        got_x, got_y = swap_x(got), swap_y(got)
-        lefts = [swap_y(keep_x[:, :half]), swap_y(got_x[:, :half])]
-        rights = [swap_x(keep_y[:, half:]), swap_x(got_y[:, half:])]
-        offsets = jnp.stack([((chip ^ k) * 2 + (core ^ o)) for k in range(4) for o in range(2)]).astype(jnp.int32)
-        w_all = place(offsets, [keep, got, keep_x, got_x, keep_y, got_y], lefts, rights)
     else:
-        attn_whole = lax.all_gather(attn_pair, "gx", axis=0, tiled=True, axis_index_groups=core_groups(size))
-        pair = jnp.concatenate(core_order(keep, got), axis=0)
-        w_all = lax.all_gather(pair, "gx", axis=0, tiled=True, axis_index_groups=core_groups(size))
+        attn_whole = lax.all_gather(attn_own, "gx", axis=0, tiled=True)
+    keep_d, keep_gu, give_d, give_gu = prepare(core_array, w_down, w_gate, w_up)
+    pair_d = jnp.concatenate(core_order(keep_d, swap_core(give_d)), axis=0)
+    pair_gu = jnp.concatenate(core_order(keep_gu, swap_core(give_gu)), axis=0)
+    w_down_all = lax.all_gather(pair_d, "gx", axis=0, tiled=True, axis_index_groups=core_groups(size))
+    w_gu_all = lax.all_gather(pair_gu, "gx", axis=0, tiled=True, axis_index_groups=core_groups(size))
     query_cols, pair_cols = w_query.shape[1], w_key.shape[1]
     qkv_cols = query_cols + 2 * pair_cols
     qkv_w = attn_whole[:, :qkv_cols]
     out_w = attn_whole[:, qkv_cols : qkv_cols + w_out.shape[1]]
     router_w = attn_whole[:, qkv_cols + w_out.shape[1] :]
 
-    joined = after(joined, keep, got)
-    token_full = joined[:length]
-    gain_full = joined[length : length + 2].astype(F32)
-    gain_one, gain_two = gain_full[0], gain_full[1]
-    cot_own = lax.all_gather(after(block_cotangent, joined), "gy", axis=1, tiled=True)
+    xf = joined[:length].astype(F32)
+    scale_one = lax.rsqrt(jnp.mean(xf * xf, axis=1, keepdims=True) + epsilon)
+    normed_one = (xf * scale_one * gains[0:1].astype(F32)).astype(BF)
+    cot_pieces = plane_pieces(after(block_cotangent, normed_one))
+    qkv_raw = dot(after(normed_one, pair_d, pair_gu), qkv_w)
+    mixed, q_rot, k_rot, v_rot, log_total = attend(qkv_raw, heads, groups)
+    attn_parts = spread(onward, mixed, out_w)
+    token_slice = tokens.astype(F32)
+    residual = token_slice + attn_parts[0].astype(F32)
+    for d in range(1, 4):
+        residual = residual + plane_shift(attn_parts[d], d).astype(F32)
+    res_pieces = plane_pieces(residual.astype(BF))
+
+    cot_own = lay_planes(before, after(tuple(cot_pieces), *attn_parts))
     cot_both = jnp.concatenate([cot_own, swap_core(cot_own)], axis=0)
-    down_raw = expert_draw(cot_both, w_all)
+    down_raw = expert_draw(cot_both, w_down_all)
 
     iota = lax.broadcasted_iota(jnp.int32, (2 * length, 128), 1)
     routes_both = jnp.concatenate([routes, swap_core(routes)], axis=0)
@@ -524,44 +615,26 @@
     for k in range(1, routes.shape[1]):
         member = member | (routes_both[:, k : k + 1] == iota)
 
-    xf = token_full.astype(F32)
-    scale_one = lax.rsqrt(jnp.mean(xf * xf, axis=1, keepdims=True) + epsilon)
-    normed_one = (xf * scale_one * gain_one).astype(BF)
-    qkv_raw = dot(normed_one, qkv_w)
-    mixed, q_rot, k_rot, v_rot, log_total = attend(qkv_raw, heads, groups)
-    whole_block = (length, heads * HD)
-    attn_parts = project([(mixed, whole_block, (0, 0), out_w, 0)], planes)
-    token_slice = tokens.astype(F32)
-    residual = token_slice + plane_scatter(attn_parts).astype(F32)
-    residual_own = lax.all_gather(residual.astype(BF), "gy", axis=1, tiled=True)
-    residual_both = jnp.concatenate([residual_own, swap_core(residual_own)], axis=0)
-
-    rf = residual_both.astype(F32)
-    scale_two = lax.rsqrt(jnp.mean(rf * rf, axis=1, keepdims=True) + epsilon)
-    normed_two = (rf * scale_two * gain_two).astype(BF)
+    normed_own, scale_own, residual_own = norm_planes(before, after(tuple(res_pieces), down_raw), gains)
+    normed_two = jnp.concatenate([normed_own, swap_core(normed_own)], axis=0)
+
     logits = jnp.where(member, dot(normed_two, router_w), masked)
     gate_exp = jnp.exp(logits - jnp.max(logits, axis=1, keepdims=True))
     gate_all = gate_exp / jnp.sum(gate_exp, axis=1, keepdims=True)
     gate_mine = pad_lanes(lax.dynamic_slice_in_dim(gate_all, core * mine_n, mine_n, 1))
-    grads, dsum = expert_forward(normed_two, w_all, down_raw, gate_mine, 2 * length, 256)
-
-    def back_half(i):
+    grads, dsum = expert_forward(normed_two, w_gu_all, down_raw, gate_mine, 2 * length, 256)
+
+    def back_half(i, grads):
         block = (1, length, span)
-        return project([(grads, block, (1, i, 0), w_all, 1), (grads, block, (2, i, 0), w_all, 2)], planes)
-
-    back_other = swap_core(back_half(1))
-    back_own = back_half(0)
+        return project([(grads, block, (1, i, 0), w_gu_all, 0), (grads, block, (2, i, 0), w_gu_all, 1)], planes)
+
+    dsum_planes = plane_sum(dsum[:, :mine_n].T)
+    back_other = back_half(1, grads)
+    back_own = back_half(0, after(grads, back_other))
+    back_other = swap_core(back_other)
+    back_own = after(back_own, dsum_planes)
     back_sum = (back_own.astype(F32) + back_other.astype(F32)).astype(BF)
     back_slice = plane_scatter(back_sum).astype(F32)
-
-    dsum_own, dsum_got = dsum[:length, :mine_n], swap_core(dsum[length:, :mine_n])
-    dsum_all = plane_sum(jnp.concatenate(core_order(dsum_own, dsum_got), axis=1).T).T
-    gate_own = gate_all[:length, :experts_n]
-    grad_picked = gate_own * (dsum_all - jnp.sum(gate_own * dsum_all, axis=1, keepdims=True))
-    grad_logits = grad_picked.astype(BF)
-    router_slice = lax.dynamic_slice_in_dim(router_w[:, :experts_n], plane * slice_cols, slice_cols, 0)
-    grad_normed_two = back_slice + dot(grad_logits, router_slice, ((1,), (1,)))
-    grad_h2_full = lax.all_gather(grad_normed_two.astype(BF), "gy", axis=1, tiled=True)
 
     if small_mesh:
         def terms(a, b, inputs):
@@ -572,13 +645,13 @@
         give_a, give_b = terms((1, 3), (2, 3), inputs)
         got_a, got_b = swap_x(give_a), swap_y(give_b)
         own_a, own_b = terms((0, 2), (0, 1), after(inputs, give_a, give_b))
-        moe_inputs = after((grads, w_all), own_a, own_b)
+        moe_inputs = after((grads, w_down_all), own_a, own_b)
         next_a = (own_a[chip_rows:].astype(F32) + got_a[chip_rows:].astype(F32)).astype(BF)
         next_b = (own_b[chip_rows:].astype(F32) + got_b[chip_rows:].astype(F32)).astype(BF)
         last_a, last_b = swap_y(next_a), swap_x(next_b)
         sum_a, sum_b = [own_a, got_a, last_a], [own_b, got_b, last_b]
     else:
-        moe_inputs = (grads, w_all)
+        moe_inputs = (grads, w_down_all)
         next_a = next_b = back_sum
 
         def whole_term(side, m):
@@ -596,13 +669,19 @@
 
         sum_a, sum_b = chips_sum(0), chips_sum(1)
 
+    dsum_got = swap_core(dsum_planes[:, length:])
+    dsum_all = jnp.concatenate(core_order(dsum_planes[:, :length], dsum_got), axis=0).T
+    gate_own = gate_all[:length, :experts_n]
+    grad_picked = gate_own * (dsum_all - jnp.sum(gate_own * dsum_all, axis=1, keepdims=True))
+    grad_logits = grad_picked.astype(BF)
+    router_slice = lax.dynamic_slice_in_dim(router_w[:, :experts_n], plane * slice_cols, slice_cols, 0)
+    grad_normed_two = back_slice + dot(grad_logits, router_slice, ((1,), (1,)))
+    grad_h2_full = lax.all_gather(grad_normed_two.astype(BF), "gy", axis=1, tiled=True)
+
     def partner_rows(parts):
         picked = [lax.dynamic_slice_in_dim(p, (1 - core) * rows_here, rows_here, 0).astype(F32) for p in parts]
         return swap_core(sum(picked).astype(BF))
 
-    down_grad, gate_grad, up_grad = finish(
-        core_array, sum_a, sum_b, partner_rows(sum_a), partner_rows(sum_b), experts_n
-    )
 
     def moe_half(i):
         return project([(moe_inputs[0], (1, length, span), (0, i, 0), moe_inputs[1], 0)], planes)
@@ -612,8 +691,7 @@
     moe_slice = plane_scatter(after(moe_parts, grad_h2_full))
     block_out = (residual + moe_slice.astype(F32)).astype(BF)
 
-    grad_h2_full = after(grad_h2_full, moe_parts, next_a, next_b)
-    scale_own = scale_two[:length]
+    grad_h2_full = after(grad_h2_full, moe_parts)
     residual_f = residual_own.astype(F32)
     grad_h2_f = grad_h2_full.astype(F32)
     inner = jnp.sum(grad_h2_f * gain_two * residual_f, axis=1, keepdims=True)
@@ -631,9 +709,13 @@
     second_gain_grad = jnp.sum(grad_normed_two * residual * scale_own, axis=0)
 
     grad_mixed = dot(grad_res_full, out_w, out=BF)
-    grad_qkv = attend_back(q_rot, k_rot, v_rot, log_total, mixed, grad_mixed)
+    grad_qkv = after(attend_back(q_rot, k_rot, v_rot, log_total, mixed, grad_mixed), next_a, next_b)
     dh_parts = project([(grad_qkv, (length, qkv_cols), (0, 0), qkv_w, 0)], planes)
-    grad_normed_one = plane_scatter(dh_parts).astype(F32)
+    grad_normed_one = plane_scatter(after(dh_parts, moe_slice)).astype(F32)
+    sum_a, sum_b = after((sum_a, sum_b), dh_parts)
+    down_grad, gate_grad, up_grad = finish(
+        core_array, sum_a, sum_b, partner_rows(sum_a), partner_rows(sum_b), experts_n
+    )
 
     left = after((grad_res_full, normed_one), dh_parts)
     attn_terms = jnp.concatenate(
@@ -650,14 +732,15 @@
 
     gain_one_slice = first_gain.astype(BF).astype(F32)
     scaled = grad_normed_one * gain_one_slice
-    inner_one = plane_sum(jnp.sum(scaled * token_slice, axis=1)[None, :])[0][:, None]
+    inner_one = jnp.sum(grad_qkv.astype(F32) * qkv_raw, axis=1)[None, :]
+    inner_one = plane_sum(after(inner_one, grad_normed_one))[0][:, None]
+    first_gain_grad = jnp.sum(grad_normed_one * token_slice * scale_one, axis=0)
+    first_gain_grad, second_gain_grad = lax.psum((first_gain_grad, second_gain_grad), "gx")
     input_grad = (
         grad_residual
         + scale_one * scaled
-        - token_slice * scale_one * scale_one * scale_one * inner_one / D
+        - token_slice * scale_one * scale_one * inner_one / D
     ).astype(BF)
-    first_gain_grad = jnp.sum(grad_normed_one * token_slice * scale_one, axis=0)
-    first_gain_grad, second_gain_grad = lax.psum((first_gain_grad, second_gain_grad), "gx")
     return (
         block_out,
         input_grad,

time: 931 us -> 764 us (0.82)
  waiting for transfers between devices: 407 us -> 239 us
  starting transfers between devices: 38.6 us -> 72.4 us
  other arithmetic: 81.3 us -> 70.7 us
  local copies, waits for them, and re-layouts: 53.1 us -> 42.9 us
    ppermute x0 -> x9, waiting for transfers between devices: none -> 113 us  [plane_shift(): return lax.ppermute(x, 'gy', [(i, (i + d) % size) for i in range(size)])]
    ppermute x10 -> x6, waiting for transfers between devices: 126 us -> 26.8 us  [swap_y(): return lax.ppermute(x, 'gx', flip(4, lax.axis_size('gx')))]
    all_gather x3, waiting for transfers between devices: 61.4 us -> 0.01 us  [the longest x1 0.01 us: shards(): lax.all_gather(jnp.concatenate([tokens, gain_rows], axis=0), 'gy', axis=1...]
    ppermute x6, waiting for transfers between devices: 43.8 us -> 2.53 us  [plane_sum(): lax.ppermute(x, 'gy', [(i, (i + d) % size) for i in range(size)])]
    reduce_scatter x4 -> x3, waiting for transfers between devices: 58.2 us -> 22.3 us  [plane_scatter(): return lax.psum_scatter(parts, 'gy', scatter_dimension=0, tiled=True)]
    ppermute x0 -> x9, starting transfers between devices: none -> 29.5 us  [plane_shift(): return lax.ppermute(x, 'gy', [(i, (i + d) % size) for i in range(size)])]
    all_gather x1, waiting for transfers between devices: 29.3 us -> 0.01 us  [shards(): lax.all_gather(grad_normed_two.astype(BF), 'gy', axis=1, tiled=True)]
    ppermute x10 -> x6, waiting for transfers between devices: 82 us -> 61.6 us  [swap_x(): return lax.ppermute(x, 'gx', flip(2, lax.axis_size('gx')))]
  transfers between devices with their start and end apart: 45 -> 46, of which waited for: 18 -> 18; matrix products, arithmetic and copies ran while one was open for 10% -> 14% of each run, Pallas kernels for 19% -> 28%
where the time goes in v3:
time: 764 us; the launch traced here: 757 us
  Pallas kernels  282 us (37%)
  waiting for transfers between devices  239 us (31%)
  starting transfers between devices  72.4 us (9%)
  other arithmetic  70.7 us (9%)
  local copies, waits for them, and re-layouts  42.9 us (6%)
  matrix products  21 us (3%)
  between operations  15.2 us (2%)
  blocking collectives  14 us (2%)
    ppermute x9, waiting for transfers between devices, plane_shift(): return lax.ppermute(x, 'gy', [(i, (i + d) % size) for i in range(size)])  113 us
    pallas_call x5, Pallas kernels, project(): pl.pallas_call(partial(project_body, n), grid=(parts // 2,), in_specs=[pl...  81.9 us
    pallas_call x2, Pallas kernels, expert_terms(): pl.pallas_call(partial(term_body, steps), grid_spec=pltpu.PrefetchScalarG...  67.1 us
    ppermute x6, waiting for transfers between devices, swap_x(): return lax.ppermute(x, 'gx', flip(2, lax.axis_size('gx')))  61.6 us
    pallas_call x1, Pallas kernels, expert_forward(): pl.pallas_call(partial(expert_body, rows, chunk), grid=(tokens // rows, s...  45.8 us
    ppermute x9, starting transfers between devices, plane_shift(): return lax.ppermute(x, 'gy', [(i, (i + d) % size) for i in range(size)])  29.5 us
    ppermute x6, waiting for transfers between devices, swap_y(): return lax.ppermute(x, 'gx', flip(4, lax.axis_size('gx')))  26.8 us
    ppermute x6, starting transfers between devices, plane_sum(): lax.ppermute(x, 'gy', [(i, (i + d) % size) for i in range(size)])  22.8 us
  transfers between devices with their start and end apart: 46, of which 18 were waited for; matrix products, arithmetic and copies ran while one was open for 14% of the time, Pallas kernels for 28%

profile of v3, /device:TPU:0, one launch (start us, length us, event | category | flops | bytes accessed | tf_op | source)
XLA Modules:
  0.0 757.1 jit_solution(16040663329605864024)
XLA Ops:
  43.9 17.6 %collective-permute-done.4 = bf16[384,1152]{1,0:T(8,128)(2,1)} collective-permute-done((bf16[384,1152]{1,0:T(8,128)(2,1)}, bf16[384,1152]{1,0:T(8,128)(2,1)}, u32[]{:S(2)}, u32[]{:S(2)}) %collective-permute-start.4) | collective-permute-done | bytes 884768 | tf_op jit(solution)/shard_map/ppermute | solution.py:376
  94.7 17.2 %shard_map.257 = (bf16[1024,384]{1,0:T(8,128)(2,1)S(1)}, bf16[6,1024,64]{2,1,0:T(8,128)(2,1)S(1)}, bf16[2,1024,64]{2,1,0:T(8,128)(2,1)S(1)}, bf16[2,1024,64]{2,1,0:T(8,128)(2,1)S(1)}, f32[1024,128]{1,0:T(8,128)S(1)}) custom-call(f32[1024,640]{1,0:T(8,128)S(1)} %fusion.54.qkv_ref, f32[1024,64]{1,0:T(8,128)S(1)} %copy-done.7, f32[1024,64]{1,0:T(8,128)S(1)} %copy-done.9), custom_call_target="tpu_custom_call" | custom-call | flops 16999999488 | bytes 42500000 | tf_op jit(solution)/shard_map/pallas_call | solution.py:85
  118.4 21.6 %collective-permute-done.14.refs_2_ = bf16[1024,384]{1,0:T(8,128)(2,1)} collective-permute-done((bf16[1024,384]{1,0:T(8,128)(2,1)}, bf16[1024,384]{1,0:T(8,128)(2,1)}, u32[]{:S(2)}, u32[]{:S(2)}) %collective-permute-start.14) | collective-permute-done | bytes 786464 | tf_op jit(solution)/shard_map/ppermute | solution.py:397
  144.0 18.4 %collective-permute-start.9 = (bf16[1024,384]{1,0:T(8,128)(2,1)}, bf16[1024,384]{1,0:T(8,128)(2,1)S(1)}, u32[]{:S(2)}, u32[]{:S(2)}) collective-permute-start(bf16[1024,384]{1,0:T(8,128)(2,1)} %get-tuple-element.79), channel_id=1, source_target_pairs={{0,3},{1,0},{2,1},{3,2},{4,7},{5,4},{6,5},{7,6},{8,11},{9,8},{10,9... | collective-permute-start | bytes 2359304 | tf_op jit(solution)/shard_map/ppermute | solution.py:397
  164.5 16.2 %collective-permute-done.9 = bf16[1024,384]{1,0:T(8,128)(2,1)S(1)} collective-permute-done((bf16[1024,384]{1,0:T(8,128)(2,1)}, bf16[1024,384]{1,0:T(8,128)(2,1)S(1)}, u32[]{:S(2)}, u32[]{:S(2)}) %collective-permute-start.9) | collective-permute-done | bytes 786464 | tf_op jit(solution)/shard_map/ppermute | solution.py:397
  180.7 50.8 %collective-permute-done.8 = bf16[1024,384]{1,0:T(8,128)(2,1)S(1)} collective-permute-done((bf16[1024,384]{1,0:T(8,128)(2,1)}, bf16[1024,384]{1,0:T(8,128)(2,1)S(1)}, u32[]{:S(2)}, u32[]{:S(2)}) %collective-permute-start.8) | collective-permute-done | bytes 786464 | tf_op jit(solution)/shard_map/ppermute | solution.py:397
  241.3 22.3 %shard_map.260.draw_ref = bf16[2048,2560]{1,0:T(8,128)(2,1)} custom-call(bf16[2048,1536]{1,0:T(8,128)(2,1)} %pad_maximum_fusion.c_ref.c0_ref.c1_ref, bf16[1536,2560]{1,0:T(8,128)(2,1)} %all-gather.7.cloned.1.call-done.w_ref.refs_1_), custom_call_target="tpu_custom_call" | custom-call | flops 22000001024 | bytes 55000000 | tf_op jit(solution)/shard_map/pallas_call | solution.py:416
  263.6 24.8 %collective-permute-done.11.refs_2_ = bf16[1024,384]{1,0:T(8,128)(2,1)S(1)} collective-permute-done((bf16[1024,384]{1,0:T(8,128)(2,1)}, bf16[1024,384]{1,0:T(8,128)(2,1)S(1)}, u32[]{:S(2)}, u32[]{:S(2)}) %collective-permute-start.11) | collective-permute-done | bytes 786464 | tf_op jit(solution)/shard_map/ppermute | solution.py:397
  289.4 6.7 shard_map.261
  315.5 45.8 %shard_map.262 = (bf16[3,2048,2560]{2,1,0:T(8,128)(2,1)}, f32[2048,128]{1,0:T(8,128)}) custom-call(bf16[2048,1536]{1,0:T(8,128)(2,1)} %copy-done.32, bf16[1536,5120]{1,0:T(8,128)(2,1)} %all-gather.9.cloned.1.call-done.wg_ref.wu_ref.refs_2_.refs_3_, bf16[1536,5120]{1,0:T(8,128)(2,1)} %all-gather.9.cloned.1.call-done.wg_ref.wu_ref.refs_2_.refs_3_, ...), custom_call_target="tpu_custom_call" | custom-call | flops 46000001024 | bytes 115000000 | tf_op jit(solution)/shard_map/pallas_call | solution.py:197
  361.3 24.5 %shard_map.263 = bf16[4,1024,384]{2,1,0:T(8,128)(2,1)} custom-call(bf16[3,2048,2560]{2,1,0:T(8,128)(2,1)} %get-tuple-element.104.refs_0_.refs_1_.g_ref, bf16[3,2048,2560]{2,1,0:T(8,128)(2,1)} %get-tuple-element.104.refs_0_.refs_1_.g_ref, bf16[1536,5120]{1,0:T(8,128)(2,1)} %all-gather.9.cloned.1.call-done.wg_ref.wu_ref.refs_2_.refs_3_, ...), custom_call_target="tpu_custom_call" | custom-call | flops 25008752640 | bytes 62521884 | tf_op jit(solution)/shard_map/pallas_call | solution.py:235
  386.6 17.5 %collective-permute-start.21 = (f32[20,2048]{1,0:T(8,128)S(1)}, f32[20,2048]{1,0:T(8,128)S(1)}, u32[]{:S(2)}, u32[]{:S(2)}) collective-permute-start(f32[20,2048]{1,0:T(8,128)S(1)} %copy.77), channel_id=1, source_target_pairs={{0,3},{1,0},{2,1},{3,2},{4,7},{5,4},{6,5},{7,6},{8,11},{9,8},{10,9... | collective-permute-start | bytes 491528 | tf_op jit(solution)/shard_map/ppermute | solution.py:391
  404.8 24.1 %shard_map.264 = bf16[4,1024,384]{2,1,0:T(8,128)(2,1)} custom-call(bf16[3,2048,2560]{2,1,0:T(8,128)(2,1)} %get-tuple-element.104.refs_0_.refs_1_.g_ref, bf16[3,2048,2560]{2,1,0:T(8,128)(2,1)} %get-tuple-element.104.refs_0_.refs_1_.g_ref, bf16[1536,5120]{1,0:T(8,128)(2,1)} %all-gather.9.cloned.1.call-done.wg_ref.wu_ref.refs_2_.refs_3_, ...), custom_call_target="tpu_custom_call" | custom-call | flops 25008752640 | bytes 62521884 | tf_op jit(solution)/shard_map/pallas_call | solution.py:235
  440.5 33.6 %shard_map.265 = (bf16[768,3840]{1,0:T(8,128)(2,1)}, bf16[768,3840]{1,0:T(8,128)(2,1)}) custom-call(s32[4]{0:T(128)} %get-tuple-element.235.ids_ref, bf16[2048,1536]{1,0:T(8,128)(2,1)} %pad_maximum_fusion.c_ref.c0_ref.c1_ref, bf16[2048,1536]{1,0:T(8,128)(2,1)} %pad_maximum_fusion.c_ref.c0_ref.c1_ref, bf16[2048,1536]{1,0:T(8,128)(2,1)} %copy-done.32, ...), custom_call_target="tpu_custom_call" | custom-call | flops 33999998976 | bytes 85000000 | tf_op jit(solution)/shard_map/pallas_call | solution.py:272
  476.3 33.5 %shard_map.266 = (bf16[768,3840]{1,0:T(8,128)(2,1)}, bf16[768,3840]{1,0:T(8,128)(2,1)}) custom-call(s32[4]{0:T(128)} %get-tuple-element.234.ids_ref, bf16[2048,1536]{1,0:T(8,128)(2,1)} %pad_maximum_fusion.c_ref.c0_ref.c1_ref, bf16[2048,1536]{1,0:T(8,128)(2,1)} %pad_maximum_fusion.c_ref.c0_ref.c1_ref, bf16[2048,1536]{1,0:T(8,128)(2,1)} %copy-done.32, ...), custom_call_target="tpu_custom_call" | custom-call | flops 33999998976 | bytes 85000000 | tf_op jit(solution)/shard_map/pallas_call | solution.py:272
  509.8 13.8 %shard_map.268 = bf16[4,1024,384]{2,1,0:T(8,128)(2,1)} custom-call(bf16[3,2048,2560]{2,1,0:T(8,128)(2,1)} %get-tuple-element.104.refs_0_.refs_1_.g_ref, bf16[1536,2560]{1,0:T(8,128)(2,1)} %all-gather.7.cloned.1.call-done.w_ref.refs_1_), custom_call_target="tpu_custom_call" | custom-call | flops 13504376832 | bytes 33760940 | tf_op jit(solution)/shard_map/pallas_call | solution.py:235
  531.3 13.7 %shard_map.267 = bf16[4,1024,384]{2,1,0:T(8,128)(2,1)} custom-call(bf16[3,2048,2560]{2,1,0:T(8,128)(2,1)} %get-tuple-element.104.refs_0_.refs_1_.g_ref, bf16[1536,2560]{1,0:T(8,128)(2,1)} %all-gather.7.cloned.1.call-done.w_ref.refs_1_), custom_call_target="tpu_custom_call" | custom-call | flops 13504376832 | bytes 33760940 | tf_op jit(solution)/shard_map/pallas_call | solution.py:235
  551.3 51.9 %collective-permute-done.25.refs_1_ = bf16[768,3840]{1,0:T(8,128)(2,1)} collective-permute-done((bf16[768,3840]{1,0:T(8,128)(2,1)}, bf16[768,3840]{1,0:T(8,128)(2,1)}, u32[]{:S(2)}, u32[]{:S(2)}) %collective-permute-start.25) | collective-permute-done | bytes 5898272 | tf_op jit(solution)/shard_map/ppermute | solution.py:372
  624.7 19.1 %shard_map.269.refs_0_ = bf16[1024,640]{1,0:T(8,128)(2,1)S(1)} custom-call(bf16[6,1024,64]{2,1,0:T(8,128)(2,1)} %copy-done.13, bf16[2,1024,64]{2,1,0:T(8,128)(2,1)S(1)} %get-tuple-element.111.k_ref, bf16[2,1024,64]{2,1,0:T(8,128)(2,1)S(1)} %get-tuple-element.112.v_ref, f32[1024,128]{1,0:T(8,128)S(1)} %get-tuple-element.113.log_ref, ...), custom_call_target="tpu_custom_call" | custom-call | flops 19000000512 | bytes 47500000 | tf_op jit(solution)/shard_map/pallas_call | solution.py:144
  660.5 8.6 %reduce-scatter.6.cloned.1.call-done = bf16[1024,384]{1,0:T(8,128)(2,1)} async-done(((bf16[4096,384]{1,0:T(8,128)(2,1)}), bf16[1024,384]{1,0:T(8,128)(2,1)}) %reduce-scatter.6.cloned.1.call-update) | async-done | bytes 786448 | tf_op jit(solution)/shard_map/reduce_scatter | solution.py:405
  694.6 6.9 collective-permute-done.33
  706.4 8.3 %shard_map.271 = (f32[192,40,128]{2,1,0:T(8,128)}, f32[192,40,128]{2,1,0:T(8,128)}, f32[192,40,128]{2,1,0:T(8,128)}) custom-call(s32[1]{0:T(128)} %bitcast.4.core_ref, bf16[768,3840]{1,0:T(8,128)(2,1)} %get-tuple-element.119.refs_0_, bf16[768,3840]{1,0:T(8,128)(2,1)} %collective-permute-done.25.refs_1_, bf16[384,3840]{1,0:T(8,128)(2,1)} %collective-permute-done.35.refs_2_, ...), custom_call_target="tpu_custom_call" | custom-call | flops 8999999488 | bytes 22500000 | tf_op jit(solution)/shard_map/pallas_call | solution.py:349
  718.1 13.7 %reduce-scatter.8.cloned.1.call-done = bf16[1024,384]{1,0:T(8,128)(2,1)} async-done(((bf16[4096,384]{1,0:T(8,128)(2,1)}), bf16[1024,384]{1,0:T(8,128)(2,1)}) %reduce-scatter.8.cloned.1.call-update) | async-done | bytes 786448 | tf_op jit(solution)/shard_map/reduce_scatter | solution.py:405
  736.1 14.0 %all-reduce.4 = (f32[384]{0:T(512)}, f32[384]{0:T(512)}) all-reduce(f32[384]{0:T(512)S(1)} %get-tuple-element.208, f32[384]{0:T(512)S(1)} %get-tuple-element.198), channel_id=1, replica_groups=mesh['gx'=8,'gy'=4] {'gx'}, use_global_device_ids=true, to_apply=%region_10.11 | all-reduce | flops 768 | bytes 6144 | tf_op jit(solution)/shard_map/psum | solution.py:738
  (285 shorter events, 217.4 us)
Async XLA Ops:
  7.2 72.3 %all-gather.5.cloned.1.call-start = ((), (), s32[]{:S(2)}) async-start(), calls=%async_computation.3 | async-start | bytes 3993600 | tf_op jit(solution)/shard_map/all_gather | solution.py:566
  10.7 230.6 %all-gather.7.cloned.1.call-start = ((), (), s32[]{:S(2)}) async-start(), calls=%async_computation.4 | async-start | bytes 9830400 | tf_op jit(solution)/shard_map/all_gather | solution.py:587
  27.1 288.3 %all-gather.9.cloned.1.call-start = ((), (), s32[]{:S(2)}) async-start(), calls=%async_computation.5 | async-start | bytes 19660800 | tf_op jit(solution)/shard_map/all_gather | solution.py:588
  33.9 491.0 %reduce-scatter.4.cloned.1.call-start = ((), (), s32[]{:S(2)}) async-start(), calls=%async_computation.6 | async-start | bytes 3932160 | tf_op jit(solution)/shard_map/reduce_scatter | solution.py:405
  86.3 32.0 %collective-permute-start.13 = (bf16[1024,384]{1,0:T(8,128)(2,1)}, bf16[1024,384]{1,0:T(8,128)(2,1)}, u32[]{:S(2)}, u32[]{:S(2)}) collective-permute-start(bf16[1024,384]{1,0:T(8,128)(2,1)} %refs_0_), channel_id=1, source_target_pairs={{0,1},{1,2},{2,3},{3,0},{4,5},{5,6},{6,7},{7,4},{8,9},{9,10},{10,1... | collective-permute-start | bytes 2359304 | tf_op jit(solution)/shard_map/ppermute | solution.py:397
  87.9 52.1 %collective-permute-start.14 = (bf16[1024,384]{1,0:T(8,128)(2,1)}, bf16[1024,384]{1,0:T(8,128)(2,1)}, u32[]{:S(2)}, u32[]{:S(2)}) collective-permute-start(bf16[1024,384]{1,0:T(8,128)(2,1)} %refs_0_), channel_id=1, source_target_pairs={{0,2},{1,3},{2,0},{3,1},{4,6},{5,7},{6,4},{7,5},{8,10},{9,11},{10,... | collective-permute-start | bytes 2359304 | tf_op jit(solution)/shard_map/ppermute | solution.py:397
  90.6 49.3 %collective-permute-start.15 = (bf16[1024,384]{1,0:T(8,128)(2,1)}, bf16[1024,384]{1,0:T(8,128)(2,1)}, u32[]{:S(2)}, u32[]{:S(2)}) collective-permute-start(bf16[1024,384]{1,0:T(8,128)(2,1)} %refs_0_), channel_id=1, source_target_pairs={{0,3},{1,0},{2,1},{3,2},{4,7},{5,4},{6,5},{7,6},{8,11},{9,8},{10,9... | collective-permute-start | bytes 2359304 | tf_op jit(solution)/shard_map/ppermute | solution.py:397
  144.0 94.2 %collective-permute-start.16 = (bf16[1024,1536]{1,0:T(8,128)(2,1)}, bf16[1024,1536]{1,0:T(8,128)(2,1)S(1)}, u32[]{:S(2)}, u32[]{:S(2)}) collective-permute-start(bf16[1024,1536]{1,0:T(8,128)(2,1)} %shard_map.259), channel_id=1, source_target_pairs={{0,4},{4,0},{8,12},{12,8},{16,20},{20,16},{24,28},{28,24},{1,5},{5... | collective-permute-start | bytes 9437192 | tf_op jit(solution)/shard_map/ppermute | solution.py:368
  144.0 36.7 %collective-permute-start.9 = (bf16[1024,384]{1,0:T(8,128)(2,1)}, bf16[1024,384]{1,0:T(8,128)(2,1)S(1)}, u32[]{:S(2)}, u32[]{:S(2)}) collective-permute-start(bf16[1024,384]{1,0:T(8,128)(2,1)} %get-tuple-element.79), channel_id=1, source_target_pairs={{0,3},{1,0},{2,1},{3,2},{4,7},{5,4},{6,5},{7,6},{8,11},{9,8},{10,9... | collective-permute-start | bytes 2359304 | tf_op jit(solution)/shard_map/ppermute | solution.py:397
  162.4 69.1 %collective-permute-start.8 = (bf16[1024,384]{1,0:T(8,128)(2,1)}, bf16[1024,384]{1,0:T(8,128)(2,1)S(1)}, u32[]{:S(2)}, u32[]{:S(2)}) collective-permute-start(bf16[1024,384]{1,0:T(8,128)(2,1)} %get-tuple-element.78), channel_id=1, source_target_pairs={{0,2},{1,3},{2,0},{3,1},{4,6},{5,7},{6,4},{7,5},{8,10},{9,11},{10,... | collective-permute-start | bytes 2359304 | tf_op jit(solution)/shard_map/ppermute | solution.py:397
  162.8 68.7 %collective-permute-start.7 = (bf16[1024,384]{1,0:T(8,128)(2,1)}, bf16[1024,384]{1,0:T(8,128)(2,1)S(1)}, u32[]{:S(2)}, u32[]{:S(2)}) collective-permute-start(bf16[1024,384]{1,0:T(8,128)(2,1)} %get-tuple-element.77), channel_id=1, source_target_pairs={{0,1},{1,2},{2,3},{3,0},{4,5},{5,6},{6,7},{7,4},{8,9},{9,10},{10,1... | collective-permute-start | bytes 2359304 | tf_op jit(solution)/shard_map/ppermute | solution.py:397
  233.4 30.2 %collective-permute-start.10 = (bf16[1024,384]{1,0:T(8,128)(2,1)}, bf16[1024,384]{1,0:T(8,128)(2,1)S(1)}, u32[]{:S(2)}, u32[]{:S(2)}) collective-permute-start(bf16[1024,384]{1,0:T(8,128)(2,1)} %get-tuple-element.85.refs_0_), channel_id=1, source_target_pairs={{0,1},{1,2},{2,3},{3,0},{4,5},{5,6},{6,7},{7,4},{8,9},{9,10},{10,1... | collective-permute-start | bytes 2359304 | tf_op jit(solution)/shard_map/ppermute | solution.py:397
  233.4 55.0 %collective-permute-start.11 = (bf16[1024,384]{1,0:T(8,128)(2,1)}, bf16[1024,384]{1,0:T(8,128)(2,1)S(1)}, u32[]{:S(2)}, u32[]{:S(2)}) collective-permute-start(bf16[1024,384]{1,0:T(8,128)(2,1)} %get-tuple-element.85.refs_0_), channel_id=1, source_target_pairs={{0,2},{1,3},{2,0},{3,1},{4,6},{5,7},{6,4},{7,5},{8,10},{9,11},{10,... | collective-permute-start | bytes 2359304 | tf_op jit(solution)/shard_map/ppermute | solution.py:397
  235.1 53.4 %collective-permute-start.12 = (bf16[1024,384]{1,0:T(8,128)(2,1)}, bf16[1024,384]{1,0:T(8,128)(2,1)}, u32[]{:S(2)}, u32[]{:S(2)}) collective-permute-start(bf16[1024,384]{1,0:T(8,128)(2,1)} %get-tuple-element.85.refs_0_), channel_id=1, source_target_pairs={{0,3},{1,0},{2,1},{3,2},{4,7},{5,4},{6,5},{7,6},{8,11},{9,8},{10,9... | collective-permute-start | bytes 2359304 | tf_op jit(solution)/shard_map/ppermute | solution.py:397
  385.8 49.7 %collective-permute-start.23 = (bf16[4096,384]{1,0:T(8,128)(2,1)}, bf16[4096,384]{1,0:T(8,128)(2,1)}, u32[]{:S(2)}, u32[]{:S(2)}) collective-permute-start(bf16[4096,384]{1,0:T(8,128)(2,1)} %bitcast.98), channel_id=1, source_target_pairs={{0,4},{4,0},{8,12},{12,8},{16,20},{20,16},{24,28},{28,24},{1,5},{5... | collective-permute-start | bytes 9437192 | tf_op jit(solution)/shard_map/ppermute | solution.py:368
  386.6 42.3 %collective-permute-start.21 = (f32[20,2048]{1,0:T(8,128)S(1)}, f32[20,2048]{1,0:T(8,128)S(1)}, u32[]{:S(2)}, u32[]{:S(2)}) collective-permute-start(f32[20,2048]{1,0:T(8,128)S(1)} %copy.77), channel_id=1, source_target_pairs={{0,3},{1,0},{2,1},{3,2},{4,7},{5,4},{6,5},{7,6},{8,11},{9,8},{10,9... | collective-permute-start | bytes 491528 | tf_op jit(solution)/shard_map/ppermute | solution.py:391
  440.5 169.1 %all-gather.11.cloned.1.call-start = ((), (), s32[]{:S(2)}) async-start(), calls=%async_computation.7 | async-start | bytes 3932160 | tf_op jit(solution)/shard_map/all_gather | solution.py:679
  474.2 129.0 %collective-permute-start.25 = (bf16[768,3840]{1,0:T(8,128)(2,1)}, bf16[768,3840]{1,0:T(8,128)(2,1)}, u32[]{:S(2)}, u32[]{:S(2)}) collective-permute-start(bf16[768,3840]{1,0:T(8,128)(2,1)} %get-tuple-element.97), channel_id=1, source_target_pairs={{0,8},{4,12},{8,0},{12,4},{16,24},{20,28},{24,16},{28,20},{1,9},{5... | collective-permute-start | bytes 17694728 | tf_op jit(solution)/shard_map/ppermute | solution.py:372
  474.8 134.9 %collective-permute-start.26 = (bf16[768,3840]{1,0:T(8,128)(2,1)}, bf16[768,3840]{1,0:T(8,128)(2,1)}, u32[]{:S(2)}, u32[]{:S(2)}) collective-permute-start(bf16[768,3840]{1,0:T(8,128)(2,1)} %get-tuple-element.98), channel_id=1, source_target_pairs={{0,16},{4,20},{8,24},{12,28},{16,0},{20,4},{24,8},{28,12},{1,17},{... | collective-permute-start | bytes 17694728 | tf_op jit(solution)/shard_map/ppermute | solution.py:376
  476.3 47.9 %collective-permute-start.24 = (f32[20,1024]{0,1:T(8,128)S(1)}, f32[20,1024]{0,1:T(8,128)S(1)}, u32[]{:S(2)}, u32[]{:S(2)}) collective-permute-start(f32[20,1024]{0,1:T(8,128)S(1)} %slice.205), channel_id=1, source_target_pairs={{0,4},{4,0},{8,12},{12,8},{16,20},{20,16},{24,28},{28,24},{1,5},{5... | collective-permute-start | bytes 245768 | tf_op jit(solution)/shard_map/ppermute | solution.py:368
  528.0 141.1 %reduce-scatter.6.cloned.1.call-start = ((), (), s32[]{:S(2)}) async-start(), calls=%async_computation.8 | async-start | bytes 3932160 | tf_op jit(solution)/shard_map/reduce_scatter | solution.py:405
  608.2 68.7 %collective-permute-start.35 = (bf16[384,3840]{1,0:T(8,128)(2,1)}, bf16[384,3840]{1,0:T(8,128)(2,1)}, u32[]{:S(2)}, u32[]{:S(2)}) collective-permute-start(bf16[384,3840]{1,0:T(8,128)(2,1)} %add_convert_fusion.2), channel_id=1, source_target_pairs={{0,16},{4,20},{8,24},{12,28},{16,0},{20,4},{24,8},{28,12},{1,17},{... | collective-permute-start | bytes 8847368 | tf_op jit(solution)/shard_map/ppermute | solution.py:376
  609.6 122.1 %reduce-scatter.8.cloned.1.call-start = ((), (), s32[]{:S(2)}) async-start(), calls=%async_computation.9 | async-start | bytes 3932160 | tf_op jit(solution)/shard_map/reduce_scatter | solution.py:405
  614.9 64.4 %collective-permute-start.36 = (bf16[384,3840]{1,0:T(8,128)(2,1)}, bf16[384,3840]{1,0:T(8,128)(2,1)}, u32[]{:S(2)}, u32[]{:S(2)}) collective-permute-start(bf16[384,3840]{1,0:T(8,128)(2,1)} %add_convert_fusion.1), channel_id=1, source_target_pairs={{0,8},{4,12},{8,0},{12,4},{16,24},{20,28},{24,16},{28,20},{1,9},{5... | collective-permute-start | bytes 8847368 | tf_op jit(solution)/shard_map/ppermute | solution.py:372
  (71 other events, 904.0 us)
Sparse Core Ops, SparseCore 0:
  10.8 66.8 all-gather.4
  80.2 81.8 all-gather.6
  164.5 148.6 all-gather.8
  440.6 60.2 reduce-scatter.3
  528.1 63.1 all-gather.10
  609.8 59.3 reduce-scatter.5
  671.4 60.3 reduce-scatter.7

commit v4 on v3

--- a/solution.py
+++ b/solution.py
@@ -21,7 +21,7 @@
 
 
 def lasts(us):
-    return pl.CostEstimate(flops=int(us * 1e9), bytes_accessed=int(us * 2.5e6), transcendentals=0)
+    return pl.CostEstimate(flops=int(us * 0.45e9), bytes_accessed=int(us * 1.1e6), transcendentals=0)
 
 
 def rope_tables(length):

time: 764 us -> 751 us (0.983)
  waiting for transfers between devices: 239 us -> 214 us
    ppermute x6, waiting for transfers between devices: 61.6 us -> 29.3 us  [swap_x(): return lax.ppermute(x, 'gx', flip(2, lax.axis_size('gx')))]
    all_gather x1, waiting for transfers between devices: 0.01 us -> 29 us  [shards(): lax.all_gather(grad_normed_two.astype(BF), 'gy', axis=1, tiled=True)]
    reduce_scatter x3, waiting for transfers between devices: 22.3 us -> 0.61 us  [plane_scatter(): return lax.psum_scatter(parts, 'gy', scatter_dimension=0, tiled=True)]
    unnamed x101 -> x113, local copies, waits for them, and re-layouts: 16.3 us -> 17.3 us
  transfers between devices with their start and end apart: 46 -> 46, of which waited for: 18 -> 18; matrix products, arithmetic and copies ran while one was open for 14% -> 16% of each run, Pallas kernels for 28% -> 28%
where the time goes in v4:
time: 751 us; the launch traced here: 745 us
  Pallas kernels  283 us (38%)
  waiting for transfers between devices  214 us (28%)
  other arithmetic  74.2 us (10%)
  starting transfers between devices  73.7 us (10%)
  local copies, waits for them, and re-layouts  45.9 us (6%)
  matrix products  25.6 us (3%)
  between operations  15.2 us (2%)
  blocking collectives  14 us (2%)
    ppermute x9, waiting for transfers between devices, plane_shift(): return lax.ppermute(x, 'gy', [(i, (i + d) % size) for i in range(size)])  112 us
    pallas_call x5, Pallas kernels, project(): pl.pallas_call(partial(project_body, n), grid=(parts // 2,), in_specs=[pl...  81.8 us
    pallas_call x2, Pallas kernels, expert_terms(): pl.pallas_call(partial(term_body, steps), grid_spec=pltpu.PrefetchScalarG...  68 us
    pallas_call x1, Pallas kernels, expert_forward(): pl.pallas_call(partial(expert_body, rows, chunk), grid=(tokens // rows, s...  46 us
    ppermute x9, starting transfers between devices, plane_shift(): return lax.ppermute(x, 'gy', [(i, (i + d) % size) for i in range(size)])  29.5 us
    ppermute x6, waiting for transfers between devices, swap_x(): return lax.ppermute(x, 'gx', flip(2, lax.axis_size('gx')))  29.3 us
    all_gather x1, waiting for transfers between devices, shards(): lax.all_gather(grad_normed_two.astype(BF), 'gy', axis=1, tiled=True)  29 us
    ppermute x6, waiting for transfers between devices, swap_y(): return lax.ppermute(x, 'gx', flip(4, lax.axis_size('gx')))  26.7 us
  transfers between devices with their start and end apart: 46, of which 18 were waited for; matrix products, arithmetic and copies ran while one was open for 16% of the time, Pallas kernels for 28%

profile of v4, /device:TPU:0, one launch (start us, length us, event | category | flops | bytes accessed | tf_op | source)
XLA Modules:
  0.0 744.9 jit_solution(8371137914959675421)
XLA Ops:
  43.9 17.6 %collective-permute-done.4 = bf16[384,1152]{1,0:T(8,128)(2,1)} collective-permute-done((bf16[384,1152]{1,0:T(8,128)(2,1)}, bf16[384,1152]{1,0:T(8,128)(2,1)}, u32[]{:S(2)}, u32[]{:S(2)}) %collective-permute-start.4) | collective-permute-done | bytes 884768 | tf_op jit(solution)/shard_map/ppermute | solution.py:376
  94.7 17.2 %shard_map.257 = (bf16[1024,384]{1,0:T(8,128)(2,1)S(1)}, bf16[6,1024,64]{2,1,0:T(8,128)(2,1)S(1)}, bf16[2,1024,64]{2,1,0:T(8,128)(2,1)S(1)}, bf16[2,1024,64]{2,1,0:T(8,128)(2,1)S(1)}, f32[1024,128]{1,0:T(8,128)S(1)}) custom-call(f32[1024,640]{1,0:T(8,128)S(1)} %fusion.54.qkv_ref, f32[1024,64]{1,0:T(8,128)S(1)} %copy-done.6, f32[1024,64]{1,0:T(8,128)S(1)} %copy-done.8), custom_call_target="tpu_custom_call" | custom-call | flops 7649999872 | bytes 18700000 | tf_op jit(solution)/shard_map/pallas_call | solution.py:85
  120.0 20.0 %collective-permute-done.14.refs_2_ = bf16[1024,384]{1,0:T(8,128)(2,1)} collective-permute-done((bf16[1024,384]{1,0:T(8,128)(2,1)}, bf16[1024,384]{1,0:T(8,128)(2,1)}, u32[]{:S(2)}, u32[]{:S(2)}) %collective-permute-start.14) | collective-permute-done | bytes 786464 | tf_op jit(solution)/shard_map/ppermute | solution.py:397
  144.0 18.4 %collective-permute-start.9 = (bf16[1024,384]{1,0:T(8,128)(2,1)}, bf16[1024,384]{1,0:T(8,128)(2,1)S(1)}, u32[]{:S(2)}, u32[]{:S(2)}) collective-permute-start(bf16[1024,384]{1,0:T(8,128)(2,1)} %get-tuple-element.79), channel_id=1, source_target_pairs={{0,3},{1,0},{2,1},{3,2},{4,7},{5,4},{6,5},{7,6},{8,11},{9,8},{10,9... | collective-permute-start | bytes 2359304 | tf_op jit(solution)/shard_map/ppermute | solution.py:397
  164.5 16.2 %collective-permute-done.9 = bf16[1024,384]{1,0:T(8,128)(2,1)S(1)} collective-permute-done((bf16[1024,384]{1,0:T(8,128)(2,1)}, bf16[1024,384]{1,0:T(8,128)(2,1)S(1)}, u32[]{:S(2)}, u32[]{:S(2)}) %collective-permute-start.9) | collective-permute-done | bytes 786464 | tf_op jit(solution)/shard_map/ppermute | solution.py:397
  180.7 50.8 %collective-permute-done.8 = bf16[1024,384]{1,0:T(8,128)(2,1)S(1)} collective-permute-done((bf16[1024,384]{1,0:T(8,128)(2,1)}, bf16[1024,384]{1,0:T(8,128)(2,1)S(1)}, u32[]{:S(2)}, u32[]{:S(2)}) %collective-permute-start.8) | collective-permute-done | bytes 786464 | tf_op jit(solution)/shard_map/ppermute | solution.py:397
  241.1 22.3 %shard_map.260.draw_ref = bf16[2048,2560]{1,0:T(8,128)(2,1)} custom-call(bf16[2048,1536]{1,0:T(8,128)(2,1)} %pad_maximum_fusion.c_ref.c0_ref.c1_ref, bf16[1536,2560]{1,0:T(8,128)(2,1)} %all-gather.7.cloned.1.call-done.w_ref.refs_1_), custom_call_target="tpu_custom_call" | custom-call | flops 9900000256 | bytes 24200000 | tf_op jit(solution)/shard_map/pallas_call | solution.py:416
  263.4 24.6 %collective-permute-done.11.refs_2_ = bf16[1024,384]{1,0:T(8,128)(2,1)S(1)} collective-permute-done((bf16[1024,384]{1,0:T(8,128)(2,1)S(1)}, bf16[1024,384]{1,0:T(8,128)(2,1)S(1)}, u32[]{:S(2)}, u32[]{:S(2)}) %collective-permute-start.11) | collective-permute-done | bytes 786464 | tf_op jit(solution)/shard_map/ppermute | solution.py:397
  289.0 6.7 shard_map.261
  313.2 46.0 %shard_map.262 = (bf16[3,2048,2560]{2,1,0:T(8,128)(2,1)}, f32[2048,128]{1,0:T(8,128)}) custom-call(bf16[2048,1536]{1,0:T(8,128)(2,1)} %copy-done.17, bf16[1536,5120]{1,0:T(8,128)(2,1)} %all-gather.9.cloned.1.call-done.wg_ref.wu_ref.refs_2_.refs_3_, bf16[1536,5120]{1,0:T(8,128)(2,1)} %all-gather.9.cloned.1.call-done.wg_ref.wu_ref.refs_2_.refs_3_, ...), custom_call_target="tpu_custom_call" | custom-call | flops 20700000256 | bytes 50600000 | tf_op jit(solution)/shard_map/pallas_call | solution.py:197
  359.2 24.5 %shard_map.263 = bf16[4,1024,384]{2,1,0:T(8,128)(2,1)} custom-call(bf16[3,2048,2560]{2,1,0:T(8,128)(2,1)} %get-tuple-element.104.refs_0_.refs_1_.g_ref, bf16[3,2048,2560]{2,1,0:T(8,128)(2,1)} %get-tuple-element.104.refs_0_.refs_1_.g_ref, bf16[1536,5120]{1,0:T(8,128)(2,1)} %all-gather.9.cloned.1.call-done.wg_ref.wu_ref.refs_2_.refs_3_, ...), custom_call_target="tpu_custom_call" | custom-call | flops 11253939200 | bytes 27509628 | tf_op jit(solution)/shard_map/pallas_call | solution.py:235
  386.3 16.9 %collective-permute-start.21 = (f32[20,2048]{1,0:T(8,128)S(1)}, f32[20,2048]{1,0:T(8,128)S(1)}, u32[]{:S(2)}, u32[]{:S(2)}) collective-permute-start(f32[20,2048]{1,0:T(8,128)S(1)} %copy.77), channel_id=1, source_target_pairs={{0,3},{1,0},{2,1},{3,2},{4,7},{5,4},{6,5},{7,6},{8,11},{9,8},{10,9... | collective-permute-start | bytes 491528 | tf_op jit(solution)/shard_map/ppermute | solution.py:391
  403.8 24.1 %shard_map.264 = bf16[4,1024,384]{2,1,0:T(8,128)(2,1)} custom-call(bf16[3,2048,2560]{2,1,0:T(8,128)(2,1)} %get-tuple-element.104.refs_0_.refs_1_.g_ref, bf16[3,2048,2560]{2,1,0:T(8,128)(2,1)} %get-tuple-element.104.refs_0_.refs_1_.g_ref, bf16[1536,5120]{1,0:T(8,128)(2,1)} %all-gather.9.cloned.1.call-done.wg_ref.wu_ref.refs_2_.refs_3_, ...), custom_call_target="tpu_custom_call" | custom-call | flops 11253939200 | bytes 27509628 | tf_op jit(solution)/shard_map/pallas_call | solution.py:235
  441.3 34.2 %shard_map.265 = (bf16[768,3840]{1,0:T(8,128)(2,1)}, bf16[768,3840]{1,0:T(8,128)(2,1)}) custom-call(s32[4]{0:T(128)} %get-tuple-element.235.ids_ref, bf16[2048,1536]{1,0:T(8,128)(2,1)} %pad_maximum_fusion.c_ref.c0_ref.c1_ref, bf16[2048,1536]{1,0:T(8,128)(2,1)} %pad_maximum_fusion.c_ref.c0_ref.c1_ref, bf16[2048,1536]{1,0:T(8,128)(2,1)} %copy-done.17, ...), custom_call_target="tpu_custom_call" | custom-call | flops 15299999744 | bytes 37400000 | tf_op jit(solution)/shard_map/pallas_call | solution.py:272
  476.9 33.8 %shard_map.266 = (bf16[768,3840]{1,0:T(8,128)(2,1)}, bf16[768,3840]{1,0:T(8,128)(2,1)}) custom-call(s32[4]{0:T(128)} %get-tuple-element.234.ids_ref, bf16[2048,1536]{1,0:T(8,128)(2,1)} %pad_maximum_fusion.c_ref.c0_ref.c1_ref, bf16[2048,1536]{1,0:T(8,128)(2,1)} %pad_maximum_fusion.c_ref.c0_ref.c1_ref, bf16[2048,1536]{1,0:T(8,128)(2,1)} %copy-done.17, ...), custom_call_target="tpu_custom_call" | custom-call | flops 15299999744 | bytes 37400000 | tf_op jit(solution)/shard_map/pallas_call | solution.py:272
  514.5 14.0 %shard_map.268 = bf16[4,1024,384]{2,1,0:T(8,128)(2,1)} custom-call(bf16[3,2048,2560]{2,1,0:T(8,128)(2,1)} %get-tuple-element.104.refs_0_.refs_1_.g_ref, bf16[1536,2560]{1,0:T(8,128)(2,1)} %all-gather.7.cloned.1.call-done.w_ref.refs_1_), custom_call_target="tpu_custom_call" | custom-call | flops 6076969472 | bytes 14854814 | tf_op jit(solution)/shard_map/pallas_call | solution.py:235
  530.6 13.5 %shard_map.267 = bf16[4,1024,384]{2,1,0:T(8,128)(2,1)} custom-call(bf16[3,2048,2560]{2,1,0:T(8,128)(2,1)} %get-tuple-element.104.refs_0_.refs_1_.g_ref, bf16[1536,2560]{1,0:T(8,128)(2,1)} %all-gather.7.cloned.1.call-done.w_ref.refs_1_), custom_call_target="tpu_custom_call" | custom-call | flops 6076969472 | bytes 14854814 | tf_op jit(solution)/shard_map/pallas_call | solution.py:235
  549.4 29.0 %all-gather.11.cloned.1.call-done = bf16[1024,1536]{1,0:T(8,128)(2,1)} async-done(((bf16[1024,384]{1,0:T(8,128)(2,1)}), bf16[1024,1536]{1,0:T(8,128)(2,1)}) %all-gather.11.cloned.1.call-update) | async-done | bytes 3145744 | tf_op jit(solution)/shard_map/all_gather | solution.py:679
  581.8 22.1 %collective-permute-done.25.refs_1_ = bf16[768,3840]{1,0:T(8,128)(2,1)} collective-permute-done((bf16[768,3840]{1,0:T(8,128)(2,1)}, bf16[768,3840]{1,0:T(8,128)(2,1)}, u32[]{:S(2)}, u32[]{:S(2)}) %collective-permute-start.25) | collective-permute-done | bytes 5898272 | tf_op jit(solution)/shard_map/ppermute | solution.py:372
  624.7 19.1 %shard_map.269.refs_0_ = bf16[1024,640]{1,0:T(8,128)(2,1)S(1)} custom-call(bf16[6,1024,64]{2,1,0:T(8,128)(2,1)} %copy-done.12, bf16[2,1024,64]{2,1,0:T(8,128)(2,1)S(1)} %get-tuple-element.111.k_ref, bf16[2,1024,64]{2,1,0:T(8,128)(2,1)S(1)} %copy-done.14, f32[1024,128]{1,0:T(8,128)S(1)} %copy-done.16, bf16[1024,384]{1,0:T(8,128)(2,1)S(1)} %copy-done.11, ...), custom_call_target="tpu_custom_call" | custom-call | flops 8550000128 | bytes 20900000 | tf_op jit(solution)/shard_map/pallas_call | solution.py:144
  644.8 5.8 shard_map.270
  694.5 6.9 collective-permute-done.33
  707.6 8.0 %shard_map.271 = (f32[192,40,128]{2,1,0:T(8,128)}, f32[192,40,128]{2,1,0:T(8,128)}, f32[192,40,128]{2,1,0:T(8,128)}) custom-call(s32[1]{0:T(128)} %bitcast.4.core_ref, bf16[768,3840]{1,0:T(8,128)(2,1)} %get-tuple-element.119.refs_0_, bf16[768,3840]{1,0:T(8,128)(2,1)} %collective-permute-done.25.refs_1_, ...), custom_call_target="tpu_custom_call" | custom-call | flops 4049999872 | bytes 9900000 | tf_op jit(solution)/shard_map/pallas_call | solution.py:349
  723.7 14.0 %all-reduce.4 = (f32[384]{0:T(512)}, f32[384]{0:T(512)}) all-reduce(f32[384]{0:T(512)S(1)} %get-tuple-element.208, f32[384]{0:T(512)S(1)} %get-tuple-element.198), channel_id=1, replica_groups=mesh['gx'=8,'gy'=4] {'gx'}, use_global_device_ids=true, to_apply=%region_10.11 | all-reduce | flops 768 | bytes 6144 | tf_op jit(solution)/shard_map/psum | solution.py:738
  (298 shorter events, 224.2 us)
Async XLA Ops:
  7.2 72.3 %all-gather.5.cloned.1.call-start = ((), (), s32[]{:S(2)}) async-start(), calls=%async_computation.3 | async-start | bytes 3993600 | tf_op jit(solution)/shard_map/all_gather | solution.py:566
  10.7 230.4 %all-gather.7.cloned.1.call-start = ((), (), s32[]{:S(2)}) async-start(), calls=%async_computation.4 | async-start | bytes 9830400 | tf_op jit(solution)/shard_map/all_gather | solution.py:587
  27.1 286.1 %all-gather.9.cloned.1.call-start = ((), (), s32[]{:S(2)}) async-start(), calls=%async_computation.5 | async-start | bytes 19660800 | tf_op jit(solution)/shard_map/all_gather | solution.py:588
  33.9 477.6 %reduce-scatter.4.cloned.1.call-start = ((), (), s32[]{:S(2)}) async-start(), calls=%async_computation.6 | async-start | bytes 3932160 | tf_op jit(solution)/shard_map/reduce_scatter | solution.py:405
  86.3 33.6 %collective-permute-start.13 = (bf16[1024,384]{1,0:T(8,128)(2,1)}, bf16[1024,384]{1,0:T(8,128)(2,1)}, u32[]{:S(2)}, u32[]{:S(2)}) collective-permute-start(bf16[1024,384]{1,0:T(8,128)(2,1)} %refs_0_), channel_id=1, source_target_pairs={{0,1},{1,2},{2,3},{3,0},{4,5},{5,6},{6,7},{7,4},{8,9},{9,10},{10,1... | collective-permute-start | bytes 2359304 | tf_op jit(solution)/shard_map/ppermute | solution.py:397
  87.9 52.1 %collective-permute-start.14 = (bf16[1024,384]{1,0:T(8,128)(2,1)}, bf16[1024,384]{1,0:T(8,128)(2,1)}, u32[]{:S(2)}, u32[]{:S(2)}) collective-permute-start(bf16[1024,384]{1,0:T(8,128)(2,1)} %refs_0_), channel_id=1, source_target_pairs={{0,2},{1,3},{2,0},{3,1},{4,6},{5,7},{6,4},{7,5},{8,10},{9,11},{10,... | collective-permute-start | bytes 2359304 | tf_op jit(solution)/shard_map/ppermute | solution.py:397
  90.6 49.3 %collective-permute-start.15 = (bf16[1024,384]{1,0:T(8,128)(2,1)}, bf16[1024,384]{1,0:T(8,128)(2,1)}, u32[]{:S(2)}, u32[]{:S(2)}) collective-permute-start(bf16[1024,384]{1,0:T(8,128)(2,1)} %refs_0_), channel_id=1, source_target_pairs={{0,3},{1,0},{2,1},{3,2},{4,7},{5,4},{6,5},{7,6},{8,11},{9,8},{10,9... | collective-permute-start | bytes 2359304 | tf_op jit(solution)/shard_map/ppermute | solution.py:397
  144.0 93.9 %collective-permute-start.16 = (bf16[1024,1536]{1,0:T(8,128)(2,1)}, bf16[1024,1536]{1,0:T(8,128)(2,1)S(1)}, u32[]{:S(2)}, u32[]{:S(2)}) collective-permute-start(bf16[1024,1536]{1,0:T(8,128)(2,1)} %shard_map.259), channel_id=1, source_target_pairs={{0,4},{4,0},{8,12},{12,8},{16,20},{20,16},{24,28},{28,24},{1,5},{5... | collective-permute-start | bytes 9437192 | tf_op jit(solution)/shard_map/ppermute | solution.py:368
  144.0 36.7 %collective-permute-start.9 = (bf16[1024,384]{1,0:T(8,128)(2,1)}, bf16[1024,384]{1,0:T(8,128)(2,1)S(1)}, u32[]{:S(2)}, u32[]{:S(2)}) collective-permute-start(bf16[1024,384]{1,0:T(8,128)(2,1)} %get-tuple-element.79), channel_id=1, source_target_pairs={{0,3},{1,0},{2,1},{3,2},{4,7},{5,4},{6,5},{7,6},{8,11},{9,8},{10,9... | collective-permute-start | bytes 2359304 | tf_op jit(solution)/shard_map/ppermute | solution.py:397
  162.4 69.1 %collective-permute-start.8 = (bf16[1024,384]{1,0:T(8,128)(2,1)}, bf16[1024,384]{1,0:T(8,128)(2,1)S(1)}, u32[]{:S(2)}, u32[]{:S(2)}) collective-permute-start(bf16[1024,384]{1,0:T(8,128)(2,1)} %get-tuple-element.78), channel_id=1, source_target_pairs={{0,2},{1,3},{2,0},{3,1},{4,6},{5,7},{6,4},{7,5},{8,10},{9,11},{10,... | collective-permute-start | bytes 2359304 | tf_op jit(solution)/shard_map/ppermute | solution.py:397
  162.8 68.7 %collective-permute-start.7 = (bf16[1024,384]{1,0:T(8,128)(2,1)S(1)}, bf16[1024,384]{1,0:T(8,128)(2,1)S(1)}, u32[]{:S(2)}, u32[]{:S(2)}) collective-permute-start(bf16[1024,384]{1,0:T(8,128)(2,1)S(1)} %copy-done.50), channel_id=1, source_target_pairs={{0,1},{1,2},{2,3},{3,0},{4,5},{5,6},{6,7},{7,4},{8,9},{9,10},{10,1... | collective-permute-start | bytes 2359304 | tf_op jit(solution)/shard_map/ppermute | solution.py:397
  233.2 30.2 %collective-permute-start.10 = (bf16[1024,384]{1,0:T(8,128)(2,1)S(1)}, bf16[1024,384]{1,0:T(8,128)(2,1)S(1)}, u32[]{:S(2)}, u32[]{:S(2)}) collective-permute-start(bf16[1024,384]{1,0:T(8,128)(2,1)S(1)} %get-tuple-element.85.refs_0_), channel_id=1, source_target_pairs={{0,1},{1,2},{2,3},{3,0},{4,5},{5,6},{6,7},{7,4},{8,9},{9,10},{10,1... | collective-permute-start | bytes 2359304 | tf_op jit(solution)/shard_map/ppermute | solution.py:397
  233.2 54.8 %collective-permute-start.11 = (bf16[1024,384]{1,0:T(8,128)(2,1)S(1)}, bf16[1024,384]{1,0:T(8,128)(2,1)S(1)}, u32[]{:S(2)}, u32[]{:S(2)}) collective-permute-start(bf16[1024,384]{1,0:T(8,128)(2,1)S(1)} %get-tuple-element.85.refs_0_), channel_id=1, source_target_pairs={{0,2},{1,3},{2,0},{3,1},{4,6},{5,7},{6,4},{7,5},{8,10},{9,11},{10,... | collective-permute-start | bytes 2359304 | tf_op jit(solution)/shard_map/ppermute | solution.py:397
  234.9 53.2 %collective-permute-start.12 = (bf16[1024,384]{1,0:T(8,128)(2,1)S(1)}, bf16[1024,384]{1,0:T(8,128)(2,1)}, u32[]{:S(2)}, u32[]{:S(2)}) collective-permute-start(bf16[1024,384]{1,0:T(8,128)(2,1)S(1)} %get-tuple-element.85.refs_0_), channel_id=1, source_target_pairs={{0,3},{1,0},{2,1},{3,2},{4,7},{5,4},{6,5},{7,6},{8,11},{9,8},{10,9... | collective-permute-start | bytes 2359304 | tf_op jit(solution)/shard_map/ppermute | solution.py:397
  383.7 50.9 %collective-permute-start.23 = (bf16[4096,384]{1,0:T(8,128)(2,1)}, bf16[4096,384]{1,0:T(8,128)(2,1)}, u32[]{:S(2)}, u32[]{:S(2)}) collective-permute-start(bf16[4096,384]{1,0:T(8,128)(2,1)} %bitcast.100), channel_id=1, source_target_pairs={{0,4},{4,0},{8,12},{12,8},{16,20},{20,16},{24,28},{28,24},{1,5},{5... | collective-permute-start | bytes 9437192 | tf_op jit(solution)/shard_map/ppermute | solution.py:368
  386.3 41.7 %collective-permute-start.21 = (f32[20,2048]{1,0:T(8,128)S(1)}, f32[20,2048]{1,0:T(8,128)S(1)}, u32[]{:S(2)}, u32[]{:S(2)}) collective-permute-start(f32[20,2048]{1,0:T(8,128)S(1)} %copy.77), channel_id=1, source_target_pairs={{0,3},{1,0},{2,1},{3,2},{4,7},{5,4},{6,5},{7,6},{8,11},{9,8},{10,9... | collective-permute-start | bytes 491528 | tf_op jit(solution)/shard_map/ppermute | solution.py:391
  439.5 138.8 %all-gather.11.cloned.1.call-start = ((), (), s32[]{:S(2)}) async-start(), calls=%async_computation.7 | async-start | bytes 3932160 | tf_op jit(solution)/shard_map/all_gather | solution.py:679
  475.4 128.5 %collective-permute-start.25 = (bf16[768,3840]{1,0:T(8,128)(2,1)}, bf16[768,3840]{1,0:T(8,128)(2,1)}, u32[]{:S(2)}, u32[]{:S(2)}) collective-permute-start(bf16[768,3840]{1,0:T(8,128)(2,1)} %get-tuple-element.97), channel_id=1, source_target_pairs={{0,8},{4,12},{8,0},{12,4},{16,24},{20,28},{24,16},{28,20},{1,9},{5... | collective-permute-start | bytes 17694728 | tf_op jit(solution)/shard_map/ppermute | solution.py:372
  475.4 134.7 %collective-permute-start.26 = (bf16[768,3840]{1,0:T(8,128)(2,1)}, bf16[768,3840]{1,0:T(8,128)(2,1)}, u32[]{:S(2)}, u32[]{:S(2)}) collective-permute-start(bf16[768,3840]{1,0:T(8,128)(2,1)} %get-tuple-element.98), channel_id=1, source_target_pairs={{0,16},{4,20},{8,24},{12,28},{16,0},{20,4},{24,8},{28,12},{1,17},{... | collective-permute-start | bytes 17694728 | tf_op jit(solution)/shard_map/ppermute | solution.py:376
  476.9 33.8 %collective-permute-start.24 = (f32[20,1024]{0,1:T(8,128)S(1)}, f32[20,1024]{0,1:T(8,128)S(1)}, u32[]{:S(2)}, u32[]{:S(2)}) collective-permute-start(f32[20,1024]{0,1:T(8,128)S(1)} %slice.205), channel_id=1, source_target_pairs={{0,4},{4,0},{8,12},{12,8},{16,20},{20,16},{24,28},{28,24},{1,5},{5... | collective-permute-start | bytes 245768 | tf_op jit(solution)/shard_map/ppermute | solution.py:368
  514.4 144.6 %reduce-scatter.6.cloned.1.call-start = ((), (), s32[]{:S(2)}) async-start(), calls=%async_computation.8 | async-start | bytes 3932160 | tf_op jit(solution)/shard_map/reduce_scatter | solution.py:405
  578.4 141.1 %reduce-scatter.8.cloned.1.call-start = ((), (), s32[]{:S(2)}) async-start(), calls=%async_computation.9 | async-start | bytes 3932160 | tf_op jit(solution)/shard_map/reduce_scatter | solution.py:405
  609.0 70.5 %collective-permute-start.35 = (bf16[384,3840]{1,0:T(8,128)(2,1)}, bf16[384,3840]{1,0:T(8,128)(2,1)S(1)}, u32[]{:S(2)}, u32[]{:S(2)}) collective-permute-start(bf16[384,3840]{1,0:T(8,128)(2,1)} %add_convert_fusion.2), channel_id=1, source_target_pairs={{0,16},{4,20},{8,24},{12,28},{16,0},{20,4},{24,8},{28,12},{1,17},{... | collective-permute-start | bytes 8847368 | tf_op jit(solution)/shard_map/ppermute | solution.py:376
  614.9 64.5 %collective-permute-start.36 = (bf16[384,3840]{1,0:T(8,128)(2,1)}, bf16[384,3840]{1,0:T(8,128)(2,1)}, u32[]{:S(2)}, u32[]{:S(2)}) collective-permute-start(bf16[384,3840]{1,0:T(8,128)(2,1)} %add_convert_fusion.1), channel_id=1, source_target_pairs={{0,8},{4,12},{8,0},{12,4},{16,24},{20,28},{24,16},{28,20},{1,9},{5... | collective-permute-start | bytes 8847368 | tf_op jit(solution)/shard_map/ppermute | solution.py:372
  (77 other events, 954.8 us)
Sparse Core Ops, SparseCore 0:
  10.8 66.8 all-gather.4
  80.2 81.8 all-gather.6
  164.5 148.6 all-gather.8
  439.7 60.1 reduce-scatter.3
  514.6 63.7 all-gather.10
  581.1 58.8 reduce-scatter.5
  659.1 60.2 reduce-scatter.7

commit v5 on v4

--- a/solution.py
+++ b/solution.py
@@ -615,7 +615,7 @@
     for k in range(1, routes.shape[1]):
         member = member | (routes_both[:, k : k + 1] == iota)
 
-    normed_own, scale_own, residual_own = norm_planes(before, after(tuple(res_pieces), down_raw), gains)
+    normed_own, scale_own, residual_own = norm_planes(before, after(tuple(res_pieces), down_raw, routes_both), gains)
     normed_two = jnp.concatenate([normed_own, swap_core(normed_own)], axis=0)
 
     logits = jnp.where(member, dot(normed_two, router_w), masked)

time: 751 us -> 750 us (level)
  transfers between devices with their start and end apart: 46 -> 46, of which waited for: 18 -> 19; matrix products, arithmetic and copies ran while one was open for 16% -> 16% of each run, Pallas kernels for 28% -> 29%
where the time goes in v5:
time: 750 us; the launch traced here: 743 us
  Pallas kernels  283 us (38%)
  waiting for transfers between devices  215 us (29%)
  other arithmetic  74.2 us (10%)
  starting transfers between devices  71.3 us (10%)
  local copies, waits for them, and re-layouts  45.8 us (6%)
  matrix products  25.5 us (3%)
  between operations  15.2 us (2%)
  blocking collectives  14 us (2%)
    ppermute x9, waiting for transfers between devices, plane_shift(): return lax.ppermute(x, 'gy', [(i, (i + d) % size) for i in range(size)])  110 us
    pallas_call x5, Pallas kernels, project(): pl.pallas_call(partial(project_body, n), grid=(parts // 2,), in_specs=[pl...  81.8 us
    pallas_call x2, Pallas kernels, expert_terms(): pl.pallas_call(partial(term_body, steps), grid_spec=pltpu.PrefetchScalarG...  67.9 us
    pallas_call x1, Pallas kernels, expert_forward(): pl.pallas_call(partial(expert_body, rows, chunk), grid=(tokens // rows, s...  46 us
    ppermute x6, waiting for transfers between devices, swap_x(): return lax.ppermute(x, 'gx', flip(2, lax.axis_size('gx')))  30.2 us
    ppermute x9, starting transfers between devices, plane_shift(): return lax.ppermute(x, 'gy', [(i, (i + d) % size) for i in range(size)])  29.5 us
    all_gather x1, waiting for transfers between devices, shards(): lax.all_gather(grad_normed_two.astype(BF), 'gy', axis=1, tiled=True)  29 us
    ppermute x6, waiting for transfers between devices, swap_y(): return lax.ppermute(x, 'gx', flip(4, lax.axis_size('gx')))  26.5 us
  transfers between devices with their start and end apart: 46, of which 19 were waited for; matrix products, arithmetic and copies ran while one was open for 16% of the time, Pallas kernels for 29%

profile of v5, /device:TPU:0, one launch (start us, length us, event | category | flops | bytes accessed | tf_op | source)
XLA Modules:
  0.0 743.4 jit_solution(13520799705651623800)
XLA Ops:
  43.9 17.6 %collective-permute-done.4 = bf16[384,1152]{1,0:T(8,128)(2,1)} collective-permute-done((bf16[384,1152]{1,0:T(8,128)(2,1)}, bf16[384,1152]{1,0:T(8,128)(2,1)}, u32[]{:S(2)}, u32[]{:S(2)}) %collective-permute-start.4) | collective-permute-done | bytes 884768 | tf_op jit(solution)/shard_map/ppermute | solution.py:376
  94.7 17.2 %shard_map.257 = (bf16[1024,384]{1,0:T(8,128)(2,1)S(1)}, bf16[6,1024,64]{2,1,0:T(8,128)(2,1)S(1)}, bf16[2,1024,64]{2,1,0:T(8,128)(2,1)S(1)}, bf16[2,1024,64]{2,1,0:T(8,128)(2,1)S(1)}, f32[1024,128]{1,0:T(8,128)S(1)}) custom-call(f32[1024,640]{1,0:T(8,128)S(1)} %fusion.54.qkv_ref, f32[1024,64]{1,0:T(8,128)S(1)} %copy-done.6, f32[1024,64]{1,0:T(8,128)S(1)} %copy-done.8), custom_call_target="tpu_custom_call" | custom-call | flops 7649999872 | bytes 18700000 | tf_op jit(solution)/shard_map/pallas_call | solution.py:85
  120.0 20.0 %collective-permute-done.14.refs_2_ = bf16[1024,384]{1,0:T(8,128)(2,1)} collective-permute-done((bf16[1024,384]{1,0:T(8,128)(2,1)}, bf16[1024,384]{1,0:T(8,128)(2,1)}, u32[]{:S(2)}, u32[]{:S(2)}) %collective-permute-start.14) | collective-permute-done | bytes 786464 | tf_op jit(solution)/shard_map/ppermute | solution.py:397
  144.1 18.4 %collective-permute-start.9 = (bf16[1024,384]{1,0:T(8,128)(2,1)}, bf16[1024,384]{1,0:T(8,128)(2,1)S(1)}, u32[]{:S(2)}, u32[]{:S(2)}) collective-permute-start(bf16[1024,384]{1,0:T(8,128)(2,1)} %get-tuple-element.79), channel_id=1, source_target_pairs={{0,3},{1,0},{2,1},{3,2},{4,7},{5,4},{6,5},{7,6},{8,11},{9,8},{10,9... | collective-permute-start | bytes 2359304 | tf_op jit(solution)/shard_map/ppermute | solution.py:397
  165.7 15.0 %collective-permute-done.9 = bf16[1024,384]{1,0:T(8,128)(2,1)S(1)} collective-permute-done((bf16[1024,384]{1,0:T(8,128)(2,1)}, bf16[1024,384]{1,0:T(8,128)(2,1)S(1)}, u32[]{:S(2)}, u32[]{:S(2)}) %collective-permute-start.9) | collective-permute-done | bytes 786464 | tf_op jit(solution)/shard_map/ppermute | solution.py:397
  180.7 50.8 %collective-permute-done.8 = bf16[1024,384]{1,0:T(8,128)(2,1)S(1)} collective-permute-done((bf16[1024,384]{1,0:T(8,128)(2,1)}, bf16[1024,384]{1,0:T(8,128)(2,1)S(1)}, u32[]{:S(2)}, u32[]{:S(2)}) %collective-permute-start.8) | collective-permute-done | bytes 786464 | tf_op jit(solution)/shard_map/ppermute | solution.py:397
  241.1 22.3 %shard_map.260.draw_ref = bf16[2048,2560]{1,0:T(8,128)(2,1)} custom-call(bf16[2048,1536]{1,0:T(8,128)(2,1)} %pad_maximum_fusion.c_ref.c0_ref.c1_ref, bf16[1536,2560]{1,0:T(8,128)(2,1)} %all-gather.7.cloned.1.call-done.w_ref.refs_1_), custom_call_target="tpu_custom_call" | custom-call | flops 9900000256 | bytes 24200000 | tf_op jit(solution)/shard_map/pallas_call | solution.py:416
  263.4 24.6 %collective-permute-done.11.refs_2_ = bf16[1024,384]{1,0:T(8,128)(2,1)S(1)} collective-permute-done((bf16[1024,384]{1,0:T(8,128)(2,1)S(1)}, bf16[1024,384]{1,0:T(8,128)(2,1)S(1)}, u32[]{:S(2)}, u32[]{:S(2)}) %collective-permute-start.11) | collective-permute-done | bytes 786464 | tf_op jit(solution)/shard_map/ppermute | solution.py:397
  289.0 6.7 shard_map.261
  313.2 46.0 %shard_map.262 = (bf16[3,2048,2560]{2,1,0:T(8,128)(2,1)}, f32[2048,128]{1,0:T(8,128)}) custom-call(bf16[2048,1536]{1,0:T(8,128)(2,1)} %copy-done.17, bf16[1536,5120]{1,0:T(8,128)(2,1)} %all-gather.9.cloned.1.call-done.wg_ref.wu_ref.refs_2_.refs_3_, bf16[1536,5120]{1,0:T(8,128)(2,1)} %all-gather.9.cloned.1.call-done.wg_ref.wu_ref.refs_2_.refs_3_, ...), custom_call_target="tpu_custom_call" | custom-call | flops 20700000256 | bytes 50600000 | tf_op jit(solution)/shard_map/pallas_call | solution.py:197
  359.2 24.5 %shard_map.263 = bf16[4,1024,384]{2,1,0:T(8,128)(2,1)} custom-call(bf16[3,2048,2560]{2,1,0:T(8,128)(2,1)} %get-tuple-element.104.refs_0_.refs_1_.g_ref, bf16[3,2048,2560]{2,1,0:T(8,128)(2,1)} %get-tuple-element.104.refs_0_.refs_1_.g_ref, bf16[1536,5120]{1,0:T(8,128)(2,1)} %all-gather.9.cloned.1.call-done.wg_ref.wu_ref.refs_2_.refs_3_, ...), custom_call_target="tpu_custom_call" | custom-call | flops 11253939200 | bytes 27509628 | tf_op jit(solution)/shard_map/pallas_call | solution.py:235
  386.3 15.2 %collective-permute-start.21 = (f32[20,2048]{1,0:T(8,128)S(1)}, f32[20,2048]{1,0:T(8,128)S(1)}, u32[]{:S(2)}, u32[]{:S(2)}) collective-permute-start(f32[20,2048]{1,0:T(8,128)S(1)} %copy.77), channel_id=1, source_target_pairs={{0,3},{1,0},{2,1},{3,2},{4,7},{5,4},{6,5},{7,6},{8,11},{9,8},{10,9... | collective-permute-start | bytes 491528 | tf_op jit(solution)/shard_map/ppermute | solution.py:391
  402.1 24.1 %shard_map.264 = bf16[4,1024,384]{2,1,0:T(8,128)(2,1)} custom-call(bf16[3,2048,2560]{2,1,0:T(8,128)(2,1)} %get-tuple-element.104.refs_0_.refs_1_.g_ref, bf16[3,2048,2560]{2,1,0:T(8,128)(2,1)} %get-tuple-element.104.refs_0_.refs_1_.g_ref, bf16[1536,5120]{1,0:T(8,128)(2,1)} %all-gather.9.cloned.1.call-done.wg_ref.wu_ref.refs_2_.refs_3_, ...), custom_call_target="tpu_custom_call" | custom-call | flops 11253939200 | bytes 27509628 | tf_op jit(solution)/shard_map/pallas_call | solution.py:235
  439.5 34.2 %shard_map.265 = (bf16[768,3840]{1,0:T(8,128)(2,1)}, bf16[768,3840]{1,0:T(8,128)(2,1)}) custom-call(s32[4]{0:T(128)} %get-tuple-element.235.ids_ref, bf16[2048,1536]{1,0:T(8,128)(2,1)} %pad_maximum_fusion.c_ref.c0_ref.c1_ref, bf16[2048,1536]{1,0:T(8,128)(2,1)} %pad_maximum_fusion.c_ref.c0_ref.c1_ref, bf16[2048,1536]{1,0:T(8,128)(2,1)} %copy-done.17, ...), custom_call_target="tpu_custom_call" | custom-call | flops 15299999744 | bytes 37400000 | tf_op jit(solution)/shard_map/pallas_call | solution.py:272
  475.1 33.8 %shard_map.266 = (bf16[768,3840]{1,0:T(8,128)(2,1)}, bf16[768,3840]{1,0:T(8,128)(2,1)}) custom-call(s32[4]{0:T(128)} %get-tuple-element.234.ids_ref, bf16[2048,1536]{1,0:T(8,128)(2,1)} %pad_maximum_fusion.c_ref.c0_ref.c1_ref, bf16[2048,1536]{1,0:T(8,128)(2,1)} %pad_maximum_fusion.c_ref.c0_ref.c1_ref, bf16[2048,1536]{1,0:T(8,128)(2,1)} %copy-done.17, ...), custom_call_target="tpu_custom_call" | custom-call | flops 15299999744 | bytes 37400000 | tf_op jit(solution)/shard_map/pallas_call | solution.py:272
  512.7 14.0 %shard_map.268 = bf16[4,1024,384]{2,1,0:T(8,128)(2,1)} custom-call(bf16[3,2048,2560]{2,1,0:T(8,128)(2,1)} %get-tuple-element.104.refs_0_.refs_1_.g_ref, bf16[1536,2560]{1,0:T(8,128)(2,1)} %all-gather.7.cloned.1.call-done.w_ref.refs_1_), custom_call_target="tpu_custom_call" | custom-call | flops 6076969472 | bytes 14854814 | tf_op jit(solution)/shard_map/pallas_call | solution.py:235
  528.9 13.5 %shard_map.267 = bf16[4,1024,384]{2,1,0:T(8,128)(2,1)} custom-call(bf16[3,2048,2560]{2,1,0:T(8,128)(2,1)} %get-tuple-element.104.refs_0_.refs_1_.g_ref, bf16[1536,2560]{1,0:T(8,128)(2,1)} %all-gather.7.cloned.1.call-done.w_ref.refs_1_), custom_call_target="tpu_custom_call" | custom-call | flops 6076969472 | bytes 14854814 | tf_op jit(solution)/shard_map/pallas_call | solution.py:235
  547.6 29.0 %all-gather.11.cloned.1.call-done = bf16[1024,1536]{1,0:T(8,128)(2,1)} async-done(((bf16[1024,384]{1,0:T(8,128)(2,1)}), bf16[1024,1536]{1,0:T(8,128)(2,1)}) %all-gather.11.cloned.1.call-update) | async-done | bytes 3145744 | tf_op jit(solution)/shard_map/all_gather | solution.py:679
  580.1 22.6 %collective-permute-done.25.refs_1_ = bf16[768,3840]{1,0:T(8,128)(2,1)} collective-permute-done((bf16[768,3840]{1,0:T(8,128)(2,1)}, bf16[768,3840]{1,0:T(8,128)(2,1)}, u32[]{:S(2)}, u32[]{:S(2)}) %collective-permute-start.25) | collective-permute-done | bytes 5898272 | tf_op jit(solution)/shard_map/ppermute | solution.py:372
  623.3 19.1 %shard_map.269.refs_0_ = bf16[1024,640]{1,0:T(8,128)(2,1)S(1)} custom-call(bf16[6,1024,64]{2,1,0:T(8,128)(2,1)} %copy-done.12, bf16[2,1024,64]{2,1,0:T(8,128)(2,1)S(1)} %get-tuple-element.111.k_ref, bf16[2,1024,64]{2,1,0:T(8,128)(2,1)S(1)} %copy-done.14, f32[1024,128]{1,0:T(8,128)S(1)} %copy-done.16, bf16[1024,384]{1,0:T(8,128)(2,1)S(1)} %copy-done.11, ...), custom_call_target="tpu_custom_call" | custom-call | flops 8550000128 | bytes 20900000 | tf_op jit(solution)/shard_map/pallas_call | solution.py:144
  643.5 5.8 shard_map.270
  693.3 6.6 collective-permute-done.33
  706.3 8.0 %shard_map.271 = (f32[192,40,128]{2,1,0:T(8,128)}, f32[192,40,128]{2,1,0:T(8,128)}, f32[192,40,128]{2,1,0:T(8,128)}) custom-call(s32[1]{0:T(128)} %bitcast.4.core_ref, bf16[768,3840]{1,0:T(8,128)(2,1)} %get-tuple-element.119.refs_0_, bf16[768,3840]{1,0:T(8,128)(2,1)} %collective-permute-done.25.refs_1_, ...), custom_call_target="tpu_custom_call" | custom-call | flops 4049999872 | bytes 9900000 | tf_op jit(solution)/shard_map/pallas_call | solution.py:349
  722.3 14.0 %all-reduce.4 = (f32[384]{0:T(512)}, f32[384]{0:T(512)}) all-reduce(f32[384]{0:T(512)S(1)} %get-tuple-element.208, f32[384]{0:T(512)S(1)} %get-tuple-element.198), channel_id=1, replica_groups=mesh['gx'=8,'gy'=4] {'gx'}, use_global_device_ids=true, to_apply=%region_10.11 | all-reduce | flops 768 | bytes 6144 | tf_op jit(solution)/shard_map/psum | solution.py:738
  (298 shorter events, 225.5 us)
Async XLA Ops:
  7.2 72.3 %all-gather.5.cloned.1.call-start = ((), (), s32[]{:S(2)}) async-start(), calls=%async_computation.3 | async-start | bytes 3993600 | tf_op jit(solution)/shard_map/all_gather | solution.py:566
  10.7 230.4 %all-gather.7.cloned.1.call-start = ((), (), s32[]{:S(2)}) async-start(), calls=%async_computation.4 | async-start | bytes 9830400 | tf_op jit(solution)/shard_map/all_gather | solution.py:587
  27.1 286.1 %all-gather.9.cloned.1.call-start = ((), (), s32[]{:S(2)}) async-start(), calls=%async_computation.5 | async-start | bytes 19660800 | tf_op jit(solution)/shard_map/all_gather | solution.py:588
  33.9 475.8 %reduce-scatter.4.cloned.1.call-start = ((), (), s32[]{:S(2)}) async-start(), calls=%async_computation.6 | async-start | bytes 3932160 | tf_op jit(solution)/shard_map/reduce_scatter | solution.py:405
  86.3 33.6 %collective-permute-start.13 = (bf16[1024,384]{1,0:T(8,128)(2,1)}, bf16[1024,384]{1,0:T(8,128)(2,1)}, u32[]{:S(2)}, u32[]{:S(2)}) collective-permute-start(bf16[1024,384]{1,0:T(8,128)(2,1)} %refs_0_), channel_id=1, source_target_pairs={{0,1},{1,2},{2,3},{3,0},{4,5},{5,6},{6,7},{7,4},{8,9},{9,10},{10,1... | collective-permute-start | bytes 2359304 | tf_op jit(solution)/shard_map/ppermute | solution.py:397
  87.9 52.1 %collective-permute-start.14 = (bf16[1024,384]{1,0:T(8,128)(2,1)}, bf16[1024,384]{1,0:T(8,128)(2,1)}, u32[]{:S(2)}, u32[]{:S(2)}) collective-permute-start(bf16[1024,384]{1,0:T(8,128)(2,1)} %refs_0_), channel_id=1, source_target_pairs={{0,2},{1,3},{2,0},{3,1},{4,6},{5,7},{6,4},{7,5},{8,10},{9,11},{10,... | collective-permute-start | bytes 2359304 | tf_op jit(solution)/shard_map/ppermute | solution.py:397
  90.6 49.3 %collective-permute-start.15 = (bf16[1024,384]{1,0:T(8,128)(2,1)}, bf16[1024,384]{1,0:T(8,128)(2,1)}, u32[]{:S(2)}, u32[]{:S(2)}) collective-permute-start(bf16[1024,384]{1,0:T(8,128)(2,1)} %refs_0_), channel_id=1, source_target_pairs={{0,3},{1,0},{2,1},{3,2},{4,7},{5,4},{6,5},{7,6},{8,11},{9,8},{10,9... | collective-permute-start | bytes 2359304 | tf_op jit(solution)/shard_map/ppermute | solution.py:397
  144.0 93.9 %collective-permute-start.16 = (bf16[1024,1536]{1,0:T(8,128)(2,1)}, bf16[1024,1536]{1,0:T(8,128)(2,1)S(1)}, u32[]{:S(2)}, u32[]{:S(2)}) collective-permute-start(bf16[1024,1536]{1,0:T(8,128)(2,1)} %shard_map.259), channel_id=1, source_target_pairs={{0,4},{4,0},{8,12},{12,8},{16,20},{20,16},{24,28},{28,24},{1,5},{5... | collective-permute-start | bytes 9437192 | tf_op jit(solution)/shard_map/ppermute | solution.py:368
  144.1 36.7 %collective-permute-start.9 = (bf16[1024,384]{1,0:T(8,128)(2,1)}, bf16[1024,384]{1,0:T(8,128)(2,1)S(1)}, u32[]{:S(2)}, u32[]{:S(2)}) collective-permute-start(bf16[1024,384]{1,0:T(8,128)(2,1)} %get-tuple-element.79), channel_id=1, source_target_pairs={{0,3},{1,0},{2,1},{3,2},{4,7},{5,4},{6,5},{7,6},{8,11},{9,8},{10,9... | collective-permute-start | bytes 2359304 | tf_op jit(solution)/shard_map/ppermute | solution.py:397
  162.4 69.1 %collective-permute-start.8 = (bf16[1024,384]{1,0:T(8,128)(2,1)}, bf16[1024,384]{1,0:T(8,128)(2,1)S(1)}, u32[]{:S(2)}, u32[]{:S(2)}) collective-permute-start(bf16[1024,384]{1,0:T(8,128)(2,1)} %get-tuple-element.78), channel_id=1, source_target_pairs={{0,2},{1,3},{2,0},{3,1},{4,6},{5,7},{6,4},{7,5},{8,10},{9,11},{10,... | collective-permute-start | bytes 2359304 | tf_op jit(solution)/shard_map/ppermute | solution.py:397
  162.8 68.7 %collective-permute-start.7 = (bf16[1024,384]{1,0:T(8,128)(2,1)S(1)}, bf16[1024,384]{1,0:T(8,128)(2,1)S(1)}, u32[]{:S(2)}, u32[]{:S(2)}) collective-permute-start(bf16[1024,384]{1,0:T(8,128)(2,1)S(1)} %copy-done.50), channel_id=1, source_target_pairs={{0,1},{1,2},{2,3},{3,0},{4,5},{5,6},{6,7},{7,4},{8,9},{9,10},{10,1... | collective-permute-start | bytes 2359304 | tf_op jit(solution)/shard_map/ppermute | solution.py:397
  233.2 30.2 %collective-permute-start.10 = (bf16[1024,384]{1,0:T(8,128)(2,1)S(1)}, bf16[1024,384]{1,0:T(8,128)(2,1)S(1)}, u32[]{:S(2)}, u32[]{:S(2)}) collective-permute-start(bf16[1024,384]{1,0:T(8,128)(2,1)S(1)} %get-tuple-element.85.refs_0_), channel_id=1, source_target_pairs={{0,1},{1,2},{2,3},{3,0},{4,5},{5,6},{6,7},{7,4},{8,9},{9,10},{10,1... | collective-permute-start | bytes 2359304 | tf_op jit(solution)/shard_map/ppermute | solution.py:397
  233.2 54.8 %collective-permute-start.11 = (bf16[1024,384]{1,0:T(8,128)(2,1)S(1)}, bf16[1024,384]{1,0:T(8,128)(2,1)S(1)}, u32[]{:S(2)}, u32[]{:S(2)}) collective-permute-start(bf16[1024,384]{1,0:T(8,128)(2,1)S(1)} %get-tuple-element.85.refs_0_), channel_id=1, source_target_pairs={{0,2},{1,3},{2,0},{3,1},{4,6},{5,7},{6,4},{7,5},{8,10},{9,11},{10,... | collective-permute-start | bytes 2359304 | tf_op jit(solution)/shard_map/ppermute | solution.py:397
  234.9 53.2 %collective-permute-start.12 = (bf16[1024,384]{1,0:T(8,128)(2,1)S(1)}, bf16[1024,384]{1,0:T(8,128)(2,1)}, u32[]{:S(2)}, u32[]{:S(2)}) collective-permute-start(bf16[1024,384]{1,0:T(8,128)(2,1)S(1)} %get-tuple-element.85.refs_0_), channel_id=1, source_target_pairs={{0,3},{1,0},{2,1},{3,2},{4,7},{5,4},{6,5},{7,6},{8,11},{9,8},{10,9... | collective-permute-start | bytes 2359304 | tf_op jit(solution)/shard_map/ppermute | solution.py:397
  383.7 49.1 %collective-permute-start.23 = (bf16[4096,384]{1,0:T(8,128)(2,1)}, bf16[4096,384]{1,0:T(8,128)(2,1)}, u32[]{:S(2)}, u32[]{:S(2)}) collective-permute-start(bf16[4096,384]{1,0:T(8,128)(2,1)} %bitcast.100), channel_id=1, source_target_pairs={{0,4},{4,0},{8,12},{12,8},{16,20},{20,16},{24,28},{28,24},{1,5},{5... | collective-permute-start | bytes 9437192 | tf_op jit(solution)/shard_map/ppermute | solution.py:368
  386.3 39.9 %collective-permute-start.21 = (f32[20,2048]{1,0:T(8,128)S(1)}, f32[20,2048]{1,0:T(8,128)S(1)}, u32[]{:S(2)}, u32[]{:S(2)}) collective-permute-start(f32[20,2048]{1,0:T(8,128)S(1)} %copy.77), channel_id=1, source_target_pairs={{0,3},{1,0},{2,1},{3,2},{4,7},{5,4},{6,5},{7,6},{8,11},{9,8},{10,9... | collective-permute-start | bytes 491528 | tf_op jit(solution)/shard_map/ppermute | solution.py:391
  437.8 138.8 %all-gather.11.cloned.1.call-start = ((), (), s32[]{:S(2)}) async-start(), calls=%async_computation.7 | async-start | bytes 3932160 | tf_op jit(solution)/shard_map/all_gather | solution.py:679
  473.7 129.0 %collective-permute-start.25 = (bf16[768,3840]{1,0:T(8,128)(2,1)}, bf16[768,3840]{1,0:T(8,128)(2,1)}, u32[]{:S(2)}, u32[]{:S(2)}) collective-permute-start(bf16[768,3840]{1,0:T(8,128)(2,1)} %get-tuple-element.97), channel_id=1, source_target_pairs={{0,8},{4,12},{8,0},{12,4},{16,24},{20,28},{24,16},{28,20},{1,9},{5... | collective-permute-start | bytes 17694728 | tf_op jit(solution)/shard_map/ppermute | solution.py:372
  473.7 135.1 %collective-permute-start.26 = (bf16[768,3840]{1,0:T(8,128)(2,1)}, bf16[768,3840]{1,0:T(8,128)(2,1)}, u32[]{:S(2)}, u32[]{:S(2)}) collective-permute-start(bf16[768,3840]{1,0:T(8,128)(2,1)} %get-tuple-element.98), channel_id=1, source_target_pairs={{0,16},{4,20},{8,24},{12,28},{16,0},{20,4},{24,8},{28,12},{1,17},{... | collective-permute-start | bytes 17694728 | tf_op jit(solution)/shard_map/ppermute | solution.py:376
  475.1 33.8 %collective-permute-start.24 = (f32[20,1024]{0,1:T(8,128)S(1)}, f32[20,1024]{0,1:T(8,128)S(1)}, u32[]{:S(2)}, u32[]{:S(2)}) collective-permute-start(f32[20,1024]{0,1:T(8,128)S(1)} %slice.205), channel_id=1, source_target_pairs={{0,4},{4,0},{8,12},{12,8},{16,20},{20,16},{24,28},{28,24},{1,5},{5... | collective-permute-start | bytes 245768 | tf_op jit(solution)/shard_map/ppermute | solution.py:368
  512.7 144.9 %reduce-scatter.6.cloned.1.call-start = ((), (), s32[]{:S(2)}) async-start(), calls=%async_computation.8 | async-start | bytes 3932160 | tf_op jit(solution)/shard_map/reduce_scatter | solution.py:405
  576.7 141.4 %reduce-scatter.8.cloned.1.call-start = ((), (), s32[]{:S(2)}) async-start(), calls=%async_computation.9 | async-start | bytes 3932160 | tf_op jit(solution)/shard_map/reduce_scatter | solution.py:405
  607.7 70.3 %collective-permute-start.35 = (bf16[384,3840]{1,0:T(8,128)(2,1)}, bf16[384,3840]{1,0:T(8,128)(2,1)S(1)}, u32[]{:S(2)}, u32[]{:S(2)}) collective-permute-start(bf16[384,3840]{1,0:T(8,128)(2,1)} %add_convert_fusion.2), channel_id=1, source_target_pairs={{0,16},{4,20},{8,24},{12,28},{16,0},{20,4},{24,8},{28,12},{1,17},{... | collective-permute-start | bytes 8847368 | tf_op jit(solution)/shard_map/ppermute | solution.py:376
  613.6 64.4 %collective-permute-start.36 = (bf16[384,3840]{1,0:T(8,128)(2,1)}, bf16[384,3840]{1,0:T(8,128)(2,1)}, u32[]{:S(2)}, u32[]{:S(2)}) collective-permute-start(bf16[384,3840]{1,0:T(8,128)(2,1)} %add_convert_fusion.1), channel_id=1, source_target_pairs={{0,8},{4,12},{8,0},{12,4},{16,24},{20,28},{24,16},{28,20},{1,9},{5... | collective-permute-start | bytes 8847368 | tf_op jit(solution)/shard_map/ppermute | solution.py:372
  (77 other events, 939.3 us)
Sparse Core Ops, SparseCore 0:
  10.8 66.8 all-gather.4
  80.2 81.8 all-gather.6
  164.5 148.6 all-gather.8
  437.9 60.1 reduce-scatter.3
  512.8 63.8 all-gather.10
  579.4 58.8 reduce-scatter.5
  657.8 60.2 reduce-scatter.7
